TPU v7x, 32 devices: a whole 2x2x4 slice. The times are simulated.
32 devices in a mesh: gx: 8 (over z, x), gz: 4 (over y, core).
Axes of the slice: x: 2, y: 2, z: 4, core: 2. Of those that a mesh axis runs over, the one named last changes fastest.
Arguments:
- state: float32 [5, 32, 32, 2048], P(None, 'gx', None, 'gz'), as said below
- mask_x: int32 [32, 32, 2048], P('gx', None, 'gz'), may hold values from 0 to 1, as said below
- mask_y: int32 [32, 32, 2048], P('gx', None, 'gz'), may hold values from 0 to 1, as said below
- span_filter: float32 [1024], replicated, may hold values from 0.25 to 1
Outputs:
- updated: float32 [5, 32, 32, 2048], P(None, 'gx', None, 'gz')
Inputs may be any that keep to these rules, and one draw needn't show every extreme that they name: `state`: density and pressure of every cell lie between 0.5 and 2; the streamwise velocity lies between 0.8 and 3.2, the others between -1.2 and 1.2. `mask_x`: 1 selects the upwind value at that face, 0 the central one. `mask_y`: 1 selects the upwind value at that face, 0 the central one.
All inputs are finite; a program needn't handle non-finite values.
Results may differ from a plain program's by a relative error of at most 0.0003.
Values sent between devices are 32-bit elements; how exact they have to be, the bound alone decides.
No kernel may reach another device: no remote copies, remote signals or barrier semaphores. Data moves between devices by JAX's collectives and lax.ppermute only.
A program may use at most 64 MiB of HBM per device.

v0:
```python
import functools

import jax
import jax.numpy as jnp
import numpy as np
from jax import lax
from jax.experimental import pallas as pl
from jax.experimental.pallas import tpu as pltpu
from jax.sharding import PartitionSpec as P

GAMMA_GAS = 1.4
SMALL_EPS = 1e-06
TIME_STEP = 0.1
ROWS = 8
LANES = 128
SUM_PARTS = 2
VMEM_BYTES = 24 * 1024 * 1024
PACK_BYTES = 60 * 1024 * 1024
FACE_SCALE = -TIME_STEP / 60.0
PLACE = pl.BlockSpec(memory_space=pltpu.VMEM)
ANYWHERE = pl.BlockSpec(memory_space=pl.ANY)
HBM = pl.BlockSpec(memory_space=pltpu.HBM)


def call(kernel, name, weight, ins, outs, out_shape, scratch=(), aliases=None, vmem=VMEM_BYTES):
    return pl.pallas_call(
        kernel,
        out_shape=out_shape,
        in_specs=ins,
        out_specs=outs,
        scratch_shapes=list(scratch),
        input_output_aliases=aliases or {},
        compiler_params=pltpu.CompilerParams(vmem_limit_bytes=vmem),
        cost_estimate=pl.CostEstimate(
            flops=int(weight * 1e8), bytes_accessed=int(weight * 3e5), transcendentals=0
        ),
        name=name,
    )


def shape_of(*dims, dtype=jnp.float32):
    return jax.ShapeDtypeStruct(dims, dtype)


def flux_of(q, normal):
    thin = pl.reciprocal(q[0], approx=True)
    velocity = [q[1] * thin, q[2] * thin, q[3] * thin]
    pressure = (GAMMA_GAS - 1.0) * (
        q[4] - 0.5 * (q[1] * velocity[0] + q[2] * velocity[1] + q[3] * velocity[2])
    )
    along = velocity[normal]
    flux = [q[normal + 1], q[1] * along, q[2] * along, q[3] * along, (q[4] + pressure) * along]
    flux[normal + 1] = flux[normal + 1] + pressure
    return flux, pressure, thin, along


def speed_of(pressure, thin, along):
    return jnp.abs(along) + jnp.sqrt(GAMMA_GAS * pressure * thin)


def weno_rest(d1, d2, d3, d4):
    low = d2 * d2 * 0.609375 + 3.0 * SMALL_EPS
    high = d3 * d3 * 0.609375 + 3.0 * SMALL_EPS
    x0 = d1 - 1.375 * d2
    x1 = d2 - 0.625 * d3
    x2 = d4 - 1.375 * d3
    t0 = low + x0 * x0
    t1 = high + x1 * x1
    t2 = high + x2 * x2
    w0 = t1 * t2
    w1 = t0 * t2
    w2 = t0 * t1
    w0 = w0 * w0
    w1 = w1 * w1
    w2 = w2 * w2 * 1.5
    top = w0 * (x0 + (d3 - 0.625 * d2)) + w2 * (x1 + x2)
    bottom = 0.5 * w0 + 3.0 * w1 + w2
    return top * pl.reciprocal(bottom, approx=True)


def face_value(dq, df, both, alpha, upwind):
    aq = [alpha * value for value in dq]
    plus = [df[k] + aq[k] for k in range(4)]
    minus = [df[k] - aq[k] for k in range(1, 5)]
    bend = df[1] - df[3]
    central = 7.0 * bend + (df[4] - df[0])
    rest = weno_rest(minus[3], minus[2], minus[1], minus[0]) - weno_rest(*plus)
    biased = 5.0 * (bend + (aq[1] + aq[3]) - (aq[2] + aq[2]) + rest)
    return 30.0 * both + jnp.where(upwind, biased, central)


def lanes(number):
    return pl.ds(pl.multiple_of(number * LANES, LANES), LANES)


def wall_kernel(low, state_ref, mask_ref, base_ref, out_ref, q_s, f_s, speed_s, dq_s, df_s):
    rows_y = state_ref.shape[2]
    width = state_ref.shape[3]
    tiles = rows_y // ROWS
    end = ROWS + rows_y
    zero = jnp.zeros((5, ROWS, LANES), jnp.float32)
    for side in (dq_s, df_s):
        side[:, 0:ROWS, :] = zero
        side[:, end : end + ROWS, :] = zero
    row = lax.broadcasted_iota(jnp.int32, (ROWS, LANES), 0)

    def column(number, carry):
        plane = number // (width // LANES)
        lane = lanes(number % (width // LANES))
        zero_row = jnp.minimum(number, 0)

        def at(r, shift):
            return pl.ds(zero_row + (r * ROWS + ROWS + shift), ROWS)

        def still(r):
            return slice(r * ROWS + ROWS, r * ROWS + 2 * ROWS)

        qs = []
        for r in range(tiles):
            mine = slice(r * ROWS, r * ROWS + ROWS)
            q = [state_ref[k, low + plane, mine, lane] for k in range(5)]
            flux, pressure, thin, along = flux_of(q, 1)
            speed = speed_of(pressure, thin, along)
            for k in range(5):
                q_s[k, still(r), :] = q[k]
                f_s[k, still(r), :] = flux[k]
            speed_s[still(r), :] = speed
            if r == 0:
                for k in range(5):
                    q_s[k, 0:ROWS, :] = jnp.broadcast_to(q[k][0:1], (ROWS, LANES))
                    f_s[k, 0:ROWS, :] = jnp.broadcast_to(flux[k][0:1], (ROWS, LANES))
                speed_s[0:ROWS, :] = jnp.broadcast_to(speed[0:1], (ROWS, LANES))
            if r == tiles - 1:
                speed_s[end : end + ROWS, :] = jnp.broadcast_to(
                    speed[ROWS - 1 : ROWS], (ROWS, LANES)
                )
        for k in range(5):
            changes = [
                (
                    q_s[k, still(r), :] - q_s[k, at(r, -1), :],
                    f_s[k, still(r), :] - f_s[k, at(r, -1), :],
                )
                for r in range(tiles)
            ]
            for r in range(tiles):
                dq_s[k, still(r), :] = changes[r][0]
                df_s[k, still(r), :] = changes[r][1]
        alphas, switches = [], []
        for r in range(tiles):
            alpha = speed_s[still(r), :]
            for shift in (-3, -2, -1, 1, 2):
                alpha = jnp.maximum(alpha, speed_s[at(r, shift), :])
            alphas.append(alpha)
            switches.append(mask_ref[low + plane, r * ROWS : r * ROWS + ROWS, lane] > 0)
        for k in range(5):
            hats = []
            for r in range(tiles):
                dq = [dq_s[k, at(r, s), :] for s in (-2, -1)]
                df = [df_s[k, at(r, s), :] for s in (-2, -1)]
                dq += [dq_s[k, still(r), :]]
                df += [df_s[k, still(r), :]]
                dq += [dq_s[k, at(r, s), :] for s in (1, 2)]
                df += [df_s[k, at(r, s), :] for s in (1, 2)]
                here = f_s[k, still(r), :]
                both = here + here - df[2]
                hats.append(face_value(dq, df, both, alphas[r], switches[r]))
            top = (
                60.0 * f_s[k, end - 1 : end, :]
                + 7.0 * df_s[k, end - 1 : end, :]
                - df_s[k, end - 2 : end - 1, :]
            )
            turned = [pltpu.roll(hat, ROWS - 1, 0) for hat in hats]
            turned.append(jnp.broadcast_to(top, (ROWS, LANES)))
            for r in range(tiles):
                after = jnp.where(row == ROWS - 1, turned[r + 1], turned[r])
                mine = slice(r * ROWS, r * ROWS + ROWS)
                out_ref[k, plane, mine, lane] = base_ref[k, low + plane, mine, lane] + FACE_SCALE * (
                    after - hats[r]
                )
        return carry

    lax.fori_loop(0, out_ref.shape[1] * (width // LANES), column, 0)


def wall_part(state, mask_y, base, low, count, after):
    fields, depth, rows_y, width = state.shape
    tall = rows_y + 2 * ROWS
    padded = pltpu.VMEM((fields, tall, LANES), jnp.float32)

    def kernel(state_ref, mask_ref, base_ref, after_ref, out_ref, *scratch):
        wall_kernel(low, state_ref, mask_ref, base_ref, out_ref, *scratch)

    return call(
        kernel,
        "wall_faces",
        5.0 * count / depth,
        [PLACE, PLACE, PLACE, ANYWHERE],
        PLACE,
        shape_of(fields, count, rows_y, width),
        [padded, padded, pltpu.VMEM((tall, LANES), jnp.float32), padded, padded],
    )(state, mask_y, base, after)


def pack_kernel(parts, state_ref, mask_ref, *refs):
    outs = refs[: len(parts)]
    mask_s, sems = refs[len(parts) :]
    planes = state_ref.shape[0]
    mask_copy = pltpu.make_async_copy(mask_ref.at[0], mask_s, sems.at[len(parts)])
    mask_copy.start()
    copies = [
        pltpu.make_async_copy(
            state_ref.at[:, pl.ds(row, rows), pl.ds(lane, width)],
            out.at[pl.ds(0, planes)],
            sems.at[c],
        )
        for c, ((row, rows, lane, width), out) in enumerate(zip(parts, outs))
    ]
    for copy in copies:
        copy.start()
    mask_copy.wait()
    for (row, rows, lane, width), out in zip(parts, outs):
        out[planes] = mask_s[row : row + rows, lane : lane + width].astype(jnp.float32)
    for copy in copies:
        copy.wait()


def pack_part(state, mask_x, parts):
    fields, depth, rows_all, width = state.shape
    planes = fields * depth
    return call(
        functools.partial(pack_kernel, parts),
        "pack_bricks",
        1.0,
        [HBM, HBM],
        [PLACE] * len(parts),
        [shape_of(planes + 1, rows, lane_count) for _, rows, _, lane_count in parts],
        [
            pltpu.VMEM((rows_all, width), jnp.int32),
            pltpu.SemaphoreType.DMA((len(parts) + 1,)),
        ],
        vmem=PACK_BYTES,
    )(state.reshape(planes, rows_all, width), mask_x)


def pass_kernel(depth, pair_ref, after_ref, out_ref):
    planes = pair_ref.shape[0] - 1
    skip = 1 - lax.rem(lax.axis_index("gx"), 2)
    for k in range(planes // depth):
        for i in range(3):
            out_ref[3 * k + i] = pair_ref[depth * k + i + skip * (depth - 3)]
    out_ref[3 * (planes // depth)] = pair_ref[planes]


def pass_part(pair, depth, after):
    planes, rows_y, width = pair.shape
    return call(
        functools.partial(pass_kernel, depth),
        "pass_planes",
        0.5,
        [PLACE, ANYWHERE],
        PLACE,
        shape_of(3 * (planes - 1) // depth + 1, rows_y, width),
    )(pair, after)


def stream_kernel(part, segments, counts, *refs):
    state_ref, pair_ref, far_ref, mask_ref = refs[:4]
    sum_refs = refs[4 : 4 + len(segments)]
    acc_refs = refs[4 + len(segments) : 4 + len(segments) + len(counts)]
    out_ref, token_ref, dq_s, df_s, both_s, alpha_s, result, sem = refs[-8:]
    token_ref[...] = jnp.zeros_like(token_ref)
    fields, depth, _, _ = state_ref.shape
    start, rows_y, start_lane, width = part
    rank = lax.axis_index("gx")
    even = lax.rem(rank, 2) == 0
    first = rank == 0
    last = rank == lax.axis_size("gx") - 1
    lane_tiles = width // LANES
    faces = depth + 1
    tiles = (rows_y // ROWS) * lane_tiles

    def rows(row, shift):
        return pl.ds(pl.multiple_of(row + shift, ROWS), ROWS)

    def place(number):
        lane = (number % lane_tiles) * LANES
        return (
            (number // lane_tiles) * ROWS,
            pl.ds(pl.multiple_of(lane, LANES), LANES),
            pl.ds(pl.multiple_of(lane + start_lane, LANES), LANES),
        )

    def point(number, carry):
        at, lane, there = place(number)
        row, mine = rows(at, 0), rows(at, start)
        own = [[state_ref[k, i, mine, there] for k in range(5)] for i in range(depth)]
        cells = []
        for i in range(3):
            cells.append(
                [
                    jnp.where(
                        first,
                        own[0][k],
                        jnp.where(
                            even,
                            far_ref[3 * k + i, row, lane],
                            pair_ref[depth * k + depth - 3 + i, row, lane],
                        ),
                    )
                    for k in range(5)
                ]
            )
        cells += own
        for i in range(3):
            cells.append(
                [
                    jnp.where(
                        last,
                        own[depth - 1][k],
                        jnp.where(
                            even,
                            pair_ref[depth * k + i, row, lane],
                            far_ref[3 * k + i, row, lane],
                        ),
                    )
                    for k in range(5)
                ]
            )
        speeds, before = [], None
        for j, q in enumerate(cells):
            flux, pressure, thin, along = flux_of(q, 0)
            speeds.append(speed_of(pressure, thin, along))
            if j > 0:
                for k in range(5):
                    dq_s[number, k, j - 1] = q[k] - cells[j - 1][k]
                    df_s[number, k, j - 1] = flux[k] - before[k]
                    if 3 <= j < 3 + faces:
                        both_s[number, k, j - 3] = flux[k] + before[k]
            before = flux
        pairs = [jnp.maximum(speeds[i], speeds[i + 1]) for i in range(depth + 5)]
        for f in range(faces):
            alpha_s[number, f] = jnp.maximum(jnp.maximum(pairs[f], pairs[f + 2]), pairs[f + 4])
        return carry

    lax.fori_loop(0, tiles, point, 0)

    def faces_of(sum_ref, sum_shift, number, carry):
        at, lane, there = place(number)
        row, mine = rows(at, 0), rows(at, start)
        border = jnp.where(
            even, pair_ref[depth * fields, row, lane], far_ref[3 * fields, row, lane]
        )
        border = jnp.where(last, 0.0, border)
        switches = [mask_ref[i, mine, there] > 0 for i in range(depth)] + [border > 0.0]
        results = []
        for k in range(5):
            dq = [dq_s[number, k, j] for j in range(depth + 5)]
            df = [df_s[number, k, j] for j in range(depth + 5)]
            hats = [
                face_value(
                    dq[f : f + 5], df[f : f + 5], both_s[number, k, f], alpha_s[number, f], switches[f]
                )
                for f in range(faces)
            ]
            plane = 0
            for acc_ref, count in zip(acc_refs, counts):
                for i in range(count):
                    results.append(
                        acc_ref[k, i, mine, there]
                        - TIME_STEP * sum_ref[k, plane, rows(at, sum_shift), there]
                        + FACE_SCALE * (hats[plane + 1] - hats[plane])
                    )
                    plane += 1
        for k in range(5):
            for i in range(depth):
                result[k, i, row, lane] = results[k * depth + i]
        hand_out(number).start()
        return carry

    def hand_out(number):
        at, lane, there = place(number)
        return pltpu.make_async_copy(
            result.at[:, :, rows(at, 0), lane],
            out_ref.at[:, :, rows(at, start), there],
            sem.at[number],
        )

    def settle(number, carry):
        hand_out(number).wait()
        return carry

    for sum_ref, (low, high, sum_shift) in zip(sum_refs, segments):
        lax.fori_loop(
            low // ROWS * lane_tiles,
            high // ROWS * lane_tiles,
            functools.partial(faces_of, sum_ref, sum_shift),
            0,
        )
    lax.fori_loop(0, tiles, settle, 0)


def stream_part(state, pair, far, mask_x, part, arrived, accs, out):
    fields, depth, rows_all, _ = state.shape
    start, rows_y, _, width = part
    tiles = rows_y * width // (ROWS * LANES)
    counts = [acc.shape[1] for acc in accs]
    extra = [] if out is None else [out]
    wide = rows_all // len(arrived)
    sums, segments = [], []
    for number, array in enumerate(arrived):
        low = max(start, number * wide)
        high = min(start + rows_y, (number + 1) * wide)
        if low < high:
            sums.append(array)
            segments.append((low - start, high - start, start - number * wide))
    count = 4 + len(sums) + len(accs)

    def vregs(*dims):
        return pltpu.VMEM(dims + (ROWS, LANES), jnp.float32)

    return call(
        functools.partial(stream_kernel, part, segments, counts),
        "stream_faces",
        0.6 * tiles,
        [PLACE] * count + [HBM] * len(extra),
        [HBM, PLACE],
        [shape_of(*state.shape), shape_of(ROWS, LANES)],
        [
            vregs(tiles, fields, depth + 5),
            vregs(tiles, fields, depth + 5),
            vregs(tiles, fields, depth + 1),
            vregs(tiles, depth + 1),
            pltpu.VMEM((fields, depth, rows_y, width), jnp.float32),
            pltpu.SemaphoreType.DMA((tiles,)),
        ],
        {count: 0} if extra else None,
    )(state, pair, far, mask_x, *sums, *accs, *extra)


def circulant_tables(span):
    half = span // 2
    step = 1
    while step * step < half:
        step *= 2
    count = half // step
    places = np.arange(span)
    period = max(2 * count, LANES)
    high = 2.0 * np.pi / span * ((np.arange(count)[:, None] * step * places[None, :period]) % span)
    low = 2.0 * np.pi / span * ((np.arange(step)[:, None] * places[None]) % span)
    tables = [np.concatenate([np.cos(a), np.sin(a)]) for a in (high, low)]
    return step, count, [jnp.asarray(t.astype(np.float32)) for t in tables]


def circulant_kernel(
    count, step, filter_ref, inner_ref, outer_ref, after_ref, high_ref, low_ref, band
):
    period = inner_ref.shape[1]
    span = outer_ref.shape[1]
    tall, wide = high_ref.shape
    order = step * lax.broadcasted_iota(
        jnp.int32, (count, step), 0
    ) + lax.broadcasted_iota(jnp.int32, (count, step), 1)
    scale = 2.0 / span * (2.0 * np.pi / span) * order.astype(jnp.float32) * filter_ref[...]

    def dot(table):
        return lax.dot_general(
            scale,
            table,
            (((0,), (0,)), ((), ())),
            precision=lax.Precision.HIGHEST,
            preferred_element_type=jnp.float32,
        )

    repeat = span // period
    inner_cos = jnp.concatenate([dot(inner_ref[:count])] * repeat, 1)
    inner_sin = jnp.concatenate([dot(inner_ref[count:])] * repeat, 1)
    line = jnp.sum(
        outer_ref[step:] * inner_cos + outer_ref[:step] * inner_sin, axis=0, keepdims=True
    )
    base = jnp.broadcast_to(-line, (ROWS, span))
    place = lax.broadcasted_iota(jnp.int32, (ROWS, span), 0)
    skew = base
    for i in range(1, ROWS):
        skew = jnp.where(place == i, pltpu.roll(base, i, 1), skew)
    for b in range(LANES // ROWS):
        rows = skew if b == 0 else pltpu.roll(skew, b * ROWS, 1)
        for q in range(tall // LANES):
            at = q * LANES + b * ROWS
            first = q * LANES
            if first:
                band[at : at + ROWS, :first] = rows[:, span - first :]
            band[at : at + ROWS, first:span] = rows[:, : span - first]
    full = band[...]
    high = full.astype(jnp.bfloat16)
    low = (full - high.astype(jnp.float32)).astype(jnp.bfloat16)
    high_ref[:, :span] = high
    low_ref[:, :span] = low
    high_ref[:, span:] = high[:, : wide - span]
    low_ref[:, span:] = low[:, : wide - span]


def circulant(span_filter, span, width, after):
    tall = min(256, width)
    step, count, tables = circulant_tables(span)
    band = shape_of(tall, span + width, dtype=jnp.bfloat16)
    return call(
        functools.partial(circulant_kernel, count, step),
        "circulant_band",
        1.0,
        [PLACE, PLACE, PLACE, ANYWHERE],
        [PLACE, PLACE],
        [band, band],
        [pltpu.VMEM((tall, span), jnp.float32)],
    )(span_filter.reshape(count, step), *tables, after)


def fill_lines(shards, x_refs):
    _, depth, rows_y, width = shards[0].shape
    xh, xl = x_refs
    for number, shard in enumerate(shards):

        def plane(index, carry):
            i = index // (width // LANES)
            t = index % (width // LANES)
            flux, _, _, _ = flux_of([shard[k, i, :, lanes(t)] for k in range(5)], 2)
            to = lanes(t + number * (width // LANES))
            for k in range(5):
                high = flux[k].astype(jnp.bfloat16)
                line = pl.ds(pl.multiple_of((k * depth + i) * rows_y, rows_y), rows_y)
                xh[line, to] = high
                xl[line, to] = (flux[k] - high.astype(jnp.float32)).astype(jnp.bfloat16)
            return carry

        lax.fori_loop(0, depth * (width // LANES), plane, 0)


def product(target, sources, high_ref, low_ref, xh, xl, w_s):
    tall, wide = high_ref.shape
    width = xh.shape[1] // len(sources)
    span = wide - width
    deep = xh.shape[1]
    for number, source in enumerate(sources):
        for q in range(width // tall):
            start = lax.rem((target - source) * width - q * tall + 2 * span, span)
            start = pl.multiple_of(start, LANES)
            at = number * width + q * tall
            w_s[at : at + tall, :] = high_ref[:, pl.ds(start, width)]
            w_s[deep + at : deep + at + tall, :] = low_ref[:, pl.ds(start, width)]
    dot = functools.partial(jnp.dot, preferred_element_type=jnp.float32)
    high = w_s[:deep, :]
    return dot(xh[...], high) + dot(xl[...], high) + dot(xh[...], w_s[deep:, :])


def away_kernel(masks, parts, high_ref, low_ref, own_ref, core_ref, after_ref, *refs):
    sums = refs[: len(masks) * parts]
    xh, xl, w_s = refs[len(masks) * parts :]
    fields, depth, rows_all, width = own_ref.shape
    rows_y = rows_all // parts
    me = lax.axis_index("gz")
    fill_lines([own_ref, core_ref], [xh, xl])
    for number, mask in enumerate(masks):
        total = product(me ^ mask, [me, me ^ 1], high_ref, low_ref, xh, xl, w_s)
        total = total.reshape(fields, depth, rows_all, width)
        for c in range(parts):
            sums[number * parts + c][...] = total[:, :, c * rows_y : (c + 1) * rows_y, :]


def away_part(band, state, core, masks, parts, after):
    fields, depth, rows_all, width = state.shape
    lines = fields * depth * rows_all
    line = shape_of(lines, 2 * width, dtype=jnp.bfloat16)
    count = len(masks) * parts
    outs = call(
        functools.partial(away_kernel, masks, parts),
        "span_away",
        3.0,
        [PLACE] * 4 + [ANYWHERE],
        [PLACE] * (count + 2),
        [shape_of(fields, depth, rows_all // parts, width)] * count + [line, line],
        [pltpu.VMEM((4 * width, width), jnp.bfloat16)],
    )(*band, state, core, after)
    return outs[:count], outs[count:]


def home_kernel(high_ref, low_ref, xh, xl, state_ref, out_ref, w_s):
    me = lax.axis_index("gz")
    total = product(me, [me, me ^ 1], high_ref, low_ref, xh, xl, w_s)
    out_ref[...] = state_ref[...] - TIME_STEP * total.reshape(state_ref.shape)


def home_part(band, lines, state):
    width = state.shape[3]
    return call(
        home_kernel,
        "span_home",
        2.0,
        [PLACE] * 5,
        PLACE,
        shape_of(*state.shape),
        [pltpu.VMEM((4 * width, width), jnp.bfloat16)],
    )(*band, *lines, state)


def per_device(state, mask_x, mask_y, span_filter):
    fields, depth, rows_all, width = state.shape
    groups = lax.axis_size("gz")
    slabs = lax.axis_size("gx")
    span = width * groups

    def flip(array, bit):
        return lax.ppermute(array, "gz", [(g, g ^ bit) for g in range(groups)])

    swap = [(i, i ^ 1) for i in range(slabs)]
    carry = [(i, i + 2) for i in range(0, slabs - 2, 2)] + [
        (i, i - 2) for i in range(3, slabs, 2)
    ]
    core = flip(state, 1)
    if width % (4 * LANES) == 0:
        narrow = width // 4
        parts = [
            (0, rows_all // 2, 0, width - narrow),
            (rows_all // 2, rows_all // 2, 0, width - narrow),
            (0, rows_all, width - narrow, narrow),
        ]
    else:
        part = rows_all // 4
        parts = [(0, 2 * part, 0, width), (2 * part, part, 0, width), (3 * part, part, 0, width)]
    bricks = pack_part(state, mask_x, parts)
    pairs = [lax.ppermute(brick, "gx", swap) for brick in bricks]
    band = circulant(span_filter, span, width, core)

    masks = list(range(2, groups, 2))
    sums, lines = away_part(band, state, core, masks, SUM_PARTS, bricks[0])
    arrived = [
        sum(flip(sums[n * SUM_PARTS + c], mask) for n, mask in enumerate(masks))
        for c in range(SUM_PARTS)
    ]
    half = depth // 2

    def hand_on(c, after):
        return lax.ppermute(pass_part(pairs[c], depth, after), "gx", carry)

    def stream(c, out):
        return stream_part(
            state, pairs[c], fars[c], mask_x, parts[c], arrived, [acc_low, acc_high], out
        )

    base = home_part(band, lines, state)
    fars = [hand_on(0, base)]
    acc_low = wall_part(state, mask_y, base, 0, half, base)
    acc_high = wall_part(state, mask_y, base, half, depth - half, acc_low)
    fars.append(hand_on(1, acc_high))
    out, token = stream(0, None)
    fars.append(hand_on(2, token))
    out, _ = stream(1, out)
    out, _ = stream(2, out)
    return out


def solution(mesh):
    return jax.shard_map(
        per_device,
        mesh=mesh,
        in_specs=(P(None, "gx", None, "gz"), P("gx", None, "gz"), P("gx", None, "gz"), P()),
        out_specs=P(None, "gx", None, "gz"),
        check_vma=False,
    )
```

profile of v0, /device:TPU:0, one launch (start us, length us, event | category | flops | bytes accessed | tf_op | source)
XLA Modules:
  0.0 49.8 jit_solution(17614450470024646799)
XLA Ops:
  0.0 0.0 copy-start.5
  0.0 0.0 copy-start.6
  0.0 0.5 collective-permute-start.2
  0.5 2.4 %pack_bricks.1 = (f32[21,16,384]{2,1,0:T(8,128)}, f32[21,16,384]{2,1,0:T(8,128)}, f32[21,32,128]{2,1,0:T(8,128)}) custom-call(f32[20,32,512]{2,1,0:T(8,128)} %bitcast.1, s32[4,32,512]{2,1,0:T(8,128)} %refs_3_.5), custom_call_target="tpu_custom_call" | custom-call | flops 100000000 | bytes 300000 | tf_op jit(solution)/shard_map/pack_bricks/pallas_call | solution.py:230
  2.9 0.0 copy-start
  2.9 2.6 %collective-permute-start.1 = (f32[21,16,384]{2,1,0:T(8,128)}, f32[21,16,384]{2,1,0:T(8,128)S(1)}, u32[]{:S(2)}, u32[]{:S(2)}) collective-permute-start(f32[21,16,384]{2,1,0:T(8,128)} %get-tuple-element.19.after_ref), channel_id=1, source_target_pairs={{0,4},{4,0},{8,12},{12,8},{16,20},{20,16},{24,28},{28,24},{1,5},{5... | collective-permute-start | bytes 1548296 | tf_op jit(solution)/shard_map/ppermute | solution.py:629
  5.5 0.0 copy-done.6
  5.5 0.1 reshape.7.filter_ref
  5.5 0.0 collective-permute-done.2.after_ref.core_ref
  5.6 0.0 copy-done.5
  5.6 0.0 copy-start.3
  5.6 1.0 %copy-done.3 = f32[64,2048]{1,0:T(8,128)S(1)} copy-done((f32[64,2048]{1,0:T(8,128)S(1)}, f32[64,2048]{1,0:T(8,128)}, u32[]{:S(2)}) %copy-start.3) | copy-done | bytes 524312
  6.6 0.0 copy-start.4
  6.6 0.8 %circulant_band.1 = (bf16[256,2560]{1,0:T(8,128)(2,1)S(1)}, bf16[256,2560]{1,0:T(8,128)(2,1)S(1)}) custom-call(f32[32,32]{1,0:T(8,128)S(1)} %reshape.7.filter_ref, f32[64,128]{1,0:T(8,128)S(1)} %copy-done.5, f32[64,2048]{1,0:T(8,128)S(1)} %copy-done.3, f32[5,4,32,512]{3,2,1,0:T(8,128)S(1)} %collective-permute-done.2.after_ref.core_ref), custom_call_target="tpu_custom_call" | custom-call | flops 100000000 | bytes 300000 | tf_op jit(solution)/shard_map/circulant_band/pallas_call | solution.py:506
  7.4 0.0 copy-done
  7.4 0.2 copy-done.4
  7.6 0.0 copy-start.7
  7.6 3.4 %span_away.1 = (f32[5,4,16,512]{3,2,1,0:T(8,128)S(1)}, f32[5,4,16,512]{3,2,1,0:T(8,128)S(1)}, bf16[640,1024]{1,0:T(8,128)(2,1)S(1)}, bf16[640,1024]{1,0:T(8,128)(2,1)S(1)}) custom-call(bf16[256,2560]{1,0:T(8,128)(2,1)S(1)} %get-tuple-element.20.high_ref, bf16[256,2560]{1,0:T(8,128)(2,1)S(1)} %get-tuple-element.21.low_ref, f32[5,4,32,512]{3,2,1,0:T(8,128)S(1)} %copy-done, ...), custom_call_target="tpu_custom_call" | custom-call | flops 300000000 | bytes 900000 | tf_op jit(solution)/shard_map/span_away/pallas_call | solution.py:573
  11.1 1.6 %collective-permute-start.4 = (f32[5,4,16,512]{3,2,1,0:T(8,128)S(1)}, f32[5,4,16,512]{3,2,1,0:T(8,128)S(1)}, u32[]{:S(2)}, u32[]{:S(2)}) collective-permute-start(f32[5,4,16,512]{3,2,1,0:T(8,128)S(1)} %get-tuple-element.24), channel_id=1, source_target_pairs={{0,2},{1,3},{2,0},{3,1},{4,6},{5,7},{6,4},{7,5},{8,10},{9,11},{10,... | collective-permute-start | bytes 1966088 | tf_op jit(solution)/shard_map/ppermute | solution.py:611
  12.6 0.0 copy-done.7
  12.6 0.6 %collective-permute-start.7 = (f32[21,16,384]{2,1,0:T(8,128)S(1)}, f32[21,16,384]{2,1,0:T(8,128)S(1)}, u32[]{:S(2)}, u32[]{:S(2)}) collective-permute-start(f32[21,16,384]{2,1,0:T(8,128)S(1)} %copy-done.7), channel_id=1, source_target_pairs={{0,4},{4,0},{8,12},{12,8},{16,20},{20,16},{24,28},{28,24},{1,5},{5... | collective-permute-start | bytes 1548296 | tf_op jit(solution)/shard_map/ppermute | solution.py:629
  13.3 2.2 %span_home.1.after_ref.base_ref = f32[5,4,32,512]{3,2,1,0:T(8,128)S(1)} custom-call(bf16[256,2560]{1,0:T(8,128)(2,1)S(1)} %get-tuple-element.20.high_ref, bf16[256,2560]{1,0:T(8,128)(2,1)S(1)} %get-tuple-element.21.low_ref, bf16[640,1024]{1,0:T(8,128)(2,1)S(1)} %get-tuple-element.22.xh, bf16[640,1024]{1,0:T(8,128)(2,1)S(1)} %get-tuple-element.23.xl, ...), custom_call_target="tpu_custom_call" | custom-call | flops 200000000 | bytes 600000 | tf_op jit(solution)/shard_map/span_home/pallas_call | solution.py:593
  15.5 0.0 copy-start.8
  15.5 0.0 copy-start.2
  15.5 2.8 %collective-permute-done.1.pair_ref.refs_1_ = f32[21,16,384]{2,1,0:T(8,128)S(1)} collective-permute-done((f32[21,16,384]{2,1,0:T(8,128)}, f32[21,16,384]{2,1,0:T(8,128)S(1)}, u32[]{:S(2)}, u32[]{:S(2)}) %collective-permute-start.1) | collective-permute-done | bytes 516128 | tf_op jit(solution)/shard_map/ppermute | solution.py:629
  18.3 4.0 %collective-permute-start.3 = (f32[16,16,384]{2,1,0:T(8,128)S(1)}, f32[16,16,384]{2,1,0:T(8,128)S(1)}, u32[]{:S(2)}, u32[]{:S(2)}) collective-permute-start(f32[16,16,384]{2,1,0:T(8,128)S(1)} %pass_planes.3), channel_id=1, source_target_pairs={{0,8},{8,16},{16,24},{12,4},{20,12},{28,20},{1,9},{9,17},{17,25},{... | collective-permute-start | bytes 1179656 | tf_op jit(solution)/shard_map/ppermute | solution.py:641
  22.3 1.6 %collective-permute-start.6 = (f32[5,4,16,512]{3,2,1,0:T(8,128)S(1)}, f32[5,4,16,512]{3,2,1,0:T(8,128)S(1)}, u32[]{:S(2)}, u32[]{:S(2)}) collective-permute-start(f32[5,4,16,512]{3,2,1,0:T(8,128)S(1)} %get-tuple-element.26), channel_id=1, source_target_pairs={{0,2},{1,3},{2,0},{3,1},{4,6},{5,7},{6,4},{7,5},{8,10},{9,11},{10,... | collective-permute-start | bytes 1966088 | tf_op jit(solution)/shard_map/ppermute | solution.py:611
  23.9 0.0 copy-done.8
  23.9 0.0 collective-permute-start
  23.9 0.0 copy-done.2
  23.9 2.9 %wall_faces.2.after_ref.refs_5_.refs_6_ = f32[5,2,32,512]{3,2,1,0:T(8,128)S(1)} custom-call(f32[5,4,32,512]{3,2,1,0:T(8,128)S(1)} %copy-done, s32[4,32,512]{2,1,0:T(8,128)S(1)} %copy-done.2, f32[5,4,32,512]{3,2,1,0:T(8,128)S(1)} %span_home.1.after_ref.base_ref, f32[5,4,32,512]{3,2,1,0:T(8,128)S(1)} %span_home.1.after_ref.base_ref), custom_call_target="tpu_custom_call" | custom-call | flops 250000000 | bytes 750000 | tf_op jit(solution)/shard_map/wall_faces/pallas_call | solution.py:193
  26.8 2.9 %wall_faces.3.refs_6_.after_ref.refs_7_ = f32[5,2,32,512]{3,2,1,0:T(8,128)S(1)} custom-call(f32[5,4,32,512]{3,2,1,0:T(8,128)S(1)} %copy-done, s32[4,32,512]{2,1,0:T(8,128)S(1)} %copy-done.2, f32[5,4,32,512]{3,2,1,0:T(8,128)S(1)} %span_home.1.after_ref.base_ref, f32[5,2,32,512]{3,2,1,0:T(8,128)S(1)} %wall_faces.2.after_ref.refs_5_.refs_6_), custom_call_target="tpu_custom_call" | custom-call | flops 250000000 | bytes 750000 | tf_op jit(solution)/shard_map/wall_faces/pallas_call | solution.py:193
  29.7 0.0 copy-start.1
  29.7 0.0 collective-permute-done.7.pair_ref.refs_1_
  29.8 3.8 %collective-permute-start.8 = (f32[16,16,384]{2,1,0:T(8,128)S(1)}, f32[16,16,384]{2,1,0:T(8,128)S(1)}, u32[]{:S(2)}, u32[]{:S(2)}) collective-permute-start(f32[16,16,384]{2,1,0:T(8,128)S(1)} %pass_planes.5), channel_id=1, source_target_pairs={{0,8},{8,16},{16,24},{12,4},{20,12},{28,20},{1,9},{9,17},{17,25},{... | collective-permute-start | bytes 1179656 | tf_op jit(solution)/shard_map/ppermute | solution.py:641
  33.6 0.0 collective-permute-done.3.refs_2_
  33.6 0.0 collective-permute-done.4.refs_4_
  33.6 0.0 copy-done.1
  33.7 3.5 %stream_faces.3 = (f32[5,4,32,512]{3,2,1,0:T(8,128)}, f32[8,128]{1,0:T(8,128)S(1)}) custom-call(f32[5,4,32,512]{3,2,1,0:T(8,128)S(1)} %copy-done, f32[21,16,384]{2,1,0:T(8,128)S(1)} %collective-permute-done.1.pair_ref.refs_1_, f32[16,16,384]{2,1,0:T(8,128)S(1)} %collective-permute-done.3.refs_2_, s32[4,32,512]{2,1,0:T(8,128)S(1)} %copy-done.1, ...), custom_call_target="tpu_custom_call" | custom-call | flops 360000000 | bytes 1080000 | tf_op jit(solution)/shard_map/stream_faces/pallas_call | solution.py:421
  37.1 0.0 collective-permute-done.pair_ref.refs_1_
  37.2 3.5 %collective-permute-start.5 = (f32[16,32,128]{2,1,0:T(8,128)S(1)}, f32[16,32,128]{2,1,0:T(8,128)S(1)}, u32[]{:S(2)}, u32[]{:S(2)}) collective-permute-start(f32[16,32,128]{2,1,0:T(8,128)S(1)} %pass_planes.4), channel_id=1, source_target_pairs={{0,8},{8,16},{16,24},{12,4},{20,12},{28,20},{1,9},{9,17},{17,25},{... | collective-permute-start | bytes 786440 | tf_op jit(solution)/shard_map/ppermute | solution.py:641
  40.7 1.5 %collective-permute-done.8.refs_2_ = f32[16,16,384]{2,1,0:T(8,128)S(1)} collective-permute-done((f32[16,16,384]{2,1,0:T(8,128)S(1)}, f32[16,16,384]{2,1,0:T(8,128)S(1)}, u32[]{:S(2)}, u32[]{:S(2)}) %collective-permute-start.8) | collective-permute-done | bytes 393248 | tf_op jit(solution)/shard_map/ppermute | solution.py:641
  42.1 0.0 collective-permute-done.6.refs_4_.refs_5_
  42.1 4.0 %stream_faces.4 = (f32[5,4,32,512]{3,2,1,0:T(8,128)}, f32[8,128]{1,0:T(8,128)}) custom-call(f32[5,4,32,512]{3,2,1,0:T(8,128)S(1)} %copy-done, f32[21,16,384]{2,1,0:T(8,128)S(1)} %collective-permute-done.7.pair_ref.refs_1_, f32[16,16,384]{2,1,0:T(8,128)S(1)} %collective-permute-done.8.refs_2_, ...), custom_call_target="tpu_custom_call", output_to_operand_aliasing={{0}: (7, {})} | custom-call | flops 360000000 | bytes 1080000 | tf_op jit(solution)/shard_map/stream_faces/pallas_call | solution.py:421
  46.2 0.6 %collective-permute-done.5.refs_2_ = f32[16,32,128]{2,1,0:T(8,128)S(1)} collective-permute-done((f32[16,32,128]{2,1,0:T(8,128)S(1)}, f32[16,32,128]{2,1,0:T(8,128)S(1)}, u32[]{:S(2)}, u32[]{:S(2)}) %collective-permute-start.5) | collective-permute-done | bytes 262176 | tf_op jit(solution)/shard_map/ppermute | solution.py:641
  46.8 3.0 %stream_faces.5 = (f32[5,4,32,512]{3,2,1,0:T(8,128)}, f32[8,128]{1,0:T(8,128)}) custom-call(f32[5,4,32,512]{3,2,1,0:T(8,128)S(1)} %copy-done, f32[21,32,128]{2,1,0:T(8,128)S(1)} %collective-permute-done.pair_ref.refs_1_, f32[16,32,128]{2,1,0:T(8,128)S(1)} %collective-permute-done.5.refs_2_, ...), custom_call_target="tpu_custom_call", output_to_operand_aliasing={{0}: (8, {})} | custom-call | flops 240000000 | bytes 720000 | tf_op jit(solution)/shard_map/stream_faces/pallas_call | solution.py:421
  (3 shorter events, 0.1 us)
Async XLA Ops:
  0.0 5.6 %copy-start.5 = (f32[64,128]{1,0:T(8,128)S(1)}, f32[64,128]{1,0:T(8,128)}, u32[]{:S(2)}) copy-start(f32[64,128]{1,0:T(8,128)} %constant.4.clone.inner_ref) | copy-start | bytes 98308
  0.0 5.5 %copy-start.6 = (f32[1024]{0:T(1024)S(1)}, f32[1024]{0:T(1024)}, u32[]{:S(2)}) copy-start(f32[1024]{0:T(1024)} %param.9) | copy-start | bytes 12292
  0.0 5.5 %collective-permute-start.2 = (f32[5,4,32,512]{3,2,1,0:T(8,128)}, f32[5,4,32,512]{3,2,1,0:T(8,128)S(1)}, u32[]{:S(2)}, u32[]{:S(2)}) collective-permute-start(f32[5,4,32,512]{3,2,1,0:T(8,128)} %refs_0_.5), channel_id=1, source_target_pairs={{0,1},{1,0},{2,3},{3,2},{4,5},{5,4},{6,7},{7,6},{8,9},{9,8},{10,11... | collective-permute-start | bytes 3932168 | tf_op jit(solution)/shard_map/ppermute | solution.py:611
  2.9 4.5 %copy-start = (f32[5,4,32,512]{3,2,1,0:T(8,128)S(1)}, f32[5,4,32,512]{3,2,1,0:T(8,128)}, u32[]{:S(2)}) copy-start(f32[5,4,32,512]{3,2,1,0:T(8,128)} %refs_0_.5) | copy-start | bytes 3932164
  2.9 15.4 %collective-permute-start.1 = (f32[21,16,384]{2,1,0:T(8,128)}, f32[21,16,384]{2,1,0:T(8,128)S(1)}, u32[]{:S(2)}, u32[]{:S(2)}) collective-permute-start(f32[21,16,384]{2,1,0:T(8,128)} %get-tuple-element.19.after_ref), channel_id=1, source_target_pairs={{0,4},{4,0},{8,12},{12,8},{16,20},{20,16},{24,28},{28,24},{1,5},{5... | collective-permute-start | bytes 1548296 | tf_op jit(solution)/shard_map/ppermute | solution.py:629
  5.6 1.0 %copy-start.3 = (f32[64,2048]{1,0:T(8,128)S(1)}, f32[64,2048]{1,0:T(8,128)}, u32[]{:S(2)}) copy-start(f32[64,2048]{1,0:T(8,128)} %constant.5.clone.outer_ref) | copy-start | bytes 1572868
  6.6 1.0 %copy-start.4 = (f32[21,16,384]{2,1,0:T(8,128)S(1)}, f32[21,16,384]{2,1,0:T(8,128)}, u32[]{:S(2)}) copy-start(f32[21,16,384]{2,1,0:T(8,128)} %get-tuple-element.19.after_ref) | copy-start | bytes 1548292
  7.6 5.0 %copy-start.7 = (f32[21,16,384]{2,1,0:T(8,128)S(1)}, f32[21,16,384]{2,1,0:T(8,128)}, u32[]{:S(2)}) copy-start(f32[21,16,384]{2,1,0:T(8,128)} %get-tuple-element.27) | copy-start | bytes 1548292
  11.1 22.6 %collective-permute-start.4 = (f32[5,4,16,512]{3,2,1,0:T(8,128)S(1)}, f32[5,4,16,512]{3,2,1,0:T(8,128)S(1)}, u32[]{:S(2)}, u32[]{:S(2)}) collective-permute-start(f32[5,4,16,512]{3,2,1,0:T(8,128)S(1)} %get-tuple-element.24), channel_id=1, source_target_pairs={{0,2},{1,3},{2,0},{3,1},{4,6},{5,7},{6,4},{7,5},{8,10},{9,11},{10,... | collective-permute-start | bytes 1966088 | tf_op jit(solution)/shard_map/ppermute | solution.py:611
  12.6 17.1 %collective-permute-start.7 = (f32[21,16,384]{2,1,0:T(8,128)S(1)}, f32[21,16,384]{2,1,0:T(8,128)S(1)}, u32[]{:S(2)}, u32[]{:S(2)}) collective-permute-start(f32[21,16,384]{2,1,0:T(8,128)S(1)} %copy-done.7), channel_id=1, source_target_pairs={{0,4},{4,0},{8,12},{12,8},{16,20},{20,16},{24,28},{28,24},{1,5},{5... | collective-permute-start | bytes 1548296 | tf_op jit(solution)/shard_map/ppermute | solution.py:629
  15.5 8.4 %copy-start.8 = (f32[21,32,128]{2,1,0:T(8,128)S(1)}, f32[21,32,128]{2,1,0:T(8,128)}, u32[]{:S(2)}) copy-start(f32[21,32,128]{2,1,0:T(8,128)} %get-tuple-element.18) | copy-start | bytes 1032196
  15.5 8.4 %copy-start.2 = (s32[4,32,512]{2,1,0:T(8,128)S(1)}, s32[4,32,512]{2,1,0:T(8,128)}, u32[]{:S(2)}) copy-start(s32[4,32,512]{2,1,0:T(8,128)} %mask_ref.5) | copy-start | bytes 786436
  18.3 15.3 %collective-permute-start.3 = (f32[16,16,384]{2,1,0:T(8,128)S(1)}, f32[16,16,384]{2,1,0:T(8,128)S(1)}, u32[]{:S(2)}, u32[]{:S(2)}) collective-permute-start(f32[16,16,384]{2,1,0:T(8,128)S(1)} %pass_planes.3), channel_id=1, source_target_pairs={{0,8},{8,16},{16,24},{12,4},{20,12},{28,20},{1,9},{9,17},{17,25},{... | collective-permute-start | bytes 1179656 | tf_op jit(solution)/shard_map/ppermute | solution.py:641
  22.3 19.9 %collective-permute-start.6 = (f32[5,4,16,512]{3,2,1,0:T(8,128)S(1)}, f32[5,4,16,512]{3,2,1,0:T(8,128)S(1)}, u32[]{:S(2)}, u32[]{:S(2)}) collective-permute-start(f32[5,4,16,512]{3,2,1,0:T(8,128)S(1)} %get-tuple-element.26), channel_id=1, source_target_pairs={{0,2},{1,3},{2,0},{3,1},{4,6},{5,7},{6,4},{7,5},{8,10},{9,11},{10,... | collective-permute-start | bytes 1966088 | tf_op jit(solution)/shard_map/ppermute | solution.py:611
  23.9 13.3 %collective-permute-start = (f32[21,32,128]{2,1,0:T(8,128)S(1)}, f32[21,32,128]{2,1,0:T(8,128)S(1)}, u32[]{:S(2)}, u32[]{:S(2)}) collective-permute-start(f32[21,32,128]{2,1,0:T(8,128)S(1)} %copy-done.8), channel_id=1, source_target_pairs={{0,4},{4,0},{8,12},{12,8},{16,20},{20,16},{24,28},{28,24},{1,5},{5... | collective-permute-start | bytes 1032200 | tf_op jit(solution)/shard_map/ppermute | solution.py:629
  29.7 3.9 %copy-start.1 = (s32[4,32,512]{2,1,0:T(8,128)S(1)}, s32[4,32,512]{2,1,0:T(8,128)}, u32[]{:S(2)}) copy-start(s32[4,32,512]{2,1,0:T(8,128)} %refs_3_.5) | copy-start | bytes 786436
  29.8 12.4 %collective-permute-start.8 = (f32[16,16,384]{2,1,0:T(8,128)S(1)}, f32[16,16,384]{2,1,0:T(8,128)S(1)}, u32[]{:S(2)}, u32[]{:S(2)}) collective-permute-start(f32[16,16,384]{2,1,0:T(8,128)S(1)} %pass_planes.5), channel_id=1, source_target_pairs={{0,8},{8,16},{16,24},{12,4},{20,12},{28,20},{1,9},{9,17},{17,25},{... | collective-permute-start | bytes 1179656 | tf_op jit(solution)/shard_map/ppermute | solution.py:641
  37.2 9.6 %collective-permute-start.5 = (f32[16,32,128]{2,1,0:T(8,128)S(1)}, f32[16,32,128]{2,1,0:T(8,128)S(1)}, u32[]{:S(2)}, u32[]{:S(2)}) collective-permute-start(f32[16,32,128]{2,1,0:T(8,128)S(1)} %pass_planes.4), channel_id=1, source_target_pairs={{0,8},{8,16},{16,24},{12,4},{20,12},{28,20},{1,9},{9,17},{17,25},{... | collective-permute-start | bytes 786440 | tf_op jit(solution)/shard_map/ppermute | solution.py:641
where the time goes:
time: 50.1 us; the launch traced here: 49.8 us
  Pallas kernels  25.3 us (50%)
  starting transfers between devices  18.1 us (36%)
  waiting for transfers between devices  4.83 us (10%)
  local copies, waits for them, and re-layouts  1.38 us (3%)
    ppermute x3, starting transfers between devices, hand_on(): return lax.ppermute(pass_part(pairs[c], depth, after), 'gx', carry)  11.3 us
    pallas_call x3, Pallas kernels, stream_part(): call(functools.partial(stream_kernel, part, segments, counts), 'stream_fa...  10.6 us
    pallas_call x2, Pallas kernels, wall_part(): call(kernel, 'wall_faces', 5.0 * count / depth, [PLACE, PLACE, PLACE, ANY...  5.83 us
    ppermute x3, starting transfers between devices, flip(): return lax.ppermute(array, 'gz', [(g, g ^ bit) for g in range(groups)])  3.62 us
    pallas_call x1, Pallas kernels, away_part(): call(functools.partial(away_kernel, masks, parts), 'span_away', 3.0, [PLA...  3.41 us
    ppermute x3, starting transfers between devices, per_device(): pairs = [lax.ppermute(brick, 'gx', swap) for brick in bricks]  3.22 us
    ppermute x3, waiting for transfers between devices, per_device(): pairs = [lax.ppermute(brick, 'gx', swap) for brick in bricks]  2.78 us
    pallas_call x1, Pallas kernels, pack_part(): call(functools.partial(pack_kernel, parts), 'pack_bricks', 1.0, [HBM, HBM...  2.42 us
  transfers between devices with their start and end apart: 9, of which 3 were waited for; matrix products, arithmetic and copies ran while one was open for 0% of the time, Pallas kernels for 45%

commit v1 on v0

--- a/solution.py
+++ b/solution.py
@@ -13,7 +13,6 @@
 TIME_STEP = 0.1
 ROWS = 8
 LANES = 128
-SUM_PARTS = 2
 VMEM_BYTES = 24 * 1024 * 1024
 PACK_BYTES = 60 * 1024 * 1024
 FACE_SCALE = -TIME_STEP / 60.0
@@ -32,7 +31,7 @@
         input_output_aliases=aliases or {},
         compiler_params=pltpu.CompilerParams(vmem_limit_bytes=vmem),
         cost_estimate=pl.CostEstimate(
-            flops=int(weight * 1e8), bytes_accessed=int(weight * 3e5), transcendentals=0
+            flops=int(weight * 1e9), bytes_accessed=int(weight * 3e6), transcendentals=0
         ),
         name=name,
     )
@@ -242,6 +241,36 @@
     )(state.reshape(planes, rows_all, width), mask_x)
 
 
+def bring_kernel(part, pieces, state_ref, mask_ref, after_ref, *outs):
+    row, rows, lane, width = part
+    fields, depth, _, _ = state_ref.shape
+    odd = lax.rem(lax.axis_index("gx"), 2)
+    for piece, out in zip(pieces, outs):
+        count = depth if piece == "all" else 3
+        skip = {"all": 0, "pair": 1 - odd, "across": odd}[piece] * (depth - 3)
+        for k in range(fields):
+            for i in range(count):
+                out[count * k + i] = state_ref[k, i + skip, row : row + rows, lane : lane + width]
+        switches = mask_ref[0, row : row + rows, lane : lane + width]
+        out[count * fields] = switches.astype(jnp.float32)
+
+
+def bring_part(state, mask_x, part, pieces, after):
+    fields, depth, _, _ = state.shape
+    _, rows, _, width = part
+    return call(
+        functools.partial(bring_kernel, part, pieces),
+        "bring_planes",
+        0.5,
+        [PLACE, PLACE, ANYWHERE],
+        [PLACE] * len(pieces),
+        [
+            shape_of((depth if piece == "all" else 3) * fields + 1, rows, width)
+            for piece in pieces
+        ],
+    )(state, mask_x, after)
+
+
 def pass_kernel(depth, pair_ref, after_ref, out_ref):
     planes = pair_ref.shape[0] - 1
     skip = 1 - lax.rem(lax.axis_index("gx"), 2)
@@ -263,14 +292,19 @@
     )(pair, after)
 
 
-def stream_kernel(part, segments, counts, *refs):
+def stream_kernel(part, others, counts, *refs):
     state_ref, pair_ref, far_ref, mask_ref = refs[:4]
-    sum_refs = refs[4 : 4 + len(segments)]
-    acc_refs = refs[4 + len(segments) : 4 + len(segments) + len(counts)]
-    out_ref, token_ref, dq_s, df_s, both_s, alpha_s, result, sem = refs[-8:]
-    token_ref[...] = jnp.zeros_like(token_ref)
+    acc_refs, refs = refs[4 : 4 + len(counts)], refs[4 + len(counts) :]
+    if others is None:
+        _, out_ref, dq_s, df_s, both_s, alpha_s = refs
+        result = out_ref
+    else:
+        sum_ref, other_refs, refs = refs[0], refs[1 : 1 + len(others)], refs[1 + len(others) :]
+        out_ref, dq_s, df_s, both_s, alpha_s, result, sem, other_sem = refs[:8]
+        staged = refs[8:]
     fields, depth, _, _ = state_ref.shape
     start, rows_y, start_lane, width = part
+    stride = (pair_ref.shape[0] - 1) // fields
     rank = lax.axis_index("gx")
     even = lax.rem(rank, 2) == 0
     first = rank == 0
@@ -304,7 +338,7 @@
                         jnp.where(
                             even,
                             far_ref[3 * k + i, row, lane],
-                            pair_ref[depth * k + depth - 3 + i, row, lane],
+                            pair_ref[stride * k + stride - 3 + i, row, lane],
                         ),
                     )
                     for k in range(5)
@@ -319,7 +353,7 @@
                         own[depth - 1][k],
                         jnp.where(
                             even,
-                            pair_ref[depth * k + i, row, lane],
+                            pair_ref[stride * k + i, row, lane],
                             far_ref[3 * k + i, row, lane],
                         ),
                     )
@@ -344,11 +378,11 @@
 
     lax.fori_loop(0, tiles, point, 0)
 
-    def faces_of(sum_ref, sum_shift, number, carry):
+    def faces_of(number, carry):
         at, lane, there = place(number)
         row, mine = rows(at, 0), rows(at, start)
         border = jnp.where(
-            even, pair_ref[depth * fields, row, lane], far_ref[3 * fields, row, lane]
+            even, pair_ref[stride * fields, row, lane], far_ref[3 * fields, row, lane]
         )
         border = jnp.where(last, 0.0, border)
         switches = [mask_ref[i, mine, there] > 0 for i in range(depth)] + [border > 0.0]
@@ -365,16 +399,16 @@
             plane = 0
             for acc_ref, count in zip(acc_refs, counts):
                 for i in range(count):
-                    results.append(
-                        acc_ref[k, i, mine, there]
-                        - TIME_STEP * sum_ref[k, plane, rows(at, sum_shift), there]
-                        + FACE_SCALE * (hats[plane + 1] - hats[plane])
-                    )
+                    value = acc_ref[k, i, mine, there] + FACE_SCALE * (hats[plane + 1] - hats[plane])
+                    if others is not None:
+                        value = value - TIME_STEP * sum_ref[k, plane, mine, there]
+                    results.append(value)
                     plane += 1
         for k in range(5):
             for i in range(depth):
                 result[k, i, row, lane] = results[k * depth + i]
-        hand_out(number).start()
+        if others is not None:
+            hand_out(number).start()
         return carry
 
     def hand_out(number):
@@ -389,52 +423,76 @@
         hand_out(number).wait()
         return carry
 
-    for sum_ref, (low, high, sum_shift) in zip(sum_refs, segments):
-        lax.fori_loop(
-            low // ROWS * lane_tiles,
-            high // ROWS * lane_tiles,
-            functools.partial(faces_of, sum_ref, sum_shift),
-            0,
+    copies = []
+    for number, other in enumerate(others or []):
+        top, tall, left, wide = other
+
+        def line(index, carry, number=number, top=top, tall=tall, left=left, wide=wide):
+            k, i = index // depth, index % depth
+            staged[number][k, i] = other_refs[number][k, i] - TIME_STEP * (
+                sum_ref[k, i, top : top + tall, left : left + wide]
+            )
+            return carry
+
+        lax.fori_loop(0, fields * depth, line, 0)
+        copy = pltpu.make_async_copy(
+            staged[number],
+            out_ref.at[:, :, pl.ds(top, tall), pl.ds(left, wide)],
+            other_sem.at[number],
         )
-    lax.fori_loop(0, tiles, settle, 0)
-
-
-def stream_part(state, pair, far, mask_x, part, arrived, accs, out):
-    fields, depth, rows_all, _ = state.shape
-    start, rows_y, _, width = part
+        copy.start()
+        copies.append(copy)
+    lax.fori_loop(0, tiles, faces_of, 0)
+    if others is not None:
+        lax.fori_loop(0, tiles, settle, 0)
+    for copy in copies:
+        copy.wait()
+
+
+def stream_part(state, pair, far, mask_x, part, accs, after=None, arrived=None, others=None):
+    fields, depth, _, _ = state.shape
+    _, rows_y, _, width = part
     tiles = rows_y * width // (ROWS * LANES)
     counts = [acc.shape[1] for acc in accs]
-    extra = [] if out is None else [out]
-    wide = rows_all // len(arrived)
-    sums, segments = [], []
-    for number, array in enumerate(arrived):
-        low = max(start, number * wide)
-        high = min(start + rows_y, (number + 1) * wide)
-        if low < high:
-            sums.append(array)
-            segments.append((low - start, high - start, start - number * wide))
-    count = 4 + len(sums) + len(accs)
 
     def vregs(*dims):
         return pltpu.VMEM(dims + (ROWS, LANES), jnp.float32)
 
+    def cells(part):
+        return (fields, depth, part[1], part[3])
+
+    scratch = [
+        vregs(tiles, fields, depth + 5),
+        vregs(tiles, fields, depth + 5),
+        vregs(tiles, fields, depth + 1),
+        vregs(tiles, depth + 1),
+    ]
+    inputs = [state, pair, far, mask_x, *accs]
+    places_in = [PLACE] * len(inputs)
+    if others is None:
+        inputs.append(after)
+        places_in.append(ANYWHERE)
+        places = None
+        target, target_shape = PLACE, shape_of(*cells(part))
+    else:
+        places = [place for place, _ in others]
+        inputs += [arrived] + [array for _, array in others]
+        places_in = [PLACE] * len(inputs)
+        target, target_shape = HBM, shape_of(*state.shape)
+        scratch += [
+            pltpu.VMEM(cells(part), jnp.float32),
+            pltpu.SemaphoreType.DMA((tiles,)),
+            pltpu.SemaphoreType.DMA((len(others),)),
+        ] + [pltpu.VMEM(cells(place), jnp.float32) for place in places]
     return call(
-        functools.partial(stream_kernel, part, segments, counts),
+        functools.partial(stream_kernel, part, places, counts),
         "stream_faces",
         0.6 * tiles,
-        [PLACE] * count + [HBM] * len(extra),
-        [HBM, PLACE],
-        [shape_of(*state.shape), shape_of(ROWS, LANES)],
-        [
-            vregs(tiles, fields, depth + 5),
-            vregs(tiles, fields, depth + 5),
-            vregs(tiles, fields, depth + 1),
-            vregs(tiles, depth + 1),
-            pltpu.VMEM((fields, depth, rows_y, width), jnp.float32),
-            pltpu.SemaphoreType.DMA((tiles,)),
-        ],
-        {count: 0} if extra else None,
-    )(state, pair, far, mask_x, *sums, *accs, *extra)
+        places_in,
+        target,
+        target_shape,
+        scratch,
+    )(*inputs)
 
 
 def circulant_tables(span):
@@ -551,35 +609,29 @@
     return dot(xh[...], high) + dot(xl[...], high) + dot(xh[...], w_s[deep:, :])
 
 
-def away_kernel(masks, parts, high_ref, low_ref, own_ref, core_ref, after_ref, *refs):
-    sums = refs[: len(masks) * parts]
-    xh, xl, w_s = refs[len(masks) * parts :]
-    fields, depth, rows_all, width = own_ref.shape
-    rows_y = rows_all // parts
+def away_kernel(masks, high_ref, low_ref, own_ref, core_ref, *refs):
+    sums = refs[: len(masks)]
+    xh, xl, w_s = refs[len(masks) :]
     me = lax.axis_index("gz")
     fill_lines([own_ref, core_ref], [xh, xl])
-    for number, mask in enumerate(masks):
+    for mask, sum_ref in zip(masks, sums):
         total = product(me ^ mask, [me, me ^ 1], high_ref, low_ref, xh, xl, w_s)
-        total = total.reshape(fields, depth, rows_all, width)
-        for c in range(parts):
-            sums[number * parts + c][...] = total[:, :, c * rows_y : (c + 1) * rows_y, :]
-
-
-def away_part(band, state, core, masks, parts, after):
+        sum_ref[...] = total.reshape(own_ref.shape)
+
+
+def away_part(band, state, core, masks):
     fields, depth, rows_all, width = state.shape
-    lines = fields * depth * rows_all
-    line = shape_of(lines, 2 * width, dtype=jnp.bfloat16)
-    count = len(masks) * parts
+    line = shape_of(fields * depth * rows_all, 2 * width, dtype=jnp.bfloat16)
     outs = call(
-        functools.partial(away_kernel, masks, parts),
+        functools.partial(away_kernel, masks),
         "span_away",
         3.0,
-        [PLACE] * 4 + [ANYWHERE],
-        [PLACE] * (count + 2),
-        [shape_of(fields, depth, rows_all // parts, width)] * count + [line, line],
+        [PLACE] * 4,
+        [PLACE] * (len(masks) + 2),
+        [shape_of(*state.shape)] * len(masks) + [line, line],
         [pltpu.VMEM((4 * width, width), jnp.bfloat16)],
-    )(*band, state, core, after)
-    return outs[:count], outs[count:]
+    )(*band, state, core)
+    return outs[: len(masks)], outs[len(masks) :]
 
 
 def home_kernel(high_ref, low_ref, xh, xl, state_ref, out_ref, w_s):
@@ -625,36 +677,39 @@
     else:
         part = rows_all // 4
         parts = [(0, 2 * part, 0, width), (2 * part, part, 0, width), (3 * part, part, 0, width)]
-    bricks = pack_part(state, mask_x, parts)
-    pairs = [lax.ppermute(brick, "gx", swap) for brick in bricks]
+    across = [(i, i + 1) for i in range(1, slabs - 1, 2)]
+    across += [(target, source) for source, target in across]
+
+    (brick,) = pack_part(state, mask_x, parts[:1])
+    pairs = [lax.ppermute(brick, "gx", swap)]
     band = circulant(span_filter, span, width, core)
 
     masks = list(range(2, groups, 2))
-    sums, lines = away_part(band, state, core, masks, SUM_PARTS, bricks[0])
-    arrived = [
-        sum(flip(sums[n * SUM_PARTS + c], mask) for n, mask in enumerate(masks))
-        for c in range(SUM_PARTS)
-    ]
+    sums, lines = away_part(band, state, core, masks)
+    arrived = sum(flip(part_sum, mask) for part_sum, mask in zip(sums, masks))
     half = depth // 2
-
-    def hand_on(c, after):
-        return lax.ppermute(pass_part(pairs[c], depth, after), "gx", carry)
-
-    def stream(c, out):
-        return stream_part(
-            state, pairs[c], fars[c], mask_x, parts[c], arrived, [acc_low, acc_high], out
-        )
-
+    (brick,) = bring_part(state, mask_x, parts[1], ["all"], lines[0])
+    pairs.append(lax.ppermute(brick, "gx", swap))
     base = home_part(band, lines, state)
-    fars = [hand_on(0, base)]
-    acc_low = wall_part(state, mask_y, base, 0, half, base)
-    acc_high = wall_part(state, mask_y, base, half, depth - half, acc_low)
-    fars.append(hand_on(1, acc_high))
-    out, token = stream(0, None)
-    fars.append(hand_on(2, token))
-    out, _ = stream(1, out)
-    out, _ = stream(2, out)
-    return out
+    inner, outer = bring_part(state, mask_x, parts[2], ["pair", "across"], base)
+    pairs.append(lax.ppermute(inner, "gx", swap))
+    last = lax.ppermute(outer, "gx", across)
+
+    planes = pass_part(pairs[0], depth, inner)
+    fars = [lax.ppermute(planes, "gx", carry)]
+    acc_low = wall_part(state, mask_y, base, 0, half, planes)
+    planes = pass_part(pairs[1], depth, acc_low)
+    fars += [lax.ppermute(planes, "gx", carry), last]
+    acc_high = wall_part(state, mask_y, base, half, depth - half, planes)
+
+    accs = [acc_low, acc_high]
+    ready, after = [], acc_high
+    for c in (0, 2):
+        after = stream_part(state, pairs[c], fars[c], mask_x, parts[c], accs, after)
+        ready.append((parts[c], after))
+    return stream_part(
+        state, pairs[1], fars[1], mask_x, parts[1], accs, arrived=arrived, others=ready
+    )
 
 
 def solution(mesh):

time: 50.1 us -> 50.2 us (level)
  waiting for transfers between devices: 4.83 us -> 10.5 us
  Pallas kernels: 25.3 us -> 22.9 us
  starting transfers between devices: 18.1 us -> 15.8 us
  local copies, waits for them, and re-layouts: 1.38 us -> 0.59 us
    ppermute x6, waiting for transfers between devices: 4.82 us -> 10.5 us  [the longest x1 8.53 us: per_device(): pairs.append(lax.ppermute(brick, 'gx', swap))]
    pallas_call x4 -> x6, Pallas kernels: 14 us -> 12.1 us  [the longest x3 8.57 us: stream_part(): call(functools.partial(stream_kernel, part, places, counts), 'stream_face...]
    ppermute x3 -> x2, starting transfers between devices: 3.62 us -> 1.97 us  [flip(): return lax.ppermute(array, 'gz', [(g, g ^ bit) for g in range(groups)])]
    unnamed x18 -> x12, local copies, waits for them, and re-layouts: 1.31 us -> 0.52 us
    ppermute x6, starting transfers between devices: 14.5 us -> 13.9 us  [the longest x1 4.5 us: per_device(): fars += [lax.ppermute(planes, 'gx', carry), last]]
  transfers between devices with their start and end apart: 9 -> 8, of which waited for: 3 -> 2; matrix products, arithmetic and copies ran while one was open for 0% -> 0% of each run, Pallas kernels for 45% -> 38%
where the time goes in v1:
time: 50.2 us; the launch traced here: 50 us
  Pallas kernels  22.9 us (46%)
  starting transfers between devices  15.8 us (31%)
  waiting for transfers between devices  10.5 us (21%)
  local copies, waits for them, and re-layouts  0.59 us (1%)
    pallas_call x3, Pallas kernels, stream_part(): call(functools.partial(stream_kernel, part, places, counts), 'stream_face...  8.57 us
    ppermute x1, waiting for transfers between devices, per_device(): pairs.append(lax.ppermute(brick, 'gx', swap))  8.53 us
    pallas_call x2, Pallas kernels, wall_part(): call(kernel, 'wall_faces', 5.0 * count / depth, [PLACE, PLACE, PLACE, ANY...  5.82 us
    ppermute x1, starting transfers between devices, per_device(): fars += [lax.ppermute(planes, 'gx', carry), last]  4.5 us
    ppermute x1, starting transfers between devices, per_device(): fars = [lax.ppermute(planes, 'gx', carry)]  3.96 us
    pallas_call x1, Pallas kernels, away_part(): call(functools.partial(away_kernel, masks), 'span_away', 3.0, [PLACE] * 4...  3.41 us
    ppermute x1, starting transfers between devices, per_device(): pairs = [lax.ppermute(brick, 'gx', swap)]  2.57 us
    pallas_call x1, Pallas kernels, home_part(): call(home_kernel, 'span_home', 2.0, [PLACE] * 5, PLACE, shape_of(*state.s...  2.19 us
  transfers between devices with their start and end apart: 8, of which 2 were waited for; matrix products, arithmetic and copies ran while one was open for 0% of the time, Pallas kernels for 38%

profile of v1, /device:TPU:0, one launch (start us, length us, event | category | flops | bytes accessed | tf_op | source)
XLA Modules:
  0.0 50.0 jit_solution(10822526524811889285)
XLA Ops:
  0.0 0.5 collective-permute-start
  0.5 0.0 copy-start.5
  0.5 0.0 copy-start.3
  0.5 0.0 copy-start.4
  0.5 1.9 %pack_bricks.1 = f32[21,16,384]{2,1,0:T(8,128)} custom-call(f32[20,32,512]{2,1,0:T(8,128)} %bitcast.1, s32[4,32,512]{2,1,0:T(8,128)} %refs_3_.5), custom_call_target="tpu_custom_call" | custom-call | flops 1000000000 | bytes 3000000 | tf_op jit(solution)/shard_map/pack_bricks/pallas_call | solution.py:229
  2.4 2.6 %collective-permute-start.2 = (f32[21,16,384]{2,1,0:T(8,128)}, f32[21,16,384]{2,1,0:T(8,128)S(1)}, u32[]{:S(2)}, u32[]{:S(2)}) collective-permute-start(f32[21,16,384]{2,1,0:T(8,128)} %pack_bricks.1), channel_id=1, source_target_pairs={{0,4},{4,0},{8,12},{12,8},{16,20},{20,16},{24,28},{28,24},{1,5},{5... | collective-permute-start | bytes 1548296 | tf_op jit(solution)/shard_map/ppermute | solution.py:684
  5.0 0.0 copy-done.5
  5.0 0.1 reshape.6.filter_ref
  5.0 0.0 copy-start
  5.0 0.0 collective-permute-done.after_ref.core_ref
  5.1 0.0 copy-done.3
  5.1 0.0 copy-done.4
  5.1 0.8 %circulant_band.1 = (bf16[256,2560]{1,0:T(8,128)(2,1)S(1)}, bf16[256,2560]{1,0:T(8,128)(2,1)S(1)}) custom-call(f32[32,32]{1,0:T(8,128)S(1)} %reshape.6.filter_ref, f32[64,128]{1,0:T(8,128)S(1)} %copy-done.4, f32[64,2048]{1,0:T(8,128)S(1)} %copy-done.3, f32[5,4,32,512]{3,2,1,0:T(8,128)S(1)} %collective-permute-done.after_ref.core_ref), custom_call_target="tpu_custom_call" | custom-call | flops 1000000000 | bytes 3000000 | tf_op jit(solution)/shard_map/circulant_band/pallas_call | solution.py:564
  5.9 0.5 copy-done
  6.4 0.0 copy-start.1
  6.4 3.4 %span_away.1 = (f32[5,4,32,512]{3,2,1,0:T(8,128)S(1)}, bf16[640,1024]{1,0:T(8,128)(2,1)S(1)}, bf16[640,1024]{1,0:T(8,128)(2,1)S(1)}) custom-call(bf16[256,2560]{1,0:T(8,128)(2,1)S(1)} %get-tuple-element.12.high_ref, bf16[256,2560]{1,0:T(8,128)(2,1)S(1)} %get-tuple-element.13.low_ref, f32[5,4,32,512]{3,2,1,0:T(8,128)S(1)} %copy-done, ...), custom_call_target="tpu_custom_call" | custom-call | flops 3000000000 | bytes 9000000 | tf_op jit(solution)/shard_map/span_away/pallas_call | solution.py:625
  9.8 0.0 copy-done.1
  9.8 0.7 %collective-permute-start.1 = (f32[21,16,384]{2,1,0:T(8,128)S(1)}, f32[21,16,384]{2,1,0:T(8,128)S(1)}, u32[]{:S(2)}, u32[]{:S(2)}) collective-permute-start(f32[21,16,384]{2,1,0:T(8,128)S(1)} %bring_planes.2), channel_id=1, source_target_pairs={{0,4},{4,0},{8,12},{12,8},{16,20},{20,16},{24,28},{28,24},{1,5},{5... | collective-permute-start | bytes 1548296 | tf_op jit(solution)/shard_map/ppermute | solution.py:692
  10.6 1.5 %collective-permute-start.4 = (f32[5,4,32,512]{3,2,1,0:T(8,128)S(1)}, f32[5,4,32,512]{3,2,1,0:T(8,128)S(1)}, u32[]{:S(2)}, u32[]{:S(2)}) collective-permute-start(f32[5,4,32,512]{3,2,1,0:T(8,128)S(1)} %get-tuple-element.17), channel_id=1, source_target_pairs={{0,2},{1,3},{2,0},{3,1},{4,6},{5,7},{6,4},{7,5},{8,10},{9,11},{10,... | collective-permute-start | bytes 3932168 | tf_op jit(solution)/shard_map/ppermute | solution.py:663
  12.1 2.2 %span_home.1.after_ref.base_ref = f32[5,4,32,512]{3,2,1,0:T(8,128)S(1)} custom-call(bf16[256,2560]{1,0:T(8,128)(2,1)S(1)} %get-tuple-element.12.high_ref, bf16[256,2560]{1,0:T(8,128)(2,1)S(1)} %get-tuple-element.13.low_ref, bf16[640,1024]{1,0:T(8,128)(2,1)S(1)} %get-tuple-element.14.after_ref.xh, bf16[640,1024]{1,0:T(8,128)(2,1)S(1)} %get-tuple-element.15.xl, ...), custom_call_target="tpu_custom_call" | custom-call | flops 2000000000 | bytes 6000000 | tf_op jit(solution)/shard_map/span_home/pallas_call | solution.py:645
  14.3 0.1 bring_planes.3
  14.4 0.0 copy-start.2
  14.4 1.4 %collective-permute-start.6 = (f32[16,32,128]{2,1,0:T(8,128)S(1)}, f32[16,32,128]{2,1,0:T(8,128)S(1)}, u32[]{:S(2)}, u32[]{:S(2)}) collective-permute-start(f32[16,32,128]{2,1,0:T(8,128)S(1)} %get-tuple-element.16.after_ref), channel_id=1, source_target_pairs={{0,4},{4,0},{8,12},{12,8},{16,20},{20,16},{24,28},{28,24},{1,5},{5... | collective-permute-start | bytes 786440 | tf_op jit(solution)/shard_map/ppermute | solution.py:695
  15.8 2.0 %collective-permute-done.2.pair_ref.refs_1_ = f32[21,16,384]{2,1,0:T(8,128)S(1)} collective-permute-done((f32[21,16,384]{2,1,0:T(8,128)}, f32[21,16,384]{2,1,0:T(8,128)S(1)}, u32[]{:S(2)}, u32[]{:S(2)}) %collective-permute-start.2) | collective-permute-done | bytes 516128 | tf_op jit(solution)/shard_map/ppermute | solution.py:684
  17.8 4.0 %collective-permute-start.5 = (f32[16,16,384]{2,1,0:T(8,128)S(1)}, f32[16,16,384]{2,1,0:T(8,128)S(1)}, u32[]{:S(2)}, u32[]{:S(2)}) collective-permute-start(f32[16,16,384]{2,1,0:T(8,128)S(1)} %pass_planes.2.after_ref), channel_id=1, source_target_pairs={{0,8},{8,16},{16,24},{12,4},{20,12},{28,20},{1,9},{9,17},{17,25},{... | collective-permute-start | bytes 1179656 | tf_op jit(solution)/shard_map/ppermute | solution.py:699
  21.8 0.0 copy-done.2
  21.8 2.9 %wall_faces.2.after_ref.refs_4_ = f32[5,2,32,512]{3,2,1,0:T(8,128)S(1)} custom-call(f32[5,4,32,512]{3,2,1,0:T(8,128)S(1)} %copy-done, s32[4,32,512]{2,1,0:T(8,128)S(1)} %copy-done.2, f32[5,4,32,512]{3,2,1,0:T(8,128)S(1)} %span_home.1.after_ref.base_ref, f32[16,16,384]{2,1,0:T(8,128)S(1)} %pass_planes.2.after_ref), custom_call_target="tpu_custom_call" | custom-call | flops 2500000000 | bytes 7500000 | tf_op jit(solution)/shard_map/wall_faces/pallas_call | solution.py:192
  24.7 0.7 %collective-permute-start.7 = (f32[16,32,128]{2,1,0:T(8,128)S(1)}, f32[16,32,128]{2,1,0:T(8,128)S(1)}, u32[]{:S(2)}, u32[]{:S(2)}) collective-permute-start(f32[16,32,128]{2,1,0:T(8,128)S(1)} %get-tuple-element.18), channel_id=1, source_target_pairs={{4,8},{12,16},{20,24},{8,4},{16,12},{24,20},{5,9},{13,17},{21,25},... | collective-permute-start | bytes 786440 | tf_op jit(solution)/shard_map/ppermute | solution.py:696
  25.4 8.5 %collective-permute-done.1.pair_ref.refs_1_ = f32[21,16,384]{2,1,0:T(8,128)S(1)} collective-permute-done((f32[21,16,384]{2,1,0:T(8,128)S(1)}, f32[21,16,384]{2,1,0:T(8,128)S(1)}, u32[]{:S(2)}, u32[]{:S(2)}) %collective-permute-start.1) | collective-permute-done | bytes 516128 | tf_op jit(solution)/shard_map/ppermute | solution.py:692
  34.0 4.5 %collective-permute-start.3 = (f32[16,16,384]{2,1,0:T(8,128)S(1)}, f32[16,16,384]{2,1,0:T(8,128)S(1)}, u32[]{:S(2)}, u32[]{:S(2)}) collective-permute-start(f32[16,16,384]{2,1,0:T(8,128)S(1)} %pass_planes.3.after_ref), channel_id=1, source_target_pairs={{0,8},{8,16},{16,24},{12,4},{20,12},{28,20},{1,9},{9,17},{17,25},{... | collective-permute-start | bytes 1179656 | tf_op jit(solution)/shard_map/ppermute | solution.py:702
  38.5 2.9 %wall_faces.3.refs_5_.refs_6_ = f32[5,2,32,512]{3,2,1,0:T(8,128)S(1)} custom-call(f32[5,4,32,512]{3,2,1,0:T(8,128)S(1)} %copy-done, s32[4,32,512]{2,1,0:T(8,128)S(1)} %copy-done.2, f32[5,4,32,512]{3,2,1,0:T(8,128)S(1)} %span_home.1.after_ref.base_ref, f32[16,16,384]{2,1,0:T(8,128)S(1)} %pass_planes.3.after_ref), custom_call_target="tpu_custom_call" | custom-call | flops 2500000000 | bytes 7500000 | tf_op jit(solution)/shard_map/wall_faces/pallas_call | solution.py:192
  41.4 0.0 collective-permute-done.5.refs_2_
  41.4 2.7 %stream_faces.3.refs_6_.refs_7_ = f32[5,4,16,384]{3,2,1,0:T(8,128)S(1)} custom-call(f32[5,4,32,512]{3,2,1,0:T(8,128)S(1)} %copy-done, f32[21,16,384]{2,1,0:T(8,128)S(1)} %collective-permute-done.2.pair_ref.refs_1_, f32[16,16,384]{2,1,0:T(8,128)S(1)} %collective-permute-done.5.refs_2_, s32[4,32,512]{2,1,0:T(8,128)S(1)} %copy-done.1, ...), custom_call_target="tpu_custom_call" | custom-call | flops 3600000000 | bytes 10799999 | tf_op jit(solution)/shard_map/stream_faces/pallas_call | solution.py:487
  44.1 0.0 collective-permute-done.6.refs_1_
  44.1 0.0 collective-permute-done.7.refs_2_
  44.1 1.8 %stream_faces.4.refs_8_ = f32[5,4,32,128]{3,2,1,0:T(8,128)S(1)} custom-call(f32[5,4,32,512]{3,2,1,0:T(8,128)S(1)} %copy-done, f32[16,32,128]{2,1,0:T(8,128)S(1)} %collective-permute-done.6.refs_1_, f32[16,32,128]{2,1,0:T(8,128)S(1)} %collective-permute-done.7.refs_2_, s32[4,32,512]{2,1,0:T(8,128)S(1)} %copy-done.1, ...), custom_call_target="tpu_custom_call" | custom-call | flops 2400000000 | bytes 7200000 | tf_op jit(solution)/shard_map/stream_faces/pallas_call | solution.py:487
  45.9 0.0 collective-permute-done.3.refs_2_
  45.9 0.0 collective-permute-done.4.refs_6_
  46.0 4.0 %stream_faces.5 = f32[5,4,32,512]{3,2,1,0:T(8,128)} custom-call(f32[5,4,32,512]{3,2,1,0:T(8,128)S(1)} %copy-done, f32[21,16,384]{2,1,0:T(8,128)S(1)} %collective-permute-done.1.pair_ref.refs_1_, f32[16,16,384]{2,1,0:T(8,128)S(1)} %collective-permute-done.3.refs_2_, s32[4,32,512]{2,1,0:T(8,128)S(1)} %copy-done.1, ...), custom_call_target="tpu_custom_call" | custom-call | flops 3600000000 | bytes 10799999 | tf_op jit(solution)/shard_map/stream_faces/pallas_call | solution.py:487
  (3 shorter events, 0.1 us)
Async XLA Ops:
  0.0 5.0 %collective-permute-start = (f32[5,4,32,512]{3,2,1,0:T(8,128)}, f32[5,4,32,512]{3,2,1,0:T(8,128)S(1)}, u32[]{:S(2)}, u32[]{:S(2)}) collective-permute-start(f32[5,4,32,512]{3,2,1,0:T(8,128)} %refs_0_.5), channel_id=1, source_target_pairs={{0,1},{1,0},{2,3},{3,2},{4,5},{5,4},{6,7},{7,6},{8,9},{9,8},{10,11... | collective-permute-start | bytes 3932168 | tf_op jit(solution)/shard_map/ppermute | solution.py:663
  0.5 4.5 %copy-start.5 = (f32[1024]{0:T(1024)S(1)}, f32[1024]{0:T(1024)}, u32[]{:S(2)}) copy-start(f32[1024]{0:T(1024)} %param.9) | copy-start | bytes 12292
  0.5 4.6 %copy-start.3 = (f32[64,2048]{1,0:T(8,128)S(1)}, f32[64,2048]{1,0:T(8,128)}, u32[]{:S(2)}) copy-start(f32[64,2048]{1,0:T(8,128)} %constant.5.clone.outer_ref) | copy-start | bytes 1572868
  0.5 4.6 %copy-start.4 = (f32[64,128]{1,0:T(8,128)S(1)}, f32[64,128]{1,0:T(8,128)}, u32[]{:S(2)}) copy-start(f32[64,128]{1,0:T(8,128)} %constant.4.clone.inner_ref) | copy-start | bytes 98308
  2.4 15.4 %collective-permute-start.2 = (f32[21,16,384]{2,1,0:T(8,128)}, f32[21,16,384]{2,1,0:T(8,128)S(1)}, u32[]{:S(2)}, u32[]{:S(2)}) collective-permute-start(f32[21,16,384]{2,1,0:T(8,128)} %pack_bricks.1), channel_id=1, source_target_pairs={{0,4},{4,0},{8,12},{12,8},{16,20},{20,16},{24,28},{28,24},{1,5},{5... | collective-permute-start | bytes 1548296 | tf_op jit(solution)/shard_map/ppermute | solution.py:684
  5.0 1.3 %copy-start = (f32[5,4,32,512]{3,2,1,0:T(8,128)S(1)}, f32[5,4,32,512]{3,2,1,0:T(8,128)}, u32[]{:S(2)}) copy-start(f32[5,4,32,512]{3,2,1,0:T(8,128)} %refs_0_.5) | copy-start | bytes 3932164
  6.4 3.4 %copy-start.1 = (s32[4,32,512]{2,1,0:T(8,128)S(1)}, s32[4,32,512]{2,1,0:T(8,128)}, u32[]{:S(2)}) copy-start(s32[4,32,512]{2,1,0:T(8,128)} %refs_3_.5) | copy-start | bytes 786436
  9.8 24.1 %collective-permute-start.1 = (f32[21,16,384]{2,1,0:T(8,128)S(1)}, f32[21,16,384]{2,1,0:T(8,128)S(1)}, u32[]{:S(2)}, u32[]{:S(2)}) collective-permute-start(f32[21,16,384]{2,1,0:T(8,128)S(1)} %bring_planes.2), channel_id=1, source_target_pairs={{0,4},{4,0},{8,12},{12,8},{16,20},{20,16},{24,28},{28,24},{1,5},{5... | collective-permute-start | bytes 1548296 | tf_op jit(solution)/shard_map/ppermute | solution.py:692
  10.6 35.4 %collective-permute-start.4 = (f32[5,4,32,512]{3,2,1,0:T(8,128)S(1)}, f32[5,4,32,512]{3,2,1,0:T(8,128)S(1)}, u32[]{:S(2)}, u32[]{:S(2)}) collective-permute-start(f32[5,4,32,512]{3,2,1,0:T(8,128)S(1)} %get-tuple-element.17), channel_id=1, source_target_pairs={{0,2},{1,3},{2,0},{3,1},{4,6},{5,7},{6,4},{7,5},{8,10},{9,11},{10,... | collective-permute-start | bytes 3932168 | tf_op jit(solution)/shard_map/ppermute | solution.py:663
  14.4 7.4 %copy-start.2 = (s32[4,32,512]{2,1,0:T(8,128)S(1)}, s32[4,32,512]{2,1,0:T(8,128)}, u32[]{:S(2)}) copy-start(s32[4,32,512]{2,1,0:T(8,128)} %mask_ref.9) | copy-start | bytes 786436
  14.4 29.7 %collective-permute-start.6 = (f32[16,32,128]{2,1,0:T(8,128)S(1)}, f32[16,32,128]{2,1,0:T(8,128)S(1)}, u32[]{:S(2)}, u32[]{:S(2)}) collective-permute-start(f32[16,32,128]{2,1,0:T(8,128)S(1)} %get-tuple-element.16.after_ref), channel_id=1, source_target_pairs={{0,4},{4,0},{8,12},{12,8},{16,20},{20,16},{24,28},{28,24},{1,5},{5... | collective-permute-start | bytes 786440 | tf_op jit(solution)/shard_map/ppermute | solution.py:695
  17.8 23.6 %collective-permute-start.5 = (f32[16,16,384]{2,1,0:T(8,128)S(1)}, f32[16,16,384]{2,1,0:T(8,128)S(1)}, u32[]{:S(2)}, u32[]{:S(2)}) collective-permute-start(f32[16,16,384]{2,1,0:T(8,128)S(1)} %pass_planes.2.after_ref), channel_id=1, source_target_pairs={{0,8},{8,16},{16,24},{12,4},{20,12},{28,20},{1,9},{9,17},{17,25},{... | collective-permute-start | bytes 1179656 | tf_op jit(solution)/shard_map/ppermute | solution.py:699
  24.7 19.4 %collective-permute-start.7 = (f32[16,32,128]{2,1,0:T(8,128)S(1)}, f32[16,32,128]{2,1,0:T(8,128)S(1)}, u32[]{:S(2)}, u32[]{:S(2)}) collective-permute-start(f32[16,32,128]{2,1,0:T(8,128)S(1)} %get-tuple-element.18), channel_id=1, source_target_pairs={{4,8},{12,16},{20,24},{8,4},{16,12},{24,20},{5,9},{13,17},{21,25},... | collective-permute-start | bytes 786440 | tf_op jit(solution)/shard_map/ppermute | solution.py:696
  34.0 12.0 %collective-permute-start.3 = (f32[16,16,384]{2,1,0:T(8,128)S(1)}, f32[16,16,384]{2,1,0:T(8,128)S(1)}, u32[]{:S(2)}, u32[]{:S(2)}) collective-permute-start(f32[16,16,384]{2,1,0:T(8,128)S(1)} %pass_planes.3.after_ref), channel_id=1, source_target_pairs={{0,8},{8,16},{16,24},{12,4},{20,12},{28,20},{1,9},{9,17},{17,25},{... | collective-permute-start | bytes 1179656 | tf_op jit(solution)/shard_map/ppermute | solution.py:702

commit v2 on v1

--- a/solution.py
+++ b/solution.py
@@ -691,15 +691,15 @@
     (brick,) = bring_part(state, mask_x, parts[1], ["all"], lines[0])
     pairs.append(lax.ppermute(brick, "gx", swap))
     base = home_part(band, lines, state)
-    inner, outer = bring_part(state, mask_x, parts[2], ["pair", "across"], base)
-    pairs.append(lax.ppermute(inner, "gx", swap))
-    last = lax.ppermute(outer, "gx", across)
-
-    planes = pass_part(pairs[0], depth, inner)
+    planes = pass_part(pairs[0], depth, base)
     fars = [lax.ppermute(planes, "gx", carry)]
     acc_low = wall_part(state, mask_y, base, 0, half, planes)
-    planes = pass_part(pairs[1], depth, acc_low)
+    (outer,) = bring_part(state, mask_x, parts[2], ["across"], acc_low)
+    last = lax.ppermute(outer, "gx", across)
+    planes = pass_part(pairs[1], depth, outer)
     fars += [lax.ppermute(planes, "gx", carry), last]
+    (inner,) = bring_part(state, mask_x, parts[2], ["pair"], planes)
+    pairs.append(lax.ppermute(inner, "gx", swap))
     acc_high = wall_part(state, mask_y, base, half, depth - half, planes)
 
     accs = [acc_low, acc_high]

time: 50.2 us -> 50.4 us (level); the launches traced: 50 us -> 49.5 us
  starting transfers between devices: 15.8 us -> 13.8 us
  waiting for transfers between devices: 10.5 us -> 12.1 us
    ppermute x1, waiting for transfers between devices: 1.96 us -> 3.47 us  [per_device(): pairs = [lax.ppermute(brick, 'gx', swap)]]
    ppermute x1, starting transfers between devices: 1.42 us -> 0.33 us  [per_device(): pairs.append(lax.ppermute(inner, 'gx', swap))]
    ppermute x1, starting transfers between devices: 4.5 us -> 3.5 us  [per_device(): fars += [lax.ppermute(planes, 'gx', carry), last]]
    ppermute x1, waiting for transfers between devices: 0.01 us -> 0.51 us  [per_device(): pairs.append(lax.ppermute(inner, 'gx', swap))]
  transfers between devices with their start and end apart: 8 -> 8, of which waited for: 2 -> 3; matrix products, arithmetic and copies ran while one was open for 0% -> 0% of each run, Pallas kernels for 38% -> 38%
where the time goes in v2:
time: 50.4 us; the launch traced here: 49.5 us
  Pallas kernels  22.9 us (45%)
  starting transfers between devices  13.8 us (27%)
  waiting for transfers between devices  12.1 us (24%)
  local copies, waits for them, and re-layouts  0.59 us (1%)
    pallas_call x3, Pallas kernels, stream_part(): call(functools.partial(stream_kernel, part, places, counts), 'stream_face...  8.54 us
    ppermute x1, waiting for transfers between devices, per_device(): pairs.append(lax.ppermute(brick, 'gx', swap))  8.08 us
    pallas_call x2, Pallas kernels, wall_part(): call(kernel, 'wall_faces', 5.0 * count / depth, [PLACE, PLACE, PLACE, ANY...  5.82 us
    ppermute x1, starting transfers between devices, per_device(): fars = [lax.ppermute(planes, 'gx', carry)]  3.96 us
    ppermute x1, starting transfers between devices, per_device(): fars += [lax.ppermute(planes, 'gx', carry), last]  3.5 us
    ppermute x1, waiting for transfers between devices, per_device(): pairs = [lax.ppermute(brick, 'gx', swap)]  3.47 us
    pallas_call x1, Pallas kernels, away_part(): call(functools.partial(away_kernel, masks), 'span_away', 3.0, [PLACE] * 4...  3.41 us
    ppermute x1, starting transfers between devices, per_device(): pairs = [lax.ppermute(brick, 'gx', swap)]  2.57 us
  transfers between devices with their start and end apart: 8, of which 3 were waited for; matrix products, arithmetic and copies ran while one was open for 0% of the time, Pallas kernels for 38%

profile of v2, /device:TPU:0, one launch (start us, length us, event | category | flops | bytes accessed | tf_op | source)
XLA Modules:
  0.0 49.5 jit_solution(10746455233494252335)
XLA Ops:
  0.0 0.5 collective-permute-start
  0.5 0.0 copy-start.5
  0.5 0.0 copy-start.3
  0.5 0.0 copy-start.4
  0.5 1.9 %pack_bricks.1 = f32[21,16,384]{2,1,0:T(8,128)} custom-call(f32[20,32,512]{2,1,0:T(8,128)} %bitcast.1, s32[4,32,512]{2,1,0:T(8,128)} %refs_3_.5), custom_call_target="tpu_custom_call" | custom-call | flops 1000000000 | bytes 3000000 | tf_op jit(solution)/shard_map/pack_bricks/pallas_call | solution.py:229
  2.4 2.6 %collective-permute-start.2 = (f32[21,16,384]{2,1,0:T(8,128)}, f32[21,16,384]{2,1,0:T(8,128)S(1)}, u32[]{:S(2)}, u32[]{:S(2)}) collective-permute-start(f32[21,16,384]{2,1,0:T(8,128)} %pack_bricks.1), channel_id=1, source_target_pairs={{0,4},{4,0},{8,12},{12,8},{16,20},{20,16},{24,28},{28,24},{1,5},{5... | collective-permute-start | bytes 1548296 | tf_op jit(solution)/shard_map/ppermute | solution.py:684
  5.0 0.0 copy-done.5
  5.0 0.1 reshape.6.filter_ref
  5.0 0.0 copy-start
  5.0 0.0 collective-permute-done.after_ref.core_ref
  5.1 0.0 copy-done.3
  5.1 0.0 copy-done.4
  5.1 0.8 %circulant_band.1 = (bf16[256,2560]{1,0:T(8,128)(2,1)S(1)}, bf16[256,2560]{1,0:T(8,128)(2,1)S(1)}) custom-call(f32[32,32]{1,0:T(8,128)S(1)} %reshape.6.filter_ref, f32[64,128]{1,0:T(8,128)S(1)} %copy-done.4, f32[64,2048]{1,0:T(8,128)S(1)} %copy-done.3, f32[5,4,32,512]{3,2,1,0:T(8,128)S(1)} %collective-permute-done.after_ref.core_ref), custom_call_target="tpu_custom_call" | custom-call | flops 1000000000 | bytes 3000000 | tf_op jit(solution)/shard_map/circulant_band/pallas_call | solution.py:564
  5.9 0.5 %copy-done = f32[5,4,32,512]{3,2,1,0:T(8,128)S(1)} copy-done((f32[5,4,32,512]{3,2,1,0:T(8,128)S(1)}, f32[5,4,32,512]{3,2,1,0:T(8,128)}, u32[]{:S(2)}) %copy-start) | copy-done | bytes 1310744
  6.4 0.0 copy-start.1
  6.4 3.4 %span_away.1 = (f32[5,4,32,512]{3,2,1,0:T(8,128)S(1)}, bf16[640,1024]{1,0:T(8,128)(2,1)S(1)}, bf16[640,1024]{1,0:T(8,128)(2,1)S(1)}) custom-call(bf16[256,2560]{1,0:T(8,128)(2,1)S(1)} %get-tuple-element.10.high_ref, bf16[256,2560]{1,0:T(8,128)(2,1)S(1)} %get-tuple-element.11.low_ref, f32[5,4,32,512]{3,2,1,0:T(8,128)S(1)} %copy-done, ...), custom_call_target="tpu_custom_call" | custom-call | flops 3000000000 | bytes 9000000 | tf_op jit(solution)/shard_map/span_away/pallas_call | solution.py:625
  9.8 0.0 copy-done.1
  9.8 0.7 %collective-permute-start.1 = (f32[21,16,384]{2,1,0:T(8,128)S(1)}, f32[21,16,384]{2,1,0:T(8,128)S(1)}, u32[]{:S(2)}, u32[]{:S(2)}) collective-permute-start(f32[21,16,384]{2,1,0:T(8,128)S(1)} %bring_planes.3), channel_id=1, source_target_pairs={{0,4},{4,0},{8,12},{12,8},{16,20},{20,16},{24,28},{28,24},{1,5},{5... | collective-permute-start | bytes 1548296 | tf_op jit(solution)/shard_map/ppermute | solution.py:692
  10.6 1.5 %collective-permute-start.4 = (f32[5,4,32,512]{3,2,1,0:T(8,128)S(1)}, f32[5,4,32,512]{3,2,1,0:T(8,128)S(1)}, u32[]{:S(2)}, u32[]{:S(2)}) collective-permute-start(f32[5,4,32,512]{3,2,1,0:T(8,128)S(1)} %get-tuple-element.14), channel_id=1, source_target_pairs={{0,2},{1,3},{2,0},{3,1},{4,6},{5,7},{6,4},{7,5},{8,10},{9,11},{10,... | collective-permute-start | bytes 3932168 | tf_op jit(solution)/shard_map/ppermute | solution.py:663
  12.1 2.2 %span_home.1.after_ref.base_ref = f32[5,4,32,512]{3,2,1,0:T(8,128)S(1)} custom-call(bf16[256,2560]{1,0:T(8,128)(2,1)S(1)} %get-tuple-element.10.high_ref, bf16[256,2560]{1,0:T(8,128)(2,1)S(1)} %get-tuple-element.11.low_ref, bf16[640,1024]{1,0:T(8,128)(2,1)S(1)} %get-tuple-element.12.after_ref.xh, bf16[640,1024]{1,0:T(8,128)(2,1)S(1)} %get-tuple-element.13.xl, ...), custom_call_target="tpu_custom_call" | custom-call | flops 2000000000 | bytes 6000000 | tf_op jit(solution)/shard_map/span_home/pallas_call | solution.py:645
  14.3 0.0 copy-start.2
  14.3 3.5 %collective-permute-done.2.pair_ref.refs_1_ = f32[21,16,384]{2,1,0:T(8,128)S(1)} collective-permute-done((f32[21,16,384]{2,1,0:T(8,128)}, f32[21,16,384]{2,1,0:T(8,128)S(1)}, u32[]{:S(2)}, u32[]{:S(2)}) %collective-permute-start.2) | collective-permute-done | bytes 516128 | tf_op jit(solution)/shard_map/ppermute | solution.py:684
  17.8 4.0 %collective-permute-start.5 = (f32[16,16,384]{2,1,0:T(8,128)S(1)}, f32[16,16,384]{2,1,0:T(8,128)S(1)}, u32[]{:S(2)}, u32[]{:S(2)}) collective-permute-start(f32[16,16,384]{2,1,0:T(8,128)S(1)} %pass_planes.2.after_ref), channel_id=1, source_target_pairs={{0,8},{8,16},{16,24},{12,4},{20,12},{28,20},{1,9},{9,17},{17,25},{... | collective-permute-start | bytes 1179656 | tf_op jit(solution)/shard_map/ppermute | solution.py:695
  21.8 0.0 copy-done.2
  21.8 2.9 %wall_faces.2.after_ref.refs_4_ = f32[5,2,32,512]{3,2,1,0:T(8,128)S(1)} custom-call(f32[5,4,32,512]{3,2,1,0:T(8,128)S(1)} %copy-done, s32[4,32,512]{2,1,0:T(8,128)S(1)} %copy-done.2, f32[5,4,32,512]{3,2,1,0:T(8,128)S(1)} %span_home.1.after_ref.base_ref, f32[16,16,384]{2,1,0:T(8,128)S(1)} %pass_planes.2.after_ref), custom_call_target="tpu_custom_call" | custom-call | flops 2500000000 | bytes 7500000 | tf_op jit(solution)/shard_map/wall_faces/pallas_call | solution.py:192
  24.8 0.7 %collective-permute-start.7 = (f32[16,32,128]{2,1,0:T(8,128)S(1)}, f32[16,32,128]{2,1,0:T(8,128)S(1)}, u32[]{:S(2)}, u32[]{:S(2)}) collective-permute-start(f32[16,32,128]{2,1,0:T(8,128)S(1)} %bring_planes.4.after_ref), channel_id=1, source_target_pairs={{4,8},{12,16},{20,24},{8,4},{16,12},{24,20},{5,9},{13,17},{21,25},... | collective-permute-start | bytes 786440 | tf_op jit(solution)/shard_map/ppermute | solution.py:698
  25.4 8.1 %collective-permute-done.1.pair_ref.refs_1_ = f32[21,16,384]{2,1,0:T(8,128)S(1)} collective-permute-done((f32[21,16,384]{2,1,0:T(8,128)S(1)}, f32[21,16,384]{2,1,0:T(8,128)S(1)}, u32[]{:S(2)}, u32[]{:S(2)}) %collective-permute-start.1) | collective-permute-done | bytes 516128 | tf_op jit(solution)/shard_map/ppermute | solution.py:692
  33.5 3.5 %collective-permute-start.3 = (f32[16,16,384]{2,1,0:T(8,128)S(1)}, f32[16,16,384]{2,1,0:T(8,128)S(1)}, u32[]{:S(2)}, u32[]{:S(2)}) collective-permute-start(f32[16,16,384]{2,1,0:T(8,128)S(1)} %pass_planes.3.after_ref), channel_id=1, source_target_pairs={{0,8},{8,16},{16,24},{12,4},{20,12},{28,20},{1,9},{9,17},{17,25},{... | collective-permute-start | bytes 1179656 | tf_op jit(solution)/shard_map/ppermute | solution.py:700
  37.1 0.3 collective-permute-start.6
  37.5 2.9 %wall_faces.3.refs_5_.refs_6_ = f32[5,2,32,512]{3,2,1,0:T(8,128)S(1)} custom-call(f32[5,4,32,512]{3,2,1,0:T(8,128)S(1)} %copy-done, s32[4,32,512]{2,1,0:T(8,128)S(1)} %copy-done.2, f32[5,4,32,512]{3,2,1,0:T(8,128)S(1)} %span_home.1.after_ref.base_ref, f32[16,16,384]{2,1,0:T(8,128)S(1)} %pass_planes.3.after_ref), custom_call_target="tpu_custom_call" | custom-call | flops 2500000000 | bytes 7500000 | tf_op jit(solution)/shard_map/wall_faces/pallas_call | solution.py:192
  40.4 0.0 collective-permute-done.5.refs_2_
  40.4 2.7 %stream_faces.3.refs_6_.refs_7_ = f32[5,4,16,384]{3,2,1,0:T(8,128)S(1)} custom-call(f32[5,4,32,512]{3,2,1,0:T(8,128)S(1)} %copy-done, f32[21,16,384]{2,1,0:T(8,128)S(1)} %collective-permute-done.2.pair_ref.refs_1_, f32[16,16,384]{2,1,0:T(8,128)S(1)} %collective-permute-done.5.refs_2_, s32[4,32,512]{2,1,0:T(8,128)S(1)} %copy-done.1, ...), custom_call_target="tpu_custom_call" | custom-call | flops 3600000000 | bytes 10799999 | tf_op jit(solution)/shard_map/stream_faces/pallas_call | solution.py:487
  43.1 0.0 collective-permute-done.7.refs_2_
  43.1 0.5 %collective-permute-done.6.refs_1_ = f32[16,32,128]{2,1,0:T(8,128)S(1)} collective-permute-done((f32[16,32,128]{2,1,0:T(8,128)S(1)}, f32[16,32,128]{2,1,0:T(8,128)S(1)}, u32[]{:S(2)}, u32[]{:S(2)}) %collective-permute-start.6) | collective-permute-done | bytes 262176 | tf_op jit(solution)/shard_map/ppermute | solution.py:702
  43.6 1.8 %stream_faces.4.refs_8_ = f32[5,4,32,128]{3,2,1,0:T(8,128)S(1)} custom-call(f32[5,4,32,512]{3,2,1,0:T(8,128)S(1)} %copy-done, f32[16,32,128]{2,1,0:T(8,128)S(1)} %collective-permute-done.6.refs_1_, f32[16,32,128]{2,1,0:T(8,128)S(1)} %collective-permute-done.7.refs_2_, s32[4,32,512]{2,1,0:T(8,128)S(1)} %copy-done.1, ...), custom_call_target="tpu_custom_call" | custom-call | flops 2400000000 | bytes 7200000 | tf_op jit(solution)/shard_map/stream_faces/pallas_call | solution.py:487
  45.4 0.0 collective-permute-done.3.refs_2_
  45.4 0.0 collective-permute-done.4.refs_6_
  45.4 4.0 %stream_faces.5 = f32[5,4,32,512]{3,2,1,0:T(8,128)} custom-call(f32[5,4,32,512]{3,2,1,0:T(8,128)S(1)} %copy-done, f32[21,16,384]{2,1,0:T(8,128)S(1)} %collective-permute-done.1.pair_ref.refs_1_, f32[16,16,384]{2,1,0:T(8,128)S(1)} %collective-permute-done.3.refs_2_, s32[4,32,512]{2,1,0:T(8,128)S(1)} %copy-done.1, ...), custom_call_target="tpu_custom_call" | custom-call | flops 3600000000 | bytes 10799999 | tf_op jit(solution)/shard_map/stream_faces/pallas_call | solution.py:487
  (5 shorter events, 0.2 us)
Async XLA Ops:
  0.0 5.0 %collective-permute-start = (f32[5,4,32,512]{3,2,1,0:T(8,128)}, f32[5,4,32,512]{3,2,1,0:T(8,128)S(1)}, u32[]{:S(2)}, u32[]{:S(2)}) collective-permute-start(f32[5,4,32,512]{3,2,1,0:T(8,128)} %refs_0_.5), channel_id=1, source_target_pairs={{0,1},{1,0},{2,3},{3,2},{4,5},{5,4},{6,7},{7,6},{8,9},{9,8},{10,11... | collective-permute-start | bytes 3932168 | tf_op jit(solution)/shard_map/ppermute | solution.py:663
  0.5 4.5 %copy-start.5 = (f32[1024]{0:T(1024)S(1)}, f32[1024]{0:T(1024)}, u32[]{:S(2)}) copy-start(f32[1024]{0:T(1024)} %param.9) | copy-start | bytes 12292
  0.5 4.6 %copy-start.3 = (f32[64,2048]{1,0:T(8,128)S(1)}, f32[64,2048]{1,0:T(8,128)}, u32[]{:S(2)}) copy-start(f32[64,2048]{1,0:T(8,128)} %constant.5.clone.outer_ref) | copy-start | bytes 1572868
  0.5 4.6 %copy-start.4 = (f32[64,128]{1,0:T(8,128)S(1)}, f32[64,128]{1,0:T(8,128)}, u32[]{:S(2)}) copy-start(f32[64,128]{1,0:T(8,128)} %constant.4.clone.inner_ref) | copy-start | bytes 98308
  2.4 15.4 %collective-permute-start.2 = (f32[21,16,384]{2,1,0:T(8,128)}, f32[21,16,384]{2,1,0:T(8,128)S(1)}, u32[]{:S(2)}, u32[]{:S(2)}) collective-permute-start(f32[21,16,384]{2,1,0:T(8,128)} %pack_bricks.1), channel_id=1, source_target_pairs={{0,4},{4,0},{8,12},{12,8},{16,20},{20,16},{24,28},{28,24},{1,5},{5... | collective-permute-start | bytes 1548296 | tf_op jit(solution)/shard_map/ppermute | solution.py:684
  5.0 1.3 %copy-start = (f32[5,4,32,512]{3,2,1,0:T(8,128)S(1)}, f32[5,4,32,512]{3,2,1,0:T(8,128)}, u32[]{:S(2)}) copy-start(f32[5,4,32,512]{3,2,1,0:T(8,128)} %refs_0_.5) | copy-start | bytes 3932164
  6.4 3.4 %copy-start.1 = (s32[4,32,512]{2,1,0:T(8,128)S(1)}, s32[4,32,512]{2,1,0:T(8,128)}, u32[]{:S(2)}) copy-start(s32[4,32,512]{2,1,0:T(8,128)} %refs_3_.5) | copy-start | bytes 786436
  9.8 23.7 %collective-permute-start.1 = (f32[21,16,384]{2,1,0:T(8,128)S(1)}, f32[21,16,384]{2,1,0:T(8,128)S(1)}, u32[]{:S(2)}, u32[]{:S(2)}) collective-permute-start(f32[21,16,384]{2,1,0:T(8,128)S(1)} %bring_planes.3), channel_id=1, source_target_pairs={{0,4},{4,0},{8,12},{12,8},{16,20},{20,16},{24,28},{28,24},{1,5},{5... | collective-permute-start | bytes 1548296 | tf_op jit(solution)/shard_map/ppermute | solution.py:692
  10.6 34.8 %collective-permute-start.4 = (f32[5,4,32,512]{3,2,1,0:T(8,128)S(1)}, f32[5,4,32,512]{3,2,1,0:T(8,128)S(1)}, u32[]{:S(2)}, u32[]{:S(2)}) collective-permute-start(f32[5,4,32,512]{3,2,1,0:T(8,128)S(1)} %get-tuple-element.14), channel_id=1, source_target_pairs={{0,2},{1,3},{2,0},{3,1},{4,6},{5,7},{6,4},{7,5},{8,10},{9,11},{10,... | collective-permute-start | bytes 3932168 | tf_op jit(solution)/shard_map/ppermute | solution.py:663
  14.3 7.5 %copy-start.2 = (s32[4,32,512]{2,1,0:T(8,128)S(1)}, s32[4,32,512]{2,1,0:T(8,128)}, u32[]{:S(2)}) copy-start(s32[4,32,512]{2,1,0:T(8,128)} %mask_ref.10) | copy-start | bytes 786436
  17.8 22.6 %collective-permute-start.5 = (f32[16,16,384]{2,1,0:T(8,128)S(1)}, f32[16,16,384]{2,1,0:T(8,128)S(1)}, u32[]{:S(2)}, u32[]{:S(2)}) collective-permute-start(f32[16,16,384]{2,1,0:T(8,128)S(1)} %pass_planes.2.after_ref), channel_id=1, source_target_pairs={{0,8},{8,16},{16,24},{12,4},{20,12},{28,20},{1,9},{9,17},{17,25},{... | collective-permute-start | bytes 1179656 | tf_op jit(solution)/shard_map/ppermute | solution.py:695
  24.8 18.4 %collective-permute-start.7 = (f32[16,32,128]{2,1,0:T(8,128)S(1)}, f32[16,32,128]{2,1,0:T(8,128)S(1)}, u32[]{:S(2)}, u32[]{:S(2)}) collective-permute-start(f32[16,32,128]{2,1,0:T(8,128)S(1)} %bring_planes.4.after_ref), channel_id=1, source_target_pairs={{4,8},{12,16},{20,24},{8,4},{16,12},{24,20},{5,9},{13,17},{21,25},... | collective-permute-start | bytes 786440 | tf_op jit(solution)/shard_map/ppermute | solution.py:698
  33.5 11.9 %collective-permute-start.3 = (f32[16,16,384]{2,1,0:T(8,128)S(1)}, f32[16,16,384]{2,1,0:T(8,128)S(1)}, u32[]{:S(2)}, u32[]{:S(2)}) collective-permute-start(f32[16,16,384]{2,1,0:T(8,128)S(1)} %pass_planes.3.after_ref), channel_id=1, source_target_pairs={{0,8},{8,16},{16,24},{12,4},{20,12},{28,20},{1,9},{9,17},{17,25},{... | collective-permute-start | bytes 1179656 | tf_op jit(solution)/shard_map/ppermute | solution.py:700
  37.1 6.5 %collective-permute-start.6 = (f32[16,32,128]{2,1,0:T(8,128)S(1)}, f32[16,32,128]{2,1,0:T(8,128)S(1)}, u32[]{:S(2)}, u32[]{:S(2)}) collective-permute-start(f32[16,32,128]{2,1,0:T(8,128)S(1)} %bring_planes.5), channel_id=1, source_target_pairs={{0,4},{4,0},{8,12},{12,8},{16,20},{20,16},{24,28},{28,24},{1,5},{5... | collective-permute-start | bytes 786440 | tf_op jit(solution)/shard_map/ppermute | solution.py:702

commit v3 on v2

--- a/solution.py
+++ b/solution.py
@@ -92,7 +92,7 @@
     return pl.ds(pl.multiple_of(number * LANES, LANES), LANES)
 
 
-def wall_kernel(low, state_ref, mask_ref, base_ref, out_ref, q_s, f_s, speed_s, dq_s, df_s):
+def wall_kernel(low, state_ref, mask_ref, out_ref, q_s, f_s, speed_s, dq_s, df_s):
     rows_y = state_ref.shape[2]
     width = state_ref.shape[3]
     tiles = rows_y // ROWS
@@ -173,31 +173,29 @@
             for r in range(tiles):
                 after = jnp.where(row == ROWS - 1, turned[r + 1], turned[r])
                 mine = slice(r * ROWS, r * ROWS + ROWS)
-                out_ref[k, plane, mine, lane] = base_ref[k, low + plane, mine, lane] + FACE_SCALE * (
-                    after - hats[r]
-                )
+                out_ref[k, plane, mine, lane] = q_s[k, still(r), :] + FACE_SCALE * (after - hats[r])
         return carry
 
     lax.fori_loop(0, out_ref.shape[1] * (width // LANES), column, 0)
 
 
-def wall_part(state, mask_y, base, low, count, after):
+def wall_part(state, mask_y, low, count, after):
     fields, depth, rows_y, width = state.shape
     tall = rows_y + 2 * ROWS
     padded = pltpu.VMEM((fields, tall, LANES), jnp.float32)
 
-    def kernel(state_ref, mask_ref, base_ref, after_ref, out_ref, *scratch):
-        wall_kernel(low, state_ref, mask_ref, base_ref, out_ref, *scratch)
+    def kernel(state_ref, mask_ref, after_ref, out_ref, *scratch):
+        wall_kernel(low, state_ref, mask_ref, out_ref, *scratch)
 
     return call(
         kernel,
         "wall_faces",
         5.0 * count / depth,
-        [PLACE, PLACE, PLACE, ANYWHERE],
+        [PLACE, PLACE, ANYWHERE],
         PLACE,
         shape_of(fields, count, rows_y, width),
         [padded, padded, pltpu.VMEM((tall, LANES), jnp.float32), padded, padded],
-    )(state, mask_y, base, after)
+    )(state, mask_y, after)
 
 
 def pack_kernel(parts, state_ref, mask_ref, *refs):
@@ -241,33 +239,26 @@
     )(state.reshape(planes, rows_all, width), mask_x)
 
 
-def bring_kernel(part, pieces, state_ref, mask_ref, after_ref, *outs):
+def bring_kernel(part, state_ref, mask_ref, after_ref, out):
     row, rows, lane, width = part
     fields, depth, _, _ = state_ref.shape
-    odd = lax.rem(lax.axis_index("gx"), 2)
-    for piece, out in zip(pieces, outs):
-        count = depth if piece == "all" else 3
-        skip = {"all": 0, "pair": 1 - odd, "across": odd}[piece] * (depth - 3)
-        for k in range(fields):
-            for i in range(count):
-                out[count * k + i] = state_ref[k, i + skip, row : row + rows, lane : lane + width]
-        switches = mask_ref[0, row : row + rows, lane : lane + width]
-        out[count * fields] = switches.astype(jnp.float32)
-
-
-def bring_part(state, mask_x, part, pieces, after):
+    for k in range(fields):
+        for i in range(depth):
+            out[depth * k + i] = state_ref[k, i, row : row + rows, lane : lane + width]
+    switches = mask_ref[0, row : row + rows, lane : lane + width]
+    out[depth * fields] = switches.astype(jnp.float32)
+
+
+def bring_part(state, mask_x, part, after):
     fields, depth, _, _ = state.shape
     _, rows, _, width = part
     return call(
-        functools.partial(bring_kernel, part, pieces),
+        functools.partial(bring_kernel, part),
         "bring_planes",
         0.5,
         [PLACE, PLACE, ANYWHERE],
-        [PLACE] * len(pieces),
-        [
-            shape_of((depth if piece == "all" else 3) * fields + 1, rows, width)
-            for piece in pieces
-        ],
+        PLACE,
+        shape_of(depth * fields + 1, rows, width),
     )(state, mask_x, after)
 
 
@@ -292,9 +283,8 @@
     )(pair, after)
 
 
-def stream_kernel(part, others, counts, *refs):
-    state_ref, pair_ref, far_ref, mask_ref = refs[:4]
-    acc_refs, refs = refs[4 : 4 + len(counts)], refs[4 + len(counts) :]
+def stream_kernel(part, others, *refs):
+    (state_ref, pair_ref, far_ref, mask_ref, base_ref), refs = refs[:5], refs[5:]
     if others is None:
         _, out_ref, dq_s, df_s, both_s, alpha_s = refs
         result = out_ref
@@ -304,7 +294,7 @@
         staged = refs[8:]
     fields, depth, _, _ = state_ref.shape
     start, rows_y, start_lane, width = part
-    stride = (pair_ref.shape[0] - 1) // fields
+    stride = depth
     rank = lax.axis_index("gx")
     even = lax.rem(rank, 2) == 0
     first = rank == 0
@@ -396,14 +386,11 @@
                 )
                 for f in range(faces)
             ]
-            plane = 0
-            for acc_ref, count in zip(acc_refs, counts):
-                for i in range(count):
-                    value = acc_ref[k, i, mine, there] + FACE_SCALE * (hats[plane + 1] - hats[plane])
-                    if others is not None:
-                        value = value - TIME_STEP * sum_ref[k, plane, mine, there]
-                    results.append(value)
-                    plane += 1
+            for i in range(depth):
+                value = base_ref[k, i, mine, there] + FACE_SCALE * (hats[i + 1] - hats[i])
+                if others is not None:
+                    value = value - TIME_STEP * sum_ref[k, i, mine, there]
+                results.append(value)
         for k in range(5):
             for i in range(depth):
                 result[k, i, row, lane] = results[k * depth + i]
@@ -449,11 +436,10 @@
         copy.wait()
 
 
-def stream_part(state, pair, far, mask_x, part, accs, after=None, arrived=None, others=None):
+def stream_part(state, pair, far, mask_x, part, base, after=None, arrived=None, others=None):
     fields, depth, _, _ = state.shape
     _, rows_y, _, width = part
     tiles = rows_y * width // (ROWS * LANES)
-    counts = [acc.shape[1] for acc in accs]
 
     def vregs(*dims):
         return pltpu.VMEM(dims + (ROWS, LANES), jnp.float32)
@@ -467,7 +453,7 @@
         vregs(tiles, fields, depth + 1),
         vregs(tiles, depth + 1),
     ]
-    inputs = [state, pair, far, mask_x, *accs]
+    inputs = [state, pair, far, mask_x, base]
     places_in = [PLACE] * len(inputs)
     if others is None:
         inputs.append(after)
@@ -485,9 +471,9 @@
             pltpu.SemaphoreType.DMA((len(others),)),
         ] + [pltpu.VMEM(cells(place), jnp.float32) for place in places]
     return call(
-        functools.partial(stream_kernel, part, places, counts),
+        functools.partial(stream_kernel, part, places),
         "stream_faces",
-        0.6 * tiles,
+        0.3 * tiles,
         places_in,
         target,
         target_shape,
@@ -634,23 +620,25 @@
     return outs[: len(masks)], outs[len(masks) :]
 
 
-def home_kernel(high_ref, low_ref, xh, xl, state_ref, out_ref, w_s):
+def home_kernel(high_ref, low_ref, xh, xl, first_ref, second_ref, out_ref, w_s):
     me = lax.axis_index("gz")
-    total = product(me, [me, me ^ 1], high_ref, low_ref, xh, xl, w_s)
-    out_ref[...] = state_ref[...] - TIME_STEP * total.reshape(state_ref.shape)
-
-
-def home_part(band, lines, state):
-    width = state.shape[3]
+    half = first_ref.shape[1]
+    total = product(me, [me, me ^ 1], high_ref, low_ref, xh, xl, w_s).reshape(out_ref.shape)
+    out_ref[:, :half] = first_ref[...] - TIME_STEP * total[:, :half]
+    out_ref[:, half:] = second_ref[...] - TIME_STEP * total[:, half:]
+
+
+def home_part(band, lines, first, second):
+    fields, half, rows_all, width = first.shape
     return call(
         home_kernel,
         "span_home",
         2.0,
-        [PLACE] * 5,
+        [PLACE] * 6,
         PLACE,
-        shape_of(*state.shape),
+        shape_of(fields, half + second.shape[1], rows_all, width),
         [pltpu.VMEM((4 * width, width), jnp.bfloat16)],
-    )(*band, *lines, state)
+    )(*band, *lines, first, second)
 
 
 def per_device(state, mask_x, mask_y, span_filter):
@@ -677,9 +665,6 @@
     else:
         part = rows_all // 4
         parts = [(0, 2 * part, 0, width), (2 * part, part, 0, width), (3 * part, part, 0, width)]
-    across = [(i, i + 1) for i in range(1, slabs - 1, 2)]
-    across += [(target, source) for source, target in across]
-
     (brick,) = pack_part(state, mask_x, parts[:1])
     pairs = [lax.ppermute(brick, "gx", swap)]
     band = circulant(span_filter, span, width, core)
@@ -688,27 +673,26 @@
     sums, lines = away_part(band, state, core, masks)
     arrived = sum(flip(part_sum, mask) for part_sum, mask in zip(sums, masks))
     half = depth // 2
-    (brick,) = bring_part(state, mask_x, parts[1], ["all"], lines[0])
+    acc_low = wall_part(state, mask_y, 0, half, lines[0])
+    brick = bring_part(state, mask_x, parts[1], acc_low)
     pairs.append(lax.ppermute(brick, "gx", swap))
-    base = home_part(band, lines, state)
-    planes = pass_part(pairs[0], depth, base)
+    planes = pass_part(pairs[0], depth, brick)
     fars = [lax.ppermute(planes, "gx", carry)]
-    acc_low = wall_part(state, mask_y, base, 0, half, planes)
-    (outer,) = bring_part(state, mask_x, parts[2], ["across"], acc_low)
-    last = lax.ppermute(outer, "gx", across)
-    planes = pass_part(pairs[1], depth, outer)
-    fars += [lax.ppermute(planes, "gx", carry), last]
-    (inner,) = bring_part(state, mask_x, parts[2], ["pair"], planes)
-    pairs.append(lax.ppermute(inner, "gx", swap))
-    acc_high = wall_part(state, mask_y, base, half, depth - half, planes)
-
-    accs = [acc_low, acc_high]
-    ready, after = [], acc_high
-    for c in (0, 2):
-        after = stream_part(state, pairs[c], fars[c], mask_x, parts[c], accs, after)
-        ready.append((parts[c], after))
+    acc_high = wall_part(state, mask_y, half, depth - half, planes)
+    base = home_part(band, lines, acc_low, acc_high)
+    brick = bring_part(state, mask_x, parts[2], base)
+    pairs.append(lax.ppermute(brick, "gx", swap))
+
+    planes = pass_part(pairs[1], depth, brick)
+    fars.append(lax.ppermute(planes, "gx", carry))
+    ready = stream_part(state, pairs[0], fars[0], mask_x, parts[0], base, planes)
+    others = [(parts[0], ready)]
+    planes = pass_part(pairs[2], depth, ready)
+    fars.append(lax.ppermute(planes, "gx", carry))
+    ready = stream_part(state, pairs[1], fars[1], mask_x, parts[1], base, planes)
+    others.append((parts[1], ready))
     return stream_part(
-        state, pairs[1], fars[1], mask_x, parts[1], accs, arrived=arrived, others=ready
+        state, pairs[2], fars[2], mask_x, parts[2], base, arrived=arrived, others=others
     )
 
 

time: 50.4 us -> 49.5 us (0.982); the launches traced: 49.5 us -> 49.3 us
  waiting for transfers between devices: 12.1 us -> 8.7 us
  starting transfers between devices: 13.8 us -> 17.1 us
    ppermute x1 -> x2, waiting for transfers between devices: 8.08 us -> 2.24 us  [per_device(): pairs.append(lax.ppermute(brick, 'gx', swap))]
    ppermute x3 -> x2, waiting for transfers between devices: 0.52 us -> 3.75 us  [per_device(): fars.append(lax.ppermute(planes, 'gx', carry))]
    ppermute x3 -> x2, starting transfers between devices: 4.52 us -> 7.7 us  [per_device(): fars.append(lax.ppermute(planes, 'gx', carry))]
    ppermute x1, waiting for transfers between devices: 3.47 us -> 2.71 us  [per_device(): pairs = [lax.ppermute(brick, 'gx', swap)]]
    pallas_call x9 -> x8, Pallas kernels: 16.7 us -> 16.6 us  [the longest x3 8.46 us: stream_part(): call(functools.partial(stream_kernel, part, places), 'stream_faces', 0.3...]
  transfers between devices with their start and end apart: 8 -> 8, of which waited for: 3 -> 5; matrix products, arithmetic and copies ran while one was open for 0% -> 0% of each run, Pallas kernels for 38% -> 40%
where the time goes in v3:
time: 49.5 us; the launch traced here: 49.3 us
  Pallas kernels  22.8 us (46%)
  starting transfers between devices  17.1 us (35%)
  waiting for transfers between devices  8.7 us (18%)
  local copies, waits for them, and re-layouts  0.59 us (1%)
    pallas_call x3, Pallas kernels, stream_part(): call(functools.partial(stream_kernel, part, places), 'stream_faces', 0.3...  8.46 us
    ppermute x2, starting transfers between devices, per_device(): fars.append(lax.ppermute(planes, 'gx', carry))  7.7 us
    pallas_call x2, Pallas kernels, wall_part(): call(kernel, 'wall_faces', 5.0 * count / depth, [PLACE, PLACE, ANYWHERE],...  5.82 us
    ppermute x1, starting transfers between devices, per_device(): fars = [lax.ppermute(planes, 'gx', carry)]  3.96 us
    ppermute x2, waiting for transfers between devices, per_device(): fars.append(lax.ppermute(planes, 'gx', carry))  3.75 us
    pallas_call x1, Pallas kernels, away_part(): call(functools.partial(away_kernel, masks), 'span_away', 3.0, [PLACE] * 4...  3.41 us
    ppermute x1, waiting for transfers between devices, per_device(): pairs = [lax.ppermute(brick, 'gx', swap)]  2.71 us
    ppermute x1, starting transfers between devices, per_device(): pairs = [lax.ppermute(brick, 'gx', swap)]  2.57 us
  transfers between devices with their start and end apart: 8, of which 5 were waited for; matrix products, arithmetic and copies ran while one was open for 0% of the time, Pallas kernels for 40%

profile of v3, /device:TPU:0, one launch (start us, length us, event | category | flops | bytes accessed | tf_op | source)
XLA Modules:
  0.0 49.3 jit_solution(1854548759372779728)
XLA Ops:
  0.0 0.5 collective-permute-start
  0.5 0.0 copy-start.5
  0.5 0.0 copy-start.3
  0.5 0.0 copy-start.4
  0.5 1.9 %pack_bricks.1 = f32[21,16,384]{2,1,0:T(8,128)} custom-call(f32[20,32,512]{2,1,0:T(8,128)} %bitcast.1, s32[4,32,512]{2,1,0:T(8,128)} %refs_3_.5), custom_call_target="tpu_custom_call" | custom-call | flops 1000000000 | bytes 3000000 | tf_op jit(solution)/shard_map/pack_bricks/pallas_call | solution.py:227
  2.4 2.6 %collective-permute-start.1 = (f32[21,16,384]{2,1,0:T(8,128)}, f32[21,16,384]{2,1,0:T(8,128)S(1)}, u32[]{:S(2)}, u32[]{:S(2)}) collective-permute-start(f32[21,16,384]{2,1,0:T(8,128)} %pack_bricks.1), channel_id=1, source_target_pairs={{0,4},{4,0},{8,12},{12,8},{16,20},{20,16},{24,28},{28,24},{1,5},{5... | collective-permute-start | bytes 1548296 | tf_op jit(solution)/shard_map/ppermute | solution.py:669
  5.0 0.0 copy-done.5
  5.0 0.1 reshape.6.filter_ref
  5.0 0.0 copy-start
  5.0 0.0 collective-permute-done.after_ref.core_ref
  5.1 0.0 copy-done.3
  5.1 0.0 copy-done.4
  5.1 0.8 %circulant_band.1 = (bf16[256,2560]{1,0:T(8,128)(2,1)S(1)}, bf16[256,2560]{1,0:T(8,128)(2,1)S(1)}) custom-call(f32[32,32]{1,0:T(8,128)S(1)} %reshape.6.filter_ref, f32[64,128]{1,0:T(8,128)S(1)} %copy-done.4, f32[64,2048]{1,0:T(8,128)S(1)} %copy-done.3, f32[5,4,32,512]{3,2,1,0:T(8,128)S(1)} %collective-permute-done.after_ref.core_ref), custom_call_target="tpu_custom_call" | custom-call | flops 1000000000 | bytes 3000000 | tf_op jit(solution)/shard_map/circulant_band/pallas_call | solution.py:550
  5.9 0.5 %copy-done = f32[5,4,32,512]{3,2,1,0:T(8,128)S(1)} copy-done((f32[5,4,32,512]{3,2,1,0:T(8,128)S(1)}, f32[5,4,32,512]{3,2,1,0:T(8,128)}, u32[]{:S(2)}) %copy-start) | copy-done | bytes 1310744
  6.4 0.0 copy-start.2
  6.4 3.4 %span_away.1 = (f32[5,4,32,512]{3,2,1,0:T(8,128)S(1)}, bf16[640,1024]{1,0:T(8,128)(2,1)S(1)}, bf16[640,1024]{1,0:T(8,128)(2,1)S(1)}) custom-call(bf16[256,2560]{1,0:T(8,128)(2,1)S(1)} %get-tuple-element.10.high_ref, bf16[256,2560]{1,0:T(8,128)(2,1)S(1)} %get-tuple-element.11.low_ref, f32[5,4,32,512]{3,2,1,0:T(8,128)S(1)} %copy-done, ...), custom_call_target="tpu_custom_call" | custom-call | flops 3000000000 | bytes 9000000 | tf_op jit(solution)/shard_map/span_away/pallas_call | solution.py:611
  9.8 1.6 %collective-permute-start.6 = (f32[5,4,32,512]{3,2,1,0:T(8,128)S(1)}, f32[5,4,32,512]{3,2,1,0:T(8,128)S(1)}, u32[]{:S(2)}, u32[]{:S(2)}) collective-permute-start(f32[5,4,32,512]{3,2,1,0:T(8,128)S(1)} %get-tuple-element.14), channel_id=1, source_target_pairs={{0,2},{1,3},{2,0},{3,1},{4,6},{5,7},{6,4},{7,5},{8,10},{9,11},{10,... | collective-permute-start | bytes 3932168 | tf_op jit(solution)/shard_map/ppermute | solution.py:651
  11.4 0.0 copy-done.2
  11.4 0.0 copy-start.1
  11.4 2.9 %wall_faces.2.after_ref.first_ref = f32[5,2,32,512]{3,2,1,0:T(8,128)S(1)} custom-call(f32[5,4,32,512]{3,2,1,0:T(8,128)S(1)} %copy-done, s32[4,32,512]{2,1,0:T(8,128)S(1)} %copy-done.2, bf16[640,1024]{1,0:T(8,128)(2,1)S(1)} %get-tuple-element.12.after_ref.xh), custom_call_target="tpu_custom_call" | custom-call | flops 2500000000 | bytes 7500000 | tf_op jit(solution)/shard_map/wall_faces/pallas_call | solution.py:190
  14.3 0.0 copy-done.1
  14.3 0.7 %collective-permute-start.4 = (f32[21,16,384]{2,1,0:T(8,128)S(1)}, f32[21,16,384]{2,1,0:T(8,128)S(1)}, u32[]{:S(2)}, u32[]{:S(2)}) collective-permute-start(f32[21,16,384]{2,1,0:T(8,128)S(1)} %bring_planes.2.after_ref), channel_id=1, source_target_pairs={{0,4},{4,0},{8,12},{12,8},{16,20},{20,16},{24,28},{28,24},{1,5},{5... | collective-permute-start | bytes 1548296 | tf_op jit(solution)/shard_map/ppermute | solution.py:678
  15.1 2.7 %collective-permute-done.1.pair_ref.refs_1_ = f32[21,16,384]{2,1,0:T(8,128)S(1)} collective-permute-done((f32[21,16,384]{2,1,0:T(8,128)}, f32[21,16,384]{2,1,0:T(8,128)S(1)}, u32[]{:S(2)}, u32[]{:S(2)}) %collective-permute-start.1) | collective-permute-done | bytes 516128 | tf_op jit(solution)/shard_map/ppermute | solution.py:669
  17.8 4.0 %collective-permute-start.3 = (f32[16,16,384]{2,1,0:T(8,128)S(1)}, f32[16,16,384]{2,1,0:T(8,128)S(1)}, u32[]{:S(2)}, u32[]{:S(2)}) collective-permute-start(f32[16,16,384]{2,1,0:T(8,128)S(1)} %pass_planes.3.after_ref), channel_id=1, source_target_pairs={{0,8},{8,16},{16,24},{12,4},{20,12},{28,20},{1,9},{9,17},{17,25},{... | collective-permute-start | bytes 1179656 | tf_op jit(solution)/shard_map/ppermute | solution.py:680
  21.8 2.9 %wall_faces.3.second_ref = f32[5,2,32,512]{3,2,1,0:T(8,128)S(1)} custom-call(f32[5,4,32,512]{3,2,1,0:T(8,128)S(1)} %copy-done, s32[4,32,512]{2,1,0:T(8,128)S(1)} %copy-done.2, f32[16,16,384]{2,1,0:T(8,128)S(1)} %pass_planes.3.after_ref), custom_call_target="tpu_custom_call" | custom-call | flops 2500000000 | bytes 7500000 | tf_op jit(solution)/shard_map/wall_faces/pallas_call | solution.py:190
  24.7 2.2 %span_home.1.after_ref.refs_4_ = f32[5,4,32,512]{3,2,1,0:T(8,128)S(1)} custom-call(bf16[256,2560]{1,0:T(8,128)(2,1)S(1)} %get-tuple-element.10.high_ref, bf16[256,2560]{1,0:T(8,128)(2,1)S(1)} %get-tuple-element.11.low_ref, bf16[640,1024]{1,0:T(8,128)(2,1)S(1)} %get-tuple-element.12.after_ref.xh, bf16[640,1024]{1,0:T(8,128)(2,1)S(1)} %get-tuple-element.13.xl, ...), custom_call_target="tpu_custom_call" | custom-call | flops 2000000000 | bytes 6000000 | tf_op jit(solution)/shard_map/span_home/pallas_call | solution.py:633
  27.0 0.1 collective-permute-start.2
  27.0 1.6 %collective-permute-done.4.pair_ref.refs_1_ = f32[21,16,384]{2,1,0:T(8,128)S(1)} collective-permute-done((f32[21,16,384]{2,1,0:T(8,128)S(1)}, f32[21,16,384]{2,1,0:T(8,128)S(1)}, u32[]{:S(2)}, u32[]{:S(2)}) %collective-permute-start.4) | collective-permute-done | bytes 516128 | tf_op jit(solution)/shard_map/ppermute | solution.py:678
  28.7 4.0 %collective-permute-start.7 = (f32[16,16,384]{2,1,0:T(8,128)S(1)}, f32[16,16,384]{2,1,0:T(8,128)S(1)}, u32[]{:S(2)}, u32[]{:S(2)}) collective-permute-start(f32[16,16,384]{2,1,0:T(8,128)S(1)} %pass_planes.4.refs_5_), channel_id=1, source_target_pairs={{0,8},{8,16},{16,24},{12,4},{20,12},{28,20},{1,9},{9,17},{17,25},{... | collective-permute-start | bytes 1179656 | tf_op jit(solution)/shard_map/ppermute | solution.py:687
  32.6 0.0 collective-permute-done.3.refs_2_
  32.6 2.7 %stream_faces.3.after_ref.refs_6_ = f32[5,4,16,384]{3,2,1,0:T(8,128)S(1)} custom-call(f32[5,4,32,512]{3,2,1,0:T(8,128)S(1)} %copy-done, f32[21,16,384]{2,1,0:T(8,128)S(1)} %collective-permute-done.1.pair_ref.refs_1_, f32[16,16,384]{2,1,0:T(8,128)S(1)} %collective-permute-done.3.refs_2_, s32[4,32,512]{2,1,0:T(8,128)S(1)} %copy-done.1, ...), custom_call_target="tpu_custom_call" | custom-call | flops 1800000000 | bytes 5399999 | tf_op jit(solution)/shard_map/stream_faces/pallas_call | solution.py:473
  35.4 0.6 %collective-permute-done.2.pair_ref.refs_1_ = f32[21,32,128]{2,1,0:T(8,128)S(1)} collective-permute-done((f32[21,32,128]{2,1,0:T(8,128)S(1)}, f32[21,32,128]{2,1,0:T(8,128)S(1)}, u32[]{:S(2)}, u32[]{:S(2)}) %collective-permute-start.2) | collective-permute-done | bytes 344096 | tf_op jit(solution)/shard_map/ppermute | solution.py:684
  36.0 3.7 %collective-permute-start.5 = (f32[16,32,128]{2,1,0:T(8,128)S(1)}, f32[16,32,128]{2,1,0:T(8,128)S(1)}, u32[]{:S(2)}, u32[]{:S(2)}) collective-permute-start(f32[16,32,128]{2,1,0:T(8,128)S(1)} %pass_planes.5.refs_5_), channel_id=1, source_target_pairs={{0,8},{8,16},{16,24},{12,4},{20,12},{28,20},{1,9},{9,17},{17,25},{... | collective-permute-start | bytes 786440 | tf_op jit(solution)/shard_map/ppermute | solution.py:691
  39.8 2.4 %collective-permute-done.7.refs_2_ = f32[16,16,384]{2,1,0:T(8,128)S(1)} collective-permute-done((f32[16,16,384]{2,1,0:T(8,128)S(1)}, f32[16,16,384]{2,1,0:T(8,128)S(1)}, u32[]{:S(2)}, u32[]{:S(2)}) %collective-permute-start.7) | collective-permute-done | bytes 393248 | tf_op jit(solution)/shard_map/ppermute | solution.py:687
  42.2 2.7 %stream_faces.4.refs_7_ = f32[5,4,16,384]{3,2,1,0:T(8,128)S(1)} custom-call(f32[5,4,32,512]{3,2,1,0:T(8,128)S(1)} %copy-done, f32[21,16,384]{2,1,0:T(8,128)S(1)} %collective-permute-done.4.pair_ref.refs_1_, f32[16,16,384]{2,1,0:T(8,128)S(1)} %collective-permute-done.7.refs_2_, s32[4,32,512]{2,1,0:T(8,128)S(1)} %copy-done.1, ...), custom_call_target="tpu_custom_call" | custom-call | flops 1800000000 | bytes 5399999 | tf_op jit(solution)/shard_map/stream_faces/pallas_call | solution.py:473
  44.9 1.4 %collective-permute-done.5.refs_2_ = f32[16,32,128]{2,1,0:T(8,128)S(1)} collective-permute-done((f32[16,32,128]{2,1,0:T(8,128)S(1)}, f32[16,32,128]{2,1,0:T(8,128)S(1)}, u32[]{:S(2)}, u32[]{:S(2)}) %collective-permute-start.5) | collective-permute-done | bytes 262176 | tf_op jit(solution)/shard_map/ppermute | solution.py:691
  46.3 0.0 collective-permute-done.6.refs_5_
  46.3 3.0 %stream_faces.5 = f32[5,4,32,512]{3,2,1,0:T(8,128)} custom-call(f32[5,4,32,512]{3,2,1,0:T(8,128)S(1)} %copy-done, f32[21,32,128]{2,1,0:T(8,128)S(1)} %collective-permute-done.2.pair_ref.refs_1_, f32[16,32,128]{2,1,0:T(8,128)S(1)} %collective-permute-done.5.refs_2_, s32[4,32,512]{2,1,0:T(8,128)S(1)} %copy-done.1, ...), custom_call_target="tpu_custom_call" | custom-call | flops 1200000000 | bytes 3600000 | tf_op jit(solution)/shard_map/stream_faces/pallas_call | solution.py:473
  (5 shorter events, 0.2 us)
Async XLA Ops:
  0.0 5.0 %collective-permute-start = (f32[5,4,32,512]{3,2,1,0:T(8,128)}, f32[5,4,32,512]{3,2,1,0:T(8,128)S(1)}, u32[]{:S(2)}, u32[]{:S(2)}) collective-permute-start(f32[5,4,32,512]{3,2,1,0:T(8,128)} %refs_0_.5), channel_id=1, source_target_pairs={{0,1},{1,0},{2,3},{3,2},{4,5},{5,4},{6,7},{7,6},{8,9},{9,8},{10,11... | collective-permute-start | bytes 3932168 | tf_op jit(solution)/shard_map/ppermute | solution.py:651
  0.5 4.5 %copy-start.5 = (f32[1024]{0:T(1024)S(1)}, f32[1024]{0:T(1024)}, u32[]{:S(2)}) copy-start(f32[1024]{0:T(1024)} %param.9) | copy-start | bytes 12292
  0.5 4.6 %copy-start.3 = (f32[64,2048]{1,0:T(8,128)S(1)}, f32[64,2048]{1,0:T(8,128)}, u32[]{:S(2)}) copy-start(f32[64,2048]{1,0:T(8,128)} %constant.5.clone.outer_ref) | copy-start | bytes 1572868
  0.5 4.6 %copy-start.4 = (f32[64,128]{1,0:T(8,128)S(1)}, f32[64,128]{1,0:T(8,128)}, u32[]{:S(2)}) copy-start(f32[64,128]{1,0:T(8,128)} %constant.4.clone.inner_ref) | copy-start | bytes 98308
  2.4 15.4 %collective-permute-start.1 = (f32[21,16,384]{2,1,0:T(8,128)}, f32[21,16,384]{2,1,0:T(8,128)S(1)}, u32[]{:S(2)}, u32[]{:S(2)}) collective-permute-start(f32[21,16,384]{2,1,0:T(8,128)} %pack_bricks.1), channel_id=1, source_target_pairs={{0,4},{4,0},{8,12},{12,8},{16,20},{20,16},{24,28},{28,24},{1,5},{5... | collective-permute-start | bytes 1548296 | tf_op jit(solution)/shard_map/ppermute | solution.py:669
  5.0 1.3 %copy-start = (f32[5,4,32,512]{3,2,1,0:T(8,128)S(1)}, f32[5,4,32,512]{3,2,1,0:T(8,128)}, u32[]{:S(2)}) copy-start(f32[5,4,32,512]{3,2,1,0:T(8,128)} %refs_0_.5) | copy-start | bytes 3932164
  6.4 5.0 %copy-start.2 = (s32[4,32,512]{2,1,0:T(8,128)S(1)}, s32[4,32,512]{2,1,0:T(8,128)}, u32[]{:S(2)}) copy-start(s32[4,32,512]{2,1,0:T(8,128)} %mask_ref.8) | copy-start | bytes 786436
  9.8 36.5 %collective-permute-start.6 = (f32[5,4,32,512]{3,2,1,0:T(8,128)S(1)}, f32[5,4,32,512]{3,2,1,0:T(8,128)S(1)}, u32[]{:S(2)}, u32[]{:S(2)}) collective-permute-start(f32[5,4,32,512]{3,2,1,0:T(8,128)S(1)} %get-tuple-element.14), channel_id=1, source_target_pairs={{0,2},{1,3},{2,0},{3,1},{4,6},{5,7},{6,4},{7,5},{8,10},{9,11},{10,... | collective-permute-start | bytes 3932168 | tf_op jit(solution)/shard_map/ppermute | solution.py:651
  11.4 2.9 %copy-start.1 = (s32[4,32,512]{2,1,0:T(8,128)S(1)}, s32[4,32,512]{2,1,0:T(8,128)}, u32[]{:S(2)}) copy-start(s32[4,32,512]{2,1,0:T(8,128)} %refs_3_.5) | copy-start | bytes 786436
  14.3 14.3 %collective-permute-start.4 = (f32[21,16,384]{2,1,0:T(8,128)S(1)}, f32[21,16,384]{2,1,0:T(8,128)S(1)}, u32[]{:S(2)}, u32[]{:S(2)}) collective-permute-start(f32[21,16,384]{2,1,0:T(8,128)S(1)} %bring_planes.2.after_ref), channel_id=1, source_target_pairs={{0,4},{4,0},{8,12},{12,8},{16,20},{20,16},{24,28},{28,24},{1,5},{5... | collective-permute-start | bytes 1548296 | tf_op jit(solution)/shard_map/ppermute | solution.py:678
  17.8 14.8 %collective-permute-start.3 = (f32[16,16,384]{2,1,0:T(8,128)S(1)}, f32[16,16,384]{2,1,0:T(8,128)S(1)}, u32[]{:S(2)}, u32[]{:S(2)}) collective-permute-start(f32[16,16,384]{2,1,0:T(8,128)S(1)} %pass_planes.3.after_ref), channel_id=1, source_target_pairs={{0,8},{8,16},{16,24},{12,4},{20,12},{28,20},{1,9},{9,17},{17,25},{... | collective-permute-start | bytes 1179656 | tf_op jit(solution)/shard_map/ppermute | solution.py:680
  27.0 9.1 %collective-permute-start.2 = (f32[21,32,128]{2,1,0:T(8,128)S(1)}, f32[21,32,128]{2,1,0:T(8,128)S(1)}, u32[]{:S(2)}, u32[]{:S(2)}) collective-permute-start(f32[21,32,128]{2,1,0:T(8,128)S(1)} %bring_planes.3.after_ref), channel_id=1, source_target_pairs={{0,4},{4,0},{8,12},{12,8},{16,20},{20,16},{24,28},{28,24},{1,5},{5... | collective-permute-start | bytes 1032200 | tf_op jit(solution)/shard_map/ppermute | solution.py:684
  28.7 13.5 %collective-permute-start.7 = (f32[16,16,384]{2,1,0:T(8,128)S(1)}, f32[16,16,384]{2,1,0:T(8,128)S(1)}, u32[]{:S(2)}, u32[]{:S(2)}) collective-permute-start(f32[16,16,384]{2,1,0:T(8,128)S(1)} %pass_planes.4.refs_5_), channel_id=1, source_target_pairs={{0,8},{8,16},{16,24},{12,4},{20,12},{28,20},{1,9},{9,17},{17,25},{... | collective-permute-start | bytes 1179656 | tf_op jit(solution)/shard_map/ppermute | solution.py:687
  36.0 10.2 %collective-permute-start.5 = (f32[16,32,128]{2,1,0:T(8,128)S(1)}, f32[16,32,128]{2,1,0:T(8,128)S(1)}, u32[]{:S(2)}, u32[]{:S(2)}) collective-permute-start(f32[16,32,128]{2,1,0:T(8,128)S(1)} %pass_planes.5.refs_5_), channel_id=1, source_target_pairs={{0,8},{8,16},{16,24},{12,4},{20,12},{28,20},{1,9},{9,17},{17,25},{... | collective-permute-start | bytes 786440 | tf_op jit(solution)/shard_map/ppermute | solution.py:691

commit v4 on v3

--- a/solution.py
+++ b/solution.py
@@ -620,7 +620,7 @@
     return outs[: len(masks)], outs[len(masks) :]
 
 
-def home_kernel(high_ref, low_ref, xh, xl, first_ref, second_ref, out_ref, w_s):
+def home_kernel(high_ref, low_ref, xh, xl, first_ref, second_ref, after_ref, out_ref, w_s):
     me = lax.axis_index("gz")
     half = first_ref.shape[1]
     total = product(me, [me, me ^ 1], high_ref, low_ref, xh, xl, w_s).reshape(out_ref.shape)
@@ -628,17 +628,17 @@
     out_ref[:, half:] = second_ref[...] - TIME_STEP * total[:, half:]
 
 
-def home_part(band, lines, first, second):
+def home_part(band, lines, first, second, after):
     fields, half, rows_all, width = first.shape
     return call(
         home_kernel,
         "span_home",
         2.0,
-        [PLACE] * 6,
+        [PLACE] * 6 + [ANYWHERE],
         PLACE,
         shape_of(fields, half + second.shape[1], rows_all, width),
         [pltpu.VMEM((4 * width, width), jnp.bfloat16)],
-    )(*band, *lines, first, second)
+    )(*band, *lines, first, second, after)
 
 
 def per_device(state, mask_x, mask_y, span_filter):
@@ -655,16 +655,17 @@
         (i, i - 2) for i in range(3, slabs, 2)
     ]
     core = flip(state, 1)
+    low = rows_all // 2
     if width % (4 * LANES) == 0:
-        narrow = width // 4
+        lane = width // 4
         parts = [
-            (0, rows_all // 2, 0, width - narrow),
-            (rows_all // 2, rows_all // 2, 0, width - narrow),
-            (0, rows_all, width - narrow, narrow),
+            (0, low, 0, 3 * lane),
+            (low, low, 0, 2 * lane),
+            (0, rows_all, 3 * lane, lane),
+            (low, low, 2 * lane, lane),
         ]
     else:
-        part = rows_all // 4
-        parts = [(0, 2 * part, 0, width), (2 * part, part, 0, width), (3 * part, part, 0, width)]
+        parts = [(row, rows_all // 4, 0, width) for row in range(0, rows_all, rows_all // 4)]
     (brick,) = pack_part(state, mask_x, parts[:1])
     pairs = [lax.ppermute(brick, "gx", swap)]
     band = circulant(span_filter, span, width, core)
@@ -673,26 +674,33 @@
     sums, lines = away_part(band, state, core, masks)
     arrived = sum(flip(part_sum, mask) for part_sum, mask in zip(sums, masks))
     half = depth // 2
+    fars, others = [], []
+
+    def exchange(c, after):
+        brick = bring_part(state, mask_x, parts[c], after)
+        pairs.append(lax.ppermute(brick, "gx", swap))
+        return brick
+
+    def hand_on(c, after):
+        planes = pass_part(pairs[c], depth, after)
+        fars.append(lax.ppermute(planes, "gx", carry))
+        return planes
+
+    def stream(c, after):
+        done = stream_part(state, pairs[c], fars[c], mask_x, parts[c], base, after)
+        others.append((parts[c], done))
+        return done
+
     acc_low = wall_part(state, mask_y, 0, half, lines[0])
-    brick = bring_part(state, mask_x, parts[1], acc_low)
-    pairs.append(lax.ppermute(brick, "gx", swap))
-    planes = pass_part(pairs[0], depth, brick)
-    fars = [lax.ppermute(planes, "gx", carry)]
-    acc_high = wall_part(state, mask_y, half, depth - half, planes)
-    base = home_part(band, lines, acc_low, acc_high)
-    brick = bring_part(state, mask_x, parts[2], base)
-    pairs.append(lax.ppermute(brick, "gx", swap))
-
-    planes = pass_part(pairs[1], depth, brick)
-    fars.append(lax.ppermute(planes, "gx", carry))
-    ready = stream_part(state, pairs[0], fars[0], mask_x, parts[0], base, planes)
-    others = [(parts[0], ready)]
-    planes = pass_part(pairs[2], depth, ready)
-    fars.append(lax.ppermute(planes, "gx", carry))
-    ready = stream_part(state, pairs[1], fars[1], mask_x, parts[1], base, planes)
-    others.append((parts[1], ready))
+    after = hand_on(0, exchange(1, acc_low))
+    acc_high = wall_part(state, mask_y, half, depth - half, after)
+    after = hand_on(1, exchange(2, acc_high))
+    base = home_part(band, lines, acc_low, acc_high, after)
+    after = hand_on(2, exchange(3, base))
+    after = hand_on(3, stream(0, after))
+    stream(2, stream(1, after))
     return stream_part(
-        state, pairs[2], fars[2], mask_x, parts[2], base, arrived=arrived, others=others
+        state, pairs[3], fars[3], mask_x, parts[3], base, arrived=arrived, others=others
     )
 
 

time: 49.5 us -> 50.6 us (1.022)
  starting transfers between devices: 17.1 us -> 20.1 us
  waiting for transfers between devices: 8.7 us -> 6.3 us
    ppermute x5 -> x7, starting transfers between devices: 12.5 us -> 15.5 us  [the longest x4 14.7 us: hand_on(): fars.append(lax.ppermute(planes, 'gx', carry))]
    ppermute x5 -> x7, waiting for transfers between devices: 5.99 us -> 3.58 us  [the longest x3 3.57 us: exchange(): pairs.append(lax.ppermute(brick, 'gx', swap))]
    pallas_call x3 -> x4, Pallas kernels: 8.46 us -> 8.74 us  [stream_part(): call(functools.partial(stream_kernel, part, places), 'stream_faces', 0.3...]
  transfers between devices with their start and end apart: 8 -> 10, of which waited for: 5 -> 3; matrix products, arithmetic and copies ran while one was open for 0% -> 0% of each run, Pallas kernels for 40% -> 41%
where the time goes in v4:
time: 50.6 us; the launch traced here: 50.3 us
  Pallas kernels  23.1 us (46%)
  starting transfers between devices  20.1 us (40%)
  waiting for transfers between devices  6.3 us (12%)
  local copies, waits for them, and re-layouts  0.59 us (1%)
    ppermute x4, starting transfers between devices, hand_on(): fars.append(lax.ppermute(planes, 'gx', carry))  14.7 us
    pallas_call x4, Pallas kernels, stream_part(): call(functools.partial(stream_kernel, part, places), 'stream_faces', 0.3...  8.74 us
    pallas_call x2, Pallas kernels, wall_part(): call(kernel, 'wall_faces', 5.0 * count / depth, [PLACE, PLACE, ANYWHERE],...  5.82 us
    ppermute x3, waiting for transfers between devices, exchange(): pairs.append(lax.ppermute(brick, 'gx', swap))  3.57 us
    pallas_call x1, Pallas kernels, away_part(): call(functools.partial(away_kernel, masks), 'span_away', 3.0, [PLACE] * 4...  3.41 us
    ppermute x1, waiting for transfers between devices, per_device(): pairs = [lax.ppermute(brick, 'gx', swap)]  2.72 us
    ppermute x1, starting transfers between devices, per_device(): pairs = [lax.ppermute(brick, 'gx', swap)]  2.57 us
    pallas_call x1, Pallas kernels, home_part(): call(home_kernel, 'span_home', 2.0, [PLACE] * 6 + [ANYWHERE], PLACE, shap...  2.2 us
  transfers between devices with their start and end apart: 10, of which 3 were waited for; matrix products, arithmetic and copies ran while one was open for 0% of the time, Pallas kernels for 41%

profile of v4, /device:TPU:0, one launch (start us, length us, event | category | flops | bytes accessed | tf_op | source)
XLA Modules:
  0.0 50.3 jit_solution(3720452316144943977)
XLA Ops:
  0.0 0.5 collective-permute-start
  0.5 0.0 copy-start.5
  0.5 0.0 copy-start.3
  0.5 0.0 copy-start.4
  0.5 1.9 %pack_bricks.1 = f32[21,16,384]{2,1,0:T(8,128)} custom-call(f32[20,32,512]{2,1,0:T(8,128)} %bitcast.1, s32[4,32,512]{2,1,0:T(8,128)} %refs_3_.7), custom_call_target="tpu_custom_call" | custom-call | flops 1000000000 | bytes 3000000 | tf_op jit(solution)/shard_map/pack_bricks/pallas_call | solution.py:227
  2.4 2.6 %collective-permute-start.1 = (f32[21,16,384]{2,1,0:T(8,128)}, f32[21,16,384]{2,1,0:T(8,128)S(1)}, u32[]{:S(2)}, u32[]{:S(2)}) collective-permute-start(f32[21,16,384]{2,1,0:T(8,128)} %pack_bricks.1), channel_id=1, source_target_pairs={{0,4},{4,0},{8,12},{12,8},{16,20},{20,16},{24,28},{28,24},{1,5},{5... | collective-permute-start | bytes 1548296 | tf_op jit(solution)/shard_map/ppermute | solution.py:670
  5.0 0.0 copy-done.5
  5.0 0.1 reshape.6.filter_ref
  5.0 0.0 copy-start
  5.0 0.0 collective-permute-done.after_ref.core_ref
  5.1 0.0 copy-done.3
  5.1 0.0 copy-done.4
  5.1 0.8 %circulant_band.1 = (bf16[256,2560]{1,0:T(8,128)(2,1)S(1)}, bf16[256,2560]{1,0:T(8,128)(2,1)S(1)}) custom-call(f32[32,32]{1,0:T(8,128)S(1)} %reshape.6.filter_ref, f32[64,128]{1,0:T(8,128)S(1)} %copy-done.4, f32[64,2048]{1,0:T(8,128)S(1)} %copy-done.3, f32[5,4,32,512]{3,2,1,0:T(8,128)S(1)} %collective-permute-done.after_ref.core_ref), custom_call_target="tpu_custom_call" | custom-call | flops 1000000000 | bytes 3000000 | tf_op jit(solution)/shard_map/circulant_band/pallas_call | solution.py:550
  5.9 0.5 copy-done
  6.4 0.0 copy-start.2
  6.4 3.4 %span_away.1 = (f32[5,4,32,512]{3,2,1,0:T(8,128)S(1)}, bf16[640,1024]{1,0:T(8,128)(2,1)S(1)}, bf16[640,1024]{1,0:T(8,128)(2,1)S(1)}) custom-call(bf16[256,2560]{1,0:T(8,128)(2,1)S(1)} %get-tuple-element.10.high_ref, bf16[256,2560]{1,0:T(8,128)(2,1)S(1)} %get-tuple-element.11.low_ref, f32[5,4,32,512]{3,2,1,0:T(8,128)S(1)} %copy-done, ...), custom_call_target="tpu_custom_call" | custom-call | flops 3000000000 | bytes 9000000 | tf_op jit(solution)/shard_map/span_away/pallas_call | solution.py:611
  9.8 1.6 %collective-permute-start.7 = (f32[5,4,32,512]{3,2,1,0:T(8,128)S(1)}, f32[5,4,32,512]{3,2,1,0:T(8,128)S(1)}, u32[]{:S(2)}, u32[]{:S(2)}) collective-permute-start(f32[5,4,32,512]{3,2,1,0:T(8,128)S(1)} %get-tuple-element.14), channel_id=1, source_target_pairs={{0,2},{1,3},{2,0},{3,1},{4,6},{5,7},{6,4},{7,5},{8,10},{9,11},{10,... | collective-permute-start | bytes 3932168 | tf_op jit(solution)/shard_map/ppermute | solution.py:651
  11.4 0.0 copy-done.2
  11.4 0.0 copy-start.1
  11.4 2.9 %wall_faces.2.after_ref.first_ref = f32[5,2,32,512]{3,2,1,0:T(8,128)S(1)} custom-call(f32[5,4,32,512]{3,2,1,0:T(8,128)S(1)} %copy-done, s32[4,32,512]{2,1,0:T(8,128)S(1)} %copy-done.2, bf16[640,1024]{1,0:T(8,128)(2,1)S(1)} %get-tuple-element.12.after_ref.xh), custom_call_target="tpu_custom_call" | custom-call | flops 2500000000 | bytes 7500000 | tf_op jit(solution)/shard_map/wall_faces/pallas_call | solution.py:190
  14.3 0.0 copy-done.1
  14.3 0.7 %collective-permute-start.2 = (f32[21,16,256]{2,1,0:T(8,128)S(1)}, f32[21,16,256]{2,1,0:T(8,128)S(1)}, u32[]{:S(2)}, u32[]{:S(2)}) collective-permute-start(f32[21,16,256]{2,1,0:T(8,128)S(1)} %bring_planes.3.after_ref), channel_id=1, source_target_pairs={{0,4},{4,0},{8,12},{12,8},{16,20},{20,16},{24,28},{28,24},{1,5},{5... | collective-permute-start | bytes 1032200 | tf_op jit(solution)/shard_map/ppermute | solution.py:681
  15.1 2.7 %collective-permute-done.1.pair_ref.refs_1_ = f32[21,16,384]{2,1,0:T(8,128)S(1)} collective-permute-done((f32[21,16,384]{2,1,0:T(8,128)}, f32[21,16,384]{2,1,0:T(8,128)S(1)}, u32[]{:S(2)}, u32[]{:S(2)}) %collective-permute-start.1) | collective-permute-done | bytes 516128 | tf_op jit(solution)/shard_map/ppermute | solution.py:670
  17.8 4.0 %collective-permute-start.4 = (f32[16,16,384]{2,1,0:T(8,128)S(1)}, f32[16,16,384]{2,1,0:T(8,128)S(1)}, u32[]{:S(2)}, u32[]{:S(2)}) collective-permute-start(f32[16,16,384]{2,1,0:T(8,128)S(1)} %pass_planes.4.after_ref), channel_id=1, source_target_pairs={{0,8},{8,16},{16,24},{12,4},{20,12},{28,20},{1,9},{9,17},{17,25},{... | collective-permute-start | bytes 1179656 | tf_op jit(solution)/shard_map/ppermute | solution.py:686
  21.8 2.9 %wall_faces.3.after_ref.second_ref = f32[5,2,32,512]{3,2,1,0:T(8,128)S(1)} custom-call(f32[5,4,32,512]{3,2,1,0:T(8,128)S(1)} %copy-done, s32[4,32,512]{2,1,0:T(8,128)S(1)} %copy-done.2, f32[16,16,384]{2,1,0:T(8,128)S(1)} %pass_planes.4.after_ref), custom_call_target="tpu_custom_call" | custom-call | flops 2500000000 | bytes 7500000 | tf_op jit(solution)/shard_map/wall_faces/pallas_call | solution.py:190
  24.7 0.1 collective-permute-start.5
  24.8 0.1 collective-permute-done.2.pair_ref.refs_1_
  25.0 3.7 %collective-permute-start.8 = (f32[16,16,256]{2,1,0:T(8,128)S(1)}, f32[16,16,256]{2,1,0:T(8,128)S(1)}, u32[]{:S(2)}, u32[]{:S(2)}) collective-permute-start(f32[16,16,256]{2,1,0:T(8,128)S(1)} %pass_planes.5.after_ref), channel_id=1, source_target_pairs={{0,8},{8,16},{16,24},{12,4},{20,12},{28,20},{1,9},{9,17},{17,25},{... | collective-permute-start | bytes 786440 | tf_op jit(solution)/shard_map/ppermute | solution.py:686
  28.7 2.2 %span_home.1.after_ref.refs_4_ = f32[5,4,32,512]{3,2,1,0:T(8,128)S(1)} custom-call(bf16[256,2560]{1,0:T(8,128)(2,1)S(1)} %get-tuple-element.10.high_ref, bf16[256,2560]{1,0:T(8,128)(2,1)S(1)} %get-tuple-element.11.low_ref, bf16[640,1024]{1,0:T(8,128)(2,1)S(1)} %get-tuple-element.12.after_ref.xh, bf16[640,1024]{1,0:T(8,128)(2,1)S(1)} %get-tuple-element.13.xl, ...), custom_call_target="tpu_custom_call" | custom-call | flops 2000000000 | bytes 6000000 | tf_op jit(solution)/shard_map/span_home/pallas_call | solution.py:633
  31.0 0.1 collective-permute-start.3
  31.1 3.4 %collective-permute-done.5.pair_ref.refs_1_ = f32[21,32,128]{2,1,0:T(8,128)S(1)} collective-permute-done((f32[21,32,128]{2,1,0:T(8,128)S(1)}, f32[21,32,128]{2,1,0:T(8,128)S(1)}, u32[]{:S(2)}, u32[]{:S(2)}) %collective-permute-start.5) | collective-permute-done | bytes 344096 | tf_op jit(solution)/shard_map/ppermute | solution.py:681
  34.5 3.5 %collective-permute-start.9 = (f32[16,32,128]{2,1,0:T(8,128)S(1)}, f32[16,32,128]{2,1,0:T(8,128)S(1)}, u32[]{:S(2)}, u32[]{:S(2)}) collective-permute-start(f32[16,32,128]{2,1,0:T(8,128)S(1)} %pass_planes.6.refs_5_), channel_id=1, source_target_pairs={{0,8},{8,16},{16,24},{12,4},{20,12},{28,20},{1,9},{9,17},{17,25},{... | collective-permute-start | bytes 786440 | tf_op jit(solution)/shard_map/ppermute | solution.py:686
  38.0 0.0 collective-permute-done.4.refs_2_
  38.0 2.7 %stream_faces.4.after_ref.refs_6_ = f32[5,4,16,384]{3,2,1,0:T(8,128)S(1)} custom-call(f32[5,4,32,512]{3,2,1,0:T(8,128)S(1)} %copy-done, f32[21,16,384]{2,1,0:T(8,128)S(1)} %collective-permute-done.1.pair_ref.refs_1_, f32[16,16,384]{2,1,0:T(8,128)S(1)} %collective-permute-done.4.refs_2_, s32[4,32,512]{2,1,0:T(8,128)S(1)} %copy-done.1, ...), custom_call_target="tpu_custom_call" | custom-call | flops 1800000000 | bytes 5399999 | tf_op jit(solution)/shard_map/stream_faces/pallas_call | solution.py:473
  40.7 0.0 collective-permute-done.3.pair_ref.refs_1_
  40.8 3.5 %collective-permute-start.6 = (f32[16,16,128]{2,1,0:T(8,128)S(1)}, f32[16,16,128]{2,1,0:T(8,128)S(1)}, u32[]{:S(2)}, u32[]{:S(2)}) collective-permute-start(f32[16,16,128]{2,1,0:T(8,128)S(1)} %pass_planes.7.refs_5_), channel_id=1, source_target_pairs={{0,8},{8,16},{16,24},{12,4},{20,12},{28,20},{1,9},{9,17},{17,25},{... | collective-permute-start | bytes 393224 | tf_op jit(solution)/shard_map/ppermute | solution.py:686
  44.3 0.0 collective-permute-done.8.refs_2_
  44.3 1.8 %stream_faces.5.refs_5_.refs_7_ = f32[5,4,16,256]{3,2,1,0:T(8,128)S(1)} custom-call(f32[5,4,32,512]{3,2,1,0:T(8,128)S(1)} %copy-done, f32[21,16,256]{2,1,0:T(8,128)S(1)} %collective-permute-done.2.pair_ref.refs_1_, f32[16,16,256]{2,1,0:T(8,128)S(1)} %collective-permute-done.8.refs_2_, s32[4,32,512]{2,1,0:T(8,128)S(1)} %copy-done.1, ...), custom_call_target="tpu_custom_call" | custom-call | flops 1200000000 | bytes 3600000 | tf_op jit(solution)/shard_map/stream_faces/pallas_call | solution.py:473
  46.1 0.0 collective-permute-done.9.refs_2_
  46.1 1.8 %stream_faces.6.refs_8_ = f32[5,4,32,128]{3,2,1,0:T(8,128)S(1)} custom-call(f32[5,4,32,512]{3,2,1,0:T(8,128)S(1)} %copy-done, f32[21,32,128]{2,1,0:T(8,128)S(1)} %collective-permute-done.5.pair_ref.refs_1_, f32[16,32,128]{2,1,0:T(8,128)S(1)} %collective-permute-done.9.refs_2_, s32[4,32,512]{2,1,0:T(8,128)S(1)} %copy-done.1, ...), custom_call_target="tpu_custom_call" | custom-call | flops 1200000000 | bytes 3600000 | tf_op jit(solution)/shard_map/stream_faces/pallas_call | solution.py:473
  47.9 0.0 collective-permute-done.6.refs_2_
  47.9 0.0 collective-permute-done.7.refs_5_
  47.9 2.4 %stream_faces.7 = f32[5,4,32,512]{3,2,1,0:T(8,128)} custom-call(f32[5,4,32,512]{3,2,1,0:T(8,128)S(1)} %copy-done, f32[21,16,128]{2,1,0:T(8,128)S(1)} %collective-permute-done.3.pair_ref.refs_1_, f32[16,16,128]{2,1,0:T(8,128)S(1)} %collective-permute-done.6.refs_2_, s32[4,32,512]{2,1,0:T(8,128)S(1)} %copy-done.1, ...), custom_call_target="tpu_custom_call" | custom-call | flops 600000000 | bytes 1800000 | tf_op jit(solution)/shard_map/stream_faces/pallas_call | solution.py:473
  (7 shorter events, 0.2 us)
Async XLA Ops:
  0.0 5.0 %collective-permute-start = (f32[5,4,32,512]{3,2,1,0:T(8,128)}, f32[5,4,32,512]{3,2,1,0:T(8,128)S(1)}, u32[]{:S(2)}, u32[]{:S(2)}) collective-permute-start(f32[5,4,32,512]{3,2,1,0:T(8,128)} %refs_0_.7), channel_id=1, source_target_pairs={{0,1},{1,0},{2,3},{3,2},{4,5},{5,4},{6,7},{7,6},{8,9},{9,8},{10,11... | collective-permute-start | bytes 3932168 | tf_op jit(solution)/shard_map/ppermute | solution.py:651
  0.5 4.5 %copy-start.5 = (f32[1024]{0:T(1024)S(1)}, f32[1024]{0:T(1024)}, u32[]{:S(2)}) copy-start(f32[1024]{0:T(1024)} %param.9) | copy-start | bytes 12292
  0.5 4.6 %copy-start.3 = (f32[64,2048]{1,0:T(8,128)S(1)}, f32[64,2048]{1,0:T(8,128)}, u32[]{:S(2)}) copy-start(f32[64,2048]{1,0:T(8,128)} %constant.5.clone.outer_ref) | copy-start | bytes 1572868
  0.5 4.6 %copy-start.4 = (f32[64,128]{1,0:T(8,128)S(1)}, f32[64,128]{1,0:T(8,128)}, u32[]{:S(2)}) copy-start(f32[64,128]{1,0:T(8,128)} %constant.4.clone.inner_ref) | copy-start | bytes 98308
  2.4 15.4 %collective-permute-start.1 = (f32[21,16,384]{2,1,0:T(8,128)}, f32[21,16,384]{2,1,0:T(8,128)S(1)}, u32[]{:S(2)}, u32[]{:S(2)}) collective-permute-start(f32[21,16,384]{2,1,0:T(8,128)} %pack_bricks.1), channel_id=1, source_target_pairs={{0,4},{4,0},{8,12},{12,8},{16,20},{20,16},{24,28},{28,24},{1,5},{5... | collective-permute-start | bytes 1548296 | tf_op jit(solution)/shard_map/ppermute | solution.py:670
  5.0 1.3 %copy-start = (f32[5,4,32,512]{3,2,1,0:T(8,128)S(1)}, f32[5,4,32,512]{3,2,1,0:T(8,128)}, u32[]{:S(2)}) copy-start(f32[5,4,32,512]{3,2,1,0:T(8,128)} %refs_0_.7) | copy-start | bytes 3932164
  6.4 5.0 %copy-start.2 = (s32[4,32,512]{2,1,0:T(8,128)S(1)}, s32[4,32,512]{2,1,0:T(8,128)}, u32[]{:S(2)}) copy-start(s32[4,32,512]{2,1,0:T(8,128)} %mask_ref.9) | copy-start | bytes 786436
  9.8 38.2 %collective-permute-start.7 = (f32[5,4,32,512]{3,2,1,0:T(8,128)S(1)}, f32[5,4,32,512]{3,2,1,0:T(8,128)S(1)}, u32[]{:S(2)}, u32[]{:S(2)}) collective-permute-start(f32[5,4,32,512]{3,2,1,0:T(8,128)S(1)} %get-tuple-element.14), channel_id=1, source_target_pairs={{0,2},{1,3},{2,0},{3,1},{4,6},{5,7},{6,4},{7,5},{8,10},{9,11},{10,... | collective-permute-start | bytes 3932168 | tf_op jit(solution)/shard_map/ppermute | solution.py:651
  11.4 2.9 %copy-start.1 = (s32[4,32,512]{2,1,0:T(8,128)S(1)}, s32[4,32,512]{2,1,0:T(8,128)}, u32[]{:S(2)}) copy-start(s32[4,32,512]{2,1,0:T(8,128)} %refs_3_.7) | copy-start | bytes 786436
  14.3 10.6 %collective-permute-start.2 = (f32[21,16,256]{2,1,0:T(8,128)S(1)}, f32[21,16,256]{2,1,0:T(8,128)S(1)}, u32[]{:S(2)}, u32[]{:S(2)}) collective-permute-start(f32[21,16,256]{2,1,0:T(8,128)S(1)} %bring_planes.3.after_ref), channel_id=1, source_target_pairs={{0,4},{4,0},{8,12},{12,8},{16,20},{20,16},{24,28},{28,24},{1,5},{5... | collective-permute-start | bytes 1032200 | tf_op jit(solution)/shard_map/ppermute | solution.py:681
  17.8 20.2 %collective-permute-start.4 = (f32[16,16,384]{2,1,0:T(8,128)S(1)}, f32[16,16,384]{2,1,0:T(8,128)S(1)}, u32[]{:S(2)}, u32[]{:S(2)}) collective-permute-start(f32[16,16,384]{2,1,0:T(8,128)S(1)} %pass_planes.4.after_ref), channel_id=1, source_target_pairs={{0,8},{8,16},{16,24},{12,4},{20,12},{28,20},{1,9},{9,17},{17,25},{... | collective-permute-start | bytes 1179656 | tf_op jit(solution)/shard_map/ppermute | solution.py:686
  24.7 9.7 %collective-permute-start.5 = (f32[21,32,128]{2,1,0:T(8,128)S(1)}, f32[21,32,128]{2,1,0:T(8,128)S(1)}, u32[]{:S(2)}, u32[]{:S(2)}) collective-permute-start(f32[21,32,128]{2,1,0:T(8,128)S(1)} %bring_planes.4.after_ref), channel_id=1, source_target_pairs={{0,4},{4,0},{8,12},{12,8},{16,20},{20,16},{24,28},{28,24},{1,5},{5... | collective-permute-start | bytes 1032200 | tf_op jit(solution)/shard_map/ppermute | solution.py:681
  25.0 19.3 %collective-permute-start.8 = (f32[16,16,256]{2,1,0:T(8,128)S(1)}, f32[16,16,256]{2,1,0:T(8,128)S(1)}, u32[]{:S(2)}, u32[]{:S(2)}) collective-permute-start(f32[16,16,256]{2,1,0:T(8,128)S(1)} %pass_planes.5.after_ref), channel_id=1, source_target_pairs={{0,8},{8,16},{16,24},{12,4},{20,12},{28,20},{1,9},{9,17},{17,25},{... | collective-permute-start | bytes 786440 | tf_op jit(solution)/shard_map/ppermute | solution.py:686
  31.0 9.8 %collective-permute-start.3 = (f32[21,16,128]{2,1,0:T(8,128)S(1)}, f32[21,16,128]{2,1,0:T(8,128)S(1)}, u32[]{:S(2)}, u32[]{:S(2)}) collective-permute-start(f32[21,16,128]{2,1,0:T(8,128)S(1)} %bring_planes.5.after_ref), channel_id=1, source_target_pairs={{0,4},{4,0},{8,12},{12,8},{16,20},{20,16},{24,28},{28,24},{1,5},{5... | collective-permute-start | bytes 516104 | tf_op jit(solution)/shard_map/ppermute | solution.py:681
  34.5 11.6 %collective-permute-start.9 = (f32[16,32,128]{2,1,0:T(8,128)S(1)}, f32[16,32,128]{2,1,0:T(8,128)S(1)}, u32[]{:S(2)}, u32[]{:S(2)}) collective-permute-start(f32[16,32,128]{2,1,0:T(8,128)S(1)} %pass_planes.6.refs_5_), channel_id=1, source_target_pairs={{0,8},{8,16},{16,24},{12,4},{20,12},{28,20},{1,9},{9,17},{17,25},{... | collective-permute-start | bytes 786440 | tf_op jit(solution)/shard_map/ppermute | solution.py:686
  40.8 7.1 %collective-permute-start.6 = (f32[16,16,128]{2,1,0:T(8,128)S(1)}, f32[16,16,128]{2,1,0:T(8,128)S(1)}, u32[]{:S(2)}, u32[]{:S(2)}) collective-permute-start(f32[16,16,128]{2,1,0:T(8,128)S(1)} %pass_planes.7.refs_5_), channel_id=1, source_target_pairs={{0,8},{8,16},{16,24},{12,4},{20,12},{28,20},{1,9},{9,17},{17,25},{... | collective-permute-start | bytes 393224 | tf_op jit(solution)/shard_map/ppermute | solution.py:686

commit v5 on v4

--- a/solution.py
+++ b/solution.py
@@ -696,8 +696,9 @@
     acc_high = wall_part(state, mask_y, half, depth - half, after)
     after = hand_on(1, exchange(2, acc_high))
     base = home_part(band, lines, acc_low, acc_high, after)
-    after = hand_on(2, exchange(3, base))
-    after = hand_on(3, stream(0, after))
+    after = exchange(3, base)
+    after = hand_on(2, stream(0, after))
+    after = hand_on(3, after)
     stream(2, stream(1, after))
     return stream_part(
         state, pairs[3], fars[3], mask_x, parts[3], base, arrived=arrived, others=others

time: 50.6 us -> 48.3 us (0.955)
  waiting for transfers between devices: 6.3 us -> 4.1 us
    ppermute x3, waiting for transfers between devices: 3.57 us -> 0.82 us  [exchange(): pairs.append(lax.ppermute(brick, 'gx', swap))]
    ppermute x4, waiting for transfers between devices: 0.01 us -> 0.55 us  [hand_on(): fars.append(lax.ppermute(planes, 'gx', carry))]
  transfers between devices with their start and end apart: 10 -> 10, of which waited for: 3 -> 4; matrix products, arithmetic and copies ran while one was open for 0% -> 0% of each run, Pallas kernels for 41% -> 43%
where the time goes in v5:
time: 48.3 us; the launch traced here: 48.1 us
  Pallas kernels  23.1 us (48%)
  starting transfers between devices  20.1 us (42%)
  waiting for transfers between devices  4.1 us (8%)
  local copies, waits for them, and re-layouts  0.59 us (1%)
    ppermute x4, starting transfers between devices, hand_on(): fars.append(lax.ppermute(planes, 'gx', carry))  14.7 us
    pallas_call x4, Pallas kernels, stream_part(): call(functools.partial(stream_kernel, part, places), 'stream_faces', 0.3...  8.72 us
    pallas_call x2, Pallas kernels, wall_part(): call(kernel, 'wall_faces', 5.0 * count / depth, [PLACE, PLACE, ANYWHERE],...  5.82 us
    pallas_call x1, Pallas kernels, away_part(): call(functools.partial(away_kernel, masks), 'span_away', 3.0, [PLACE] * 4...  3.41 us
    ppermute x1, waiting for transfers between devices, per_device(): pairs = [lax.ppermute(brick, 'gx', swap)]  2.72 us
    ppermute x1, starting transfers between devices, per_device(): pairs = [lax.ppermute(brick, 'gx', swap)]  2.57 us
    pallas_call x1, Pallas kernels, home_part(): call(home_kernel, 'span_home', 2.0, [PLACE] * 6 + [ANYWHERE], PLACE, shap...  2.2 us
    ppermute x2, starting transfers between devices, flip(): return lax.ppermute(array, 'gz', [(g, g ^ bit) for g in range(groups)])  2.04 us
  transfers between devices with their start and end apart: 10, of which 4 were waited for; matrix products, arithmetic and copies ran while one was open for 0% of the time, Pallas kernels for 43%

profile of v5, /device:TPU:0, one launch (start us, length us, event | category | flops | bytes accessed | tf_op | source)
XLA Modules:
  0.0 48.1 jit_solution(6440696624688557771)
XLA Ops:
  0.0 0.5 collective-permute-start
  0.5 0.0 copy-start.5
  0.5 0.0 copy-start.3
  0.5 0.0 copy-start.4
  0.5 1.9 %pack_bricks.1 = f32[21,16,384]{2,1,0:T(8,128)} custom-call(f32[20,32,512]{2,1,0:T(8,128)} %bitcast.1, s32[4,32,512]{2,1,0:T(8,128)} %refs_3_.7), custom_call_target="tpu_custom_call" | custom-call | flops 1000000000 | bytes 3000000 | tf_op jit(solution)/shard_map/pack_bricks/pallas_call | solution.py:227
  2.4 2.6 %collective-permute-start.1 = (f32[21,16,384]{2,1,0:T(8,128)}, f32[21,16,384]{2,1,0:T(8,128)S(1)}, u32[]{:S(2)}, u32[]{:S(2)}) collective-permute-start(f32[21,16,384]{2,1,0:T(8,128)} %pack_bricks.1), channel_id=1, source_target_pairs={{0,4},{4,0},{8,12},{12,8},{16,20},{20,16},{24,28},{28,24},{1,5},{5... | collective-permute-start | bytes 1548296 | tf_op jit(solution)/shard_map/ppermute | solution.py:670
  5.0 0.0 copy-done.5
  5.0 0.1 reshape.6.filter_ref
  5.0 0.0 copy-start
  5.0 0.0 collective-permute-done.after_ref.core_ref
  5.1 0.0 copy-done.3
  5.1 0.0 copy-done.4
  5.1 0.8 %circulant_band.1 = (bf16[256,2560]{1,0:T(8,128)(2,1)S(1)}, bf16[256,2560]{1,0:T(8,128)(2,1)S(1)}) custom-call(f32[32,32]{1,0:T(8,128)S(1)} %reshape.6.filter_ref, f32[64,128]{1,0:T(8,128)S(1)} %copy-done.4, f32[64,2048]{1,0:T(8,128)S(1)} %copy-done.3, f32[5,4,32,512]{3,2,1,0:T(8,128)S(1)} %collective-permute-done.after_ref.core_ref), custom_call_target="tpu_custom_call" | custom-call | flops 1000000000 | bytes 3000000 | tf_op jit(solution)/shard_map/circulant_band/pallas_call | solution.py:550
  5.9 0.5 %copy-done = f32[5,4,32,512]{3,2,1,0:T(8,128)S(1)} copy-done((f32[5,4,32,512]{3,2,1,0:T(8,128)S(1)}, f32[5,4,32,512]{3,2,1,0:T(8,128)}, u32[]{:S(2)}) %copy-start) | copy-done | bytes 1310744
  6.4 0.0 copy-start.2
  6.4 3.4 %span_away.1 = (f32[5,4,32,512]{3,2,1,0:T(8,128)S(1)}, bf16[640,1024]{1,0:T(8,128)(2,1)S(1)}, bf16[640,1024]{1,0:T(8,128)(2,1)S(1)}) custom-call(bf16[256,2560]{1,0:T(8,128)(2,1)S(1)} %get-tuple-element.10.high_ref, bf16[256,2560]{1,0:T(8,128)(2,1)S(1)} %get-tuple-element.11.low_ref, f32[5,4,32,512]{3,2,1,0:T(8,128)S(1)} %copy-done, ...), custom_call_target="tpu_custom_call" | custom-call | flops 3000000000 | bytes 9000000 | tf_op jit(solution)/shard_map/span_away/pallas_call | solution.py:611
  9.8 1.6 %collective-permute-start.7 = (f32[5,4,32,512]{3,2,1,0:T(8,128)S(1)}, f32[5,4,32,512]{3,2,1,0:T(8,128)S(1)}, u32[]{:S(2)}, u32[]{:S(2)}) collective-permute-start(f32[5,4,32,512]{3,2,1,0:T(8,128)S(1)} %get-tuple-element.14), channel_id=1, source_target_pairs={{0,2},{1,3},{2,0},{3,1},{4,6},{5,7},{6,4},{7,5},{8,10},{9,11},{10,... | collective-permute-start | bytes 3932168 | tf_op jit(solution)/shard_map/ppermute | solution.py:651
  11.4 0.0 copy-done.2
  11.4 0.0 copy-start.1
  11.4 2.9 %wall_faces.2.after_ref.first_ref = f32[5,2,32,512]{3,2,1,0:T(8,128)S(1)} custom-call(f32[5,4,32,512]{3,2,1,0:T(8,128)S(1)} %copy-done, s32[4,32,512]{2,1,0:T(8,128)S(1)} %copy-done.2, bf16[640,1024]{1,0:T(8,128)(2,1)S(1)} %get-tuple-element.12.after_ref.xh), custom_call_target="tpu_custom_call" | custom-call | flops 2500000000 | bytes 7500000 | tf_op jit(solution)/shard_map/wall_faces/pallas_call | solution.py:190
  14.3 0.0 copy-done.1
  14.3 0.7 %collective-permute-start.2 = (f32[21,16,256]{2,1,0:T(8,128)S(1)}, f32[21,16,256]{2,1,0:T(8,128)S(1)}, u32[]{:S(2)}, u32[]{:S(2)}) collective-permute-start(f32[21,16,256]{2,1,0:T(8,128)S(1)} %bring_planes.3.after_ref), channel_id=1, source_target_pairs={{0,4},{4,0},{8,12},{12,8},{16,20},{20,16},{24,28},{28,24},{1,5},{5... | collective-permute-start | bytes 1032200 | tf_op jit(solution)/shard_map/ppermute | solution.py:681
  15.1 2.7 %collective-permute-done.1.pair_ref.refs_1_ = f32[21,16,384]{2,1,0:T(8,128)S(1)} collective-permute-done((f32[21,16,384]{2,1,0:T(8,128)}, f32[21,16,384]{2,1,0:T(8,128)S(1)}, u32[]{:S(2)}, u32[]{:S(2)}) %collective-permute-start.1) | collective-permute-done | bytes 516128 | tf_op jit(solution)/shard_map/ppermute | solution.py:670
  17.8 4.0 %collective-permute-start.5 = (f32[16,16,384]{2,1,0:T(8,128)S(1)}, f32[16,16,384]{2,1,0:T(8,128)S(1)}, u32[]{:S(2)}, u32[]{:S(2)}) collective-permute-start(f32[16,16,384]{2,1,0:T(8,128)S(1)} %pass_planes.4.after_ref), channel_id=1, source_target_pairs={{0,8},{8,16},{16,24},{12,4},{20,12},{28,20},{1,9},{9,17},{17,25},{... | collective-permute-start | bytes 1179656 | tf_op jit(solution)/shard_map/ppermute | solution.py:686
  21.8 2.9 %wall_faces.3.after_ref.second_ref = f32[5,2,32,512]{3,2,1,0:T(8,128)S(1)} custom-call(f32[5,4,32,512]{3,2,1,0:T(8,128)S(1)} %copy-done, s32[4,32,512]{2,1,0:T(8,128)S(1)} %copy-done.2, f32[16,16,384]{2,1,0:T(8,128)S(1)} %pass_planes.4.after_ref), custom_call_target="tpu_custom_call" | custom-call | flops 2500000000 | bytes 7500000 | tf_op jit(solution)/shard_map/wall_faces/pallas_call | solution.py:190
  24.7 0.1 collective-permute-start.4
  24.8 0.1 collective-permute-done.2.pair_ref.refs_1_
  25.0 3.7 %collective-permute-start.8 = (f32[16,16,256]{2,1,0:T(8,128)S(1)}, f32[16,16,256]{2,1,0:T(8,128)S(1)}, u32[]{:S(2)}, u32[]{:S(2)}) collective-permute-start(f32[16,16,256]{2,1,0:T(8,128)S(1)} %pass_planes.5.after_ref), channel_id=1, source_target_pairs={{0,8},{8,16},{16,24},{12,4},{20,12},{28,20},{1,9},{9,17},{17,25},{... | collective-permute-start | bytes 786440 | tf_op jit(solution)/shard_map/ppermute | solution.py:686
  28.7 2.2 %span_home.1.after_ref.refs_4_ = f32[5,4,32,512]{3,2,1,0:T(8,128)S(1)} custom-call(bf16[256,2560]{1,0:T(8,128)(2,1)S(1)} %get-tuple-element.10.high_ref, bf16[256,2560]{1,0:T(8,128)(2,1)S(1)} %get-tuple-element.11.low_ref, bf16[640,1024]{1,0:T(8,128)(2,1)S(1)} %get-tuple-element.12.after_ref.xh, bf16[640,1024]{1,0:T(8,128)(2,1)S(1)} %get-tuple-element.13.xl, ...), custom_call_target="tpu_custom_call" | custom-call | flops 2000000000 | bytes 6000000 | tf_op jit(solution)/shard_map/span_home/pallas_call | solution.py:633
  31.0 0.1 collective-permute-start.3
  31.1 0.0 collective-permute-done.5.refs_2_
  31.1 2.7 %stream_faces.4.after_ref.refs_6_ = f32[5,4,16,384]{3,2,1,0:T(8,128)S(1)} custom-call(f32[5,4,32,512]{3,2,1,0:T(8,128)S(1)} %copy-done, f32[21,16,384]{2,1,0:T(8,128)S(1)} %collective-permute-done.1.pair_ref.refs_1_, f32[16,16,384]{2,1,0:T(8,128)S(1)} %collective-permute-done.5.refs_2_, s32[4,32,512]{2,1,0:T(8,128)S(1)} %copy-done.1, ...), custom_call_target="tpu_custom_call" | custom-call | flops 1800000000 | bytes 5399999 | tf_op jit(solution)/shard_map/stream_faces/pallas_call | solution.py:473
  33.8 0.7 %collective-permute-done.4.pair_ref.refs_1_ = f32[21,32,128]{2,1,0:T(8,128)S(1)} collective-permute-done((f32[21,32,128]{2,1,0:T(8,128)S(1)}, f32[21,32,128]{2,1,0:T(8,128)S(1)}, u32[]{:S(2)}, u32[]{:S(2)}) %collective-permute-start.4) | collective-permute-done | bytes 344096 | tf_op jit(solution)/shard_map/ppermute | solution.py:681
  34.5 3.5 %collective-permute-start.9 = (f32[16,32,128]{2,1,0:T(8,128)S(1)}, f32[16,32,128]{2,1,0:T(8,128)S(1)}, u32[]{:S(2)}, u32[]{:S(2)}) collective-permute-start(f32[16,32,128]{2,1,0:T(8,128)S(1)} %pass_planes.6.after_ref), channel_id=1, source_target_pairs={{0,8},{8,16},{16,24},{12,4},{20,12},{28,20},{1,9},{9,17},{17,25},{... | collective-permute-start | bytes 786440 | tf_op jit(solution)/shard_map/ppermute | solution.py:686
  38.0 0.0 collective-permute-done.3.pair_ref.refs_1_
  38.0 3.5 %collective-permute-start.6 = (f32[16,16,128]{2,1,0:T(8,128)S(1)}, f32[16,16,128]{2,1,0:T(8,128)S(1)}, u32[]{:S(2)}, u32[]{:S(2)}) collective-permute-start(f32[16,16,128]{2,1,0:T(8,128)S(1)} %pass_planes.7.refs_5_), channel_id=1, source_target_pairs={{0,8},{8,16},{16,24},{12,4},{20,12},{28,20},{1,9},{9,17},{17,25},{... | collective-permute-start | bytes 393224 | tf_op jit(solution)/shard_map/ppermute | solution.py:686
  41.5 0.0 collective-permute-done.8.refs_2_
  41.5 1.8 %stream_faces.5.refs_5_.refs_7_ = f32[5,4,16,256]{3,2,1,0:T(8,128)S(1)} custom-call(f32[5,4,32,512]{3,2,1,0:T(8,128)S(1)} %copy-done, f32[21,16,256]{2,1,0:T(8,128)S(1)} %collective-permute-done.2.pair_ref.refs_1_, f32[16,16,256]{2,1,0:T(8,128)S(1)} %collective-permute-done.8.refs_2_, s32[4,32,512]{2,1,0:T(8,128)S(1)} %copy-done.1, ...), custom_call_target="tpu_custom_call" | custom-call | flops 1200000000 | bytes 3600000 | tf_op jit(solution)/shard_map/stream_faces/pallas_call | solution.py:473
  43.4 0.5 %collective-permute-done.9.refs_2_ = f32[16,32,128]{2,1,0:T(8,128)S(1)} collective-permute-done((f32[16,32,128]{2,1,0:T(8,128)S(1)}, f32[16,32,128]{2,1,0:T(8,128)S(1)}, u32[]{:S(2)}, u32[]{:S(2)}) %collective-permute-start.9) | collective-permute-done | bytes 262176 | tf_op jit(solution)/shard_map/ppermute | solution.py:686
  43.9 1.8 %stream_faces.6.refs_8_ = f32[5,4,32,128]{3,2,1,0:T(8,128)S(1)} custom-call(f32[5,4,32,512]{3,2,1,0:T(8,128)S(1)} %copy-done, f32[21,32,128]{2,1,0:T(8,128)S(1)} %collective-permute-done.4.pair_ref.refs_1_, f32[16,32,128]{2,1,0:T(8,128)S(1)} %collective-permute-done.9.refs_2_, s32[4,32,512]{2,1,0:T(8,128)S(1)} %copy-done.1, ...), custom_call_target="tpu_custom_call" | custom-call | flops 1200000000 | bytes 3600000 | tf_op jit(solution)/shard_map/stream_faces/pallas_call | solution.py:473
  45.7 0.0 collective-permute-done.6.refs_2_
  45.7 0.0 collective-permute-done.7.refs_5_
  45.7 2.4 %stream_faces.7 = f32[5,4,32,512]{3,2,1,0:T(8,128)} custom-call(f32[5,4,32,512]{3,2,1,0:T(8,128)S(1)} %copy-done, f32[21,16,128]{2,1,0:T(8,128)S(1)} %collective-permute-done.3.pair_ref.refs_1_, f32[16,16,128]{2,1,0:T(8,128)S(1)} %collective-permute-done.6.refs_2_, s32[4,32,512]{2,1,0:T(8,128)S(1)} %copy-done.1, ...), custom_call_target="tpu_custom_call" | custom-call | flops 600000000 | bytes 1800000 | tf_op jit(solution)/shard_map/stream_faces/pallas_call | solution.py:473
  (7 shorter events, 0.2 us)
Async XLA Ops:
  0.0 5.0 %collective-permute-start = (f32[5,4,32,512]{3,2,1,0:T(8,128)}, f32[5,4,32,512]{3,2,1,0:T(8,128)S(1)}, u32[]{:S(2)}, u32[]{:S(2)}) collective-permute-start(f32[5,4,32,512]{3,2,1,0:T(8,128)} %refs_0_.7), channel_id=1, source_target_pairs={{0,1},{1,0},{2,3},{3,2},{4,5},{5,4},{6,7},{7,6},{8,9},{9,8},{10,11... | collective-permute-start | bytes 3932168 | tf_op jit(solution)/shard_map/ppermute | solution.py:651
  0.5 4.5 %copy-start.5 = (f32[1024]{0:T(1024)S(1)}, f32[1024]{0:T(1024)}, u32[]{:S(2)}) copy-start(f32[1024]{0:T(1024)} %param.9) | copy-start | bytes 12292
  0.5 4.6 %copy-start.3 = (f32[64,2048]{1,0:T(8,128)S(1)}, f32[64,2048]{1,0:T(8,128)}, u32[]{:S(2)}) copy-start(f32[64,2048]{1,0:T(8,128)} %constant.5.clone.outer_ref) | copy-start | bytes 1572868
  0.5 4.6 %copy-start.4 = (f32[64,128]{1,0:T(8,128)S(1)}, f32[64,128]{1,0:T(8,128)}, u32[]{:S(2)}) copy-start(f32[64,128]{1,0:T(8,128)} %constant.4.clone.inner_ref) | copy-start | bytes 98308
  2.4 15.4 %collective-permute-start.1 = (f32[21,16,384]{2,1,0:T(8,128)}, f32[21,16,384]{2,1,0:T(8,128)S(1)}, u32[]{:S(2)}, u32[]{:S(2)}) collective-permute-start(f32[21,16,384]{2,1,0:T(8,128)} %pack_bricks.1), channel_id=1, source_target_pairs={{0,4},{4,0},{8,12},{12,8},{16,20},{20,16},{24,28},{28,24},{1,5},{5... | collective-permute-start | bytes 1548296 | tf_op jit(solution)/shard_map/ppermute | solution.py:670
  5.0 1.3 %copy-start = (f32[5,4,32,512]{3,2,1,0:T(8,128)S(1)}, f32[5,4,32,512]{3,2,1,0:T(8,128)}, u32[]{:S(2)}) copy-start(f32[5,4,32,512]{3,2,1,0:T(8,128)} %refs_0_.7) | copy-start | bytes 3932164
  6.4 5.0 %copy-start.2 = (s32[4,32,512]{2,1,0:T(8,128)S(1)}, s32[4,32,512]{2,1,0:T(8,128)}, u32[]{:S(2)}) copy-start(s32[4,32,512]{2,1,0:T(8,128)} %mask_ref.9) | copy-start | bytes 786436
  9.8 35.9 %collective-permute-start.7 = (f32[5,4,32,512]{3,2,1,0:T(8,128)S(1)}, f32[5,4,32,512]{3,2,1,0:T(8,128)S(1)}, u32[]{:S(2)}, u32[]{:S(2)}) collective-permute-start(f32[5,4,32,512]{3,2,1,0:T(8,128)S(1)} %get-tuple-element.14), channel_id=1, source_target_pairs={{0,2},{1,3},{2,0},{3,1},{4,6},{5,7},{6,4},{7,5},{8,10},{9,11},{10,... | collective-permute-start | bytes 3932168 | tf_op jit(solution)/shard_map/ppermute | solution.py:651
  11.4 2.9 %copy-start.1 = (s32[4,32,512]{2,1,0:T(8,128)S(1)}, s32[4,32,512]{2,1,0:T(8,128)}, u32[]{:S(2)}) copy-start(s32[4,32,512]{2,1,0:T(8,128)} %refs_3_.7) | copy-start | bytes 786436
  14.3 10.6 %collective-permute-start.2 = (f32[21,16,256]{2,1,0:T(8,128)S(1)}, f32[21,16,256]{2,1,0:T(8,128)S(1)}, u32[]{:S(2)}, u32[]{:S(2)}) collective-permute-start(f32[21,16,256]{2,1,0:T(8,128)S(1)} %bring_planes.3.after_ref), channel_id=1, source_target_pairs={{0,4},{4,0},{8,12},{12,8},{16,20},{20,16},{24,28},{28,24},{1,5},{5... | collective-permute-start | bytes 1032200 | tf_op jit(solution)/shard_map/ppermute | solution.py:681
  17.8 13.2 %collective-permute-start.5 = (f32[16,16,384]{2,1,0:T(8,128)S(1)}, f32[16,16,384]{2,1,0:T(8,128)S(1)}, u32[]{:S(2)}, u32[]{:S(2)}) collective-permute-start(f32[16,16,384]{2,1,0:T(8,128)S(1)} %pass_planes.4.after_ref), channel_id=1, source_target_pairs={{0,8},{8,16},{16,24},{12,4},{20,12},{28,20},{1,9},{9,17},{17,25},{... | collective-permute-start | bytes 1179656 | tf_op jit(solution)/shard_map/ppermute | solution.py:686
  24.7 9.7 %collective-permute-start.4 = (f32[21,32,128]{2,1,0:T(8,128)S(1)}, f32[21,32,128]{2,1,0:T(8,128)S(1)}, u32[]{:S(2)}, u32[]{:S(2)}) collective-permute-start(f32[21,32,128]{2,1,0:T(8,128)S(1)} %bring_planes.4.after_ref), channel_id=1, source_target_pairs={{0,4},{4,0},{8,12},{12,8},{16,20},{20,16},{24,28},{28,24},{1,5},{5... | collective-permute-start | bytes 1032200 | tf_op jit(solution)/shard_map/ppermute | solution.py:681
  25.0 16.5 %collective-permute-start.8 = (f32[16,16,256]{2,1,0:T(8,128)S(1)}, f32[16,16,256]{2,1,0:T(8,128)S(1)}, u32[]{:S(2)}, u32[]{:S(2)}) collective-permute-start(f32[16,16,256]{2,1,0:T(8,128)S(1)} %pass_planes.5.after_ref), channel_id=1, source_target_pairs={{0,8},{8,16},{16,24},{12,4},{20,12},{28,20},{1,9},{9,17},{17,25},{... | collective-permute-start | bytes 786440 | tf_op jit(solution)/shard_map/ppermute | solution.py:686
  31.0 7.0 %collective-permute-start.3 = (f32[21,16,128]{2,1,0:T(8,128)S(1)}, f32[21,16,128]{2,1,0:T(8,128)S(1)}, u32[]{:S(2)}, u32[]{:S(2)}) collective-permute-start(f32[21,16,128]{2,1,0:T(8,128)S(1)} %bring_planes.5.refs_5_), channel_id=1, source_target_pairs={{0,4},{4,0},{8,12},{12,8},{16,20},{20,16},{24,28},{28,24},{1,5},{5... | collective-permute-start | bytes 516104 | tf_op jit(solution)/shard_map/ppermute | solution.py:681
  34.5 9.4 %collective-permute-start.9 = (f32[16,32,128]{2,1,0:T(8,128)S(1)}, f32[16,32,128]{2,1,0:T(8,128)S(1)}, u32[]{:S(2)}, u32[]{:S(2)}) collective-permute-start(f32[16,32,128]{2,1,0:T(8,128)S(1)} %pass_planes.6.after_ref), channel_id=1, source_target_pairs={{0,8},{8,16},{16,24},{12,4},{20,12},{28,20},{1,9},{9,17},{17,25},{... | collective-permute-start | bytes 786440 | tf_op jit(solution)/shard_map/ppermute | solution.py:686
  38.0 7.7 %collective-permute-start.6 = (f32[16,16,128]{2,1,0:T(8,128)S(1)}, f32[16,16,128]{2,1,0:T(8,128)S(1)}, u32[]{:S(2)}, u32[]{:S(2)}) collective-permute-start(f32[16,16,128]{2,1,0:T(8,128)S(1)} %pass_planes.7.refs_5_), channel_id=1, source_target_pairs={{0,8},{8,16},{16,24},{12,4},{20,12},{28,20},{1,9},{9,17},{17,25},{... | collective-permute-start | bytes 393224 | tf_op jit(solution)/shard_map/ppermute | solution.py:686

commit v6 on v5

--- a/solution.py
+++ b/solution.py
@@ -692,11 +692,11 @@
         return done
 
     acc_low = wall_part(state, mask_y, 0, half, lines[0])
-    after = hand_on(0, exchange(1, acc_low))
+    after = exchange(1, acc_low)
     acc_high = wall_part(state, mask_y, half, depth - half, after)
-    after = hand_on(1, exchange(2, acc_high))
+    after = exchange(2, hand_on(0, acc_high))
     base = home_part(band, lines, acc_low, acc_high, after)
-    after = exchange(3, base)
+    after = exchange(3, hand_on(1, base))
     after = hand_on(2, stream(0, after))
     after = hand_on(3, after)
     stream(2, stream(1, after))

time: 48.3 us -> 47.6 us (0.986)
  waiting for transfers between devices: 4.1 us -> 2.69 us
  starting transfers between devices: 20.1 us -> 20.8 us
    ppermute x1, waiting for transfers between devices: 2.72 us -> 0.01 us  [per_device(): pairs = [lax.ppermute(brick, 'gx', swap)]]
    ppermute x4, waiting for transfers between devices: 0.55 us -> 1.4 us  [hand_on(): fars.append(lax.ppermute(planes, 'gx', carry))]
    ppermute x4, starting transfers between devices: 14.7 us -> 15.3 us  [hand_on(): fars.append(lax.ppermute(planes, 'gx', carry))]
  transfers between devices with their start and end apart: 10 -> 10, of which waited for: 4 -> 2; matrix products, arithmetic and copies ran while one was open for 0% -> 0% of each run, Pallas kernels for 43% -> 44%
where the time goes in v6:
time: 47.6 us; the launch traced here: 47.4 us
  Pallas kernels  23.1 us (49%)
  starting transfers between devices  20.8 us (44%)
  waiting for transfers between devices  2.69 us (6%)
  local copies, waits for them, and re-layouts  0.59 us (1%)
    ppermute x4, starting transfers between devices, hand_on(): fars.append(lax.ppermute(planes, 'gx', carry))  15.3 us
    pallas_call x4, Pallas kernels, stream_part(): call(functools.partial(stream_kernel, part, places), 'stream_faces', 0.3...  8.71 us
    pallas_call x2, Pallas kernels, wall_part(): call(kernel, 'wall_faces', 5.0 * count / depth, [PLACE, PLACE, ANYWHERE],...  5.81 us
    pallas_call x1, Pallas kernels, away_part(): call(functools.partial(away_kernel, masks), 'span_away', 3.0, [PLACE] * 4...  3.41 us
    ppermute x1, starting transfers between devices, per_device(): pairs = [lax.ppermute(brick, 'gx', swap)]  2.57 us
    pallas_call x1, Pallas kernels, home_part(): call(home_kernel, 'span_home', 2.0, [PLACE] * 6 + [ANYWHERE], PLACE, shap...  2.2 us
    ppermute x2, starting transfers between devices, flip(): return lax.ppermute(array, 'gz', [(g, g ^ bit) for g in range(groups)])  2.04 us
    pallas_call x1, Pallas kernels, pack_part(): call(functools.partial(pack_kernel, parts), 'pack_bricks', 1.0, [HBM, HBM...  1.93 us
  transfers between devices with their start and end apart: 10, of which 2 were waited for; matrix products, arithmetic and copies ran while one was open for 0% of the time, Pallas kernels for 44%

profile of v6, /device:TPU:0, one launch (start us, length us, event | category | flops | bytes accessed | tf_op | source)
XLA Modules:
  0.0 47.4 jit_solution(15879545023118884290)
XLA Ops:
  0.0 0.5 collective-permute-start
  0.5 0.0 copy-start.5
  0.5 0.0 copy-start.3
  0.5 0.0 copy-start.4
  0.5 1.9 %pack_bricks.1 = f32[21,16,384]{2,1,0:T(8,128)} custom-call(f32[20,32,512]{2,1,0:T(8,128)} %bitcast.1, s32[4,32,512]{2,1,0:T(8,128)} %refs_3_.7), custom_call_target="tpu_custom_call" | custom-call | flops 1000000000 | bytes 3000000 | tf_op jit(solution)/shard_map/pack_bricks/pallas_call | solution.py:227
  2.4 2.6 %collective-permute-start.2 = (f32[21,16,384]{2,1,0:T(8,128)}, f32[21,16,384]{2,1,0:T(8,128)S(1)}, u32[]{:S(2)}, u32[]{:S(2)}) collective-permute-start(f32[21,16,384]{2,1,0:T(8,128)} %pack_bricks.1), channel_id=1, source_target_pairs={{0,4},{4,0},{8,12},{12,8},{16,20},{20,16},{24,28},{28,24},{1,5},{5... | collective-permute-start | bytes 1548296 | tf_op jit(solution)/shard_map/ppermute | solution.py:670
  5.0 0.0 copy-done.5
  5.0 0.1 reshape.6.filter_ref
  5.0 0.0 copy-start
  5.0 0.0 collective-permute-done.after_ref.core_ref
  5.1 0.0 copy-done.3
  5.1 0.0 copy-done.4
  5.1 0.8 %circulant_band.1 = (bf16[256,2560]{1,0:T(8,128)(2,1)S(1)}, bf16[256,2560]{1,0:T(8,128)(2,1)S(1)}) custom-call(f32[32,32]{1,0:T(8,128)S(1)} %reshape.6.filter_ref, f32[64,128]{1,0:T(8,128)S(1)} %copy-done.4, f32[64,2048]{1,0:T(8,128)S(1)} %copy-done.3, f32[5,4,32,512]{3,2,1,0:T(8,128)S(1)} %collective-permute-done.after_ref.core_ref), custom_call_target="tpu_custom_call" | custom-call | flops 1000000000 | bytes 3000000 | tf_op jit(solution)/shard_map/circulant_band/pallas_call | solution.py:550
  5.9 0.5 %copy-done = f32[5,4,32,512]{3,2,1,0:T(8,128)S(1)} copy-done((f32[5,4,32,512]{3,2,1,0:T(8,128)S(1)}, f32[5,4,32,512]{3,2,1,0:T(8,128)}, u32[]{:S(2)}) %copy-start) | copy-done | bytes 1310744
  6.4 0.0 copy-start.2
  6.4 3.4 %span_away.1 = (f32[5,4,32,512]{3,2,1,0:T(8,128)S(1)}, bf16[640,1024]{1,0:T(8,128)(2,1)S(1)}, bf16[640,1024]{1,0:T(8,128)(2,1)S(1)}) custom-call(bf16[256,2560]{1,0:T(8,128)(2,1)S(1)} %get-tuple-element.10.high_ref, bf16[256,2560]{1,0:T(8,128)(2,1)S(1)} %get-tuple-element.11.low_ref, f32[5,4,32,512]{3,2,1,0:T(8,128)S(1)} %copy-done, ...), custom_call_target="tpu_custom_call" | custom-call | flops 3000000000 | bytes 9000000 | tf_op jit(solution)/shard_map/span_away/pallas_call | solution.py:611
  9.8 1.6 %collective-permute-start.7 = (f32[5,4,32,512]{3,2,1,0:T(8,128)S(1)}, f32[5,4,32,512]{3,2,1,0:T(8,128)S(1)}, u32[]{:S(2)}, u32[]{:S(2)}) collective-permute-start(f32[5,4,32,512]{3,2,1,0:T(8,128)S(1)} %get-tuple-element.14), channel_id=1, source_target_pairs={{0,2},{1,3},{2,0},{3,1},{4,6},{5,7},{6,4},{7,5},{8,10},{9,11},{10,... | collective-permute-start | bytes 3932168 | tf_op jit(solution)/shard_map/ppermute | solution.py:651
  11.4 0.0 copy-done.2
  11.4 0.0 copy-start.1
  11.4 2.9 %wall_faces.2.after_ref.first_ref = f32[5,2,32,512]{3,2,1,0:T(8,128)S(1)} custom-call(f32[5,4,32,512]{3,2,1,0:T(8,128)S(1)} %copy-done, s32[4,32,512]{2,1,0:T(8,128)S(1)} %copy-done.2, bf16[640,1024]{1,0:T(8,128)(2,1)S(1)} %get-tuple-element.12.after_ref.xh), custom_call_target="tpu_custom_call" | custom-call | flops 2500000000 | bytes 7500000 | tf_op jit(solution)/shard_map/wall_faces/pallas_call | solution.py:190
  14.3 0.0 copy-done.1
  14.3 0.7 %collective-permute-start.1 = (f32[21,16,256]{2,1,0:T(8,128)S(1)}, f32[21,16,256]{2,1,0:T(8,128)S(1)}, u32[]{:S(2)}, u32[]{:S(2)}) collective-permute-start(f32[21,16,256]{2,1,0:T(8,128)S(1)} %bring_planes.3.after_ref), channel_id=1, source_target_pairs={{0,4},{4,0},{8,12},{12,8},{16,20},{20,16},{24,28},{28,24},{1,5},{5... | collective-permute-start | bytes 1032200 | tf_op jit(solution)/shard_map/ppermute | solution.py:681
  15.1 2.9 %wall_faces.3.after_ref.second_ref = f32[5,2,32,512]{3,2,1,0:T(8,128)S(1)} custom-call(f32[5,4,32,512]{3,2,1,0:T(8,128)S(1)} %copy-done, s32[4,32,512]{2,1,0:T(8,128)S(1)} %copy-done.2, f32[21,16,256]{2,1,0:T(8,128)S(1)} %bring_planes.3.after_ref), custom_call_target="tpu_custom_call" | custom-call | flops 2500000000 | bytes 7500000 | tf_op jit(solution)/shard_map/wall_faces/pallas_call | solution.py:190
  18.0 0.0 collective-permute-done.2.pair_ref.refs_1_
  18.0 3.7 %collective-permute-start.5 = (f32[16,16,384]{2,1,0:T(8,128)S(1)}, f32[16,16,384]{2,1,0:T(8,128)S(1)}, u32[]{:S(2)}, u32[]{:S(2)}) collective-permute-start(f32[16,16,384]{2,1,0:T(8,128)S(1)} %pass_planes.4.after_ref), channel_id=1, source_target_pairs={{0,8},{8,16},{16,24},{12,4},{20,12},{28,20},{1,9},{9,17},{17,25},{... | collective-permute-start | bytes 1179656 | tf_op jit(solution)/shard_map/ppermute | solution.py:686
  21.8 0.1 collective-permute-start.4
  21.9 2.2 %span_home.1.after_ref.refs_4_ = f32[5,4,32,512]{3,2,1,0:T(8,128)S(1)} custom-call(bf16[256,2560]{1,0:T(8,128)(2,1)S(1)} %get-tuple-element.10.high_ref, bf16[256,2560]{1,0:T(8,128)(2,1)S(1)} %get-tuple-element.11.low_ref, bf16[640,1024]{1,0:T(8,128)(2,1)S(1)} %get-tuple-element.12.after_ref.xh, bf16[640,1024]{1,0:T(8,128)(2,1)S(1)} %get-tuple-element.13.xl, ...), custom_call_target="tpu_custom_call" | custom-call | flops 2000000000 | bytes 6000000 | tf_op jit(solution)/shard_map/span_home/pallas_call | solution.py:633
  24.1 1.3 %collective-permute-done.1.pair_ref.refs_1_ = f32[21,16,256]{2,1,0:T(8,128)S(1)} collective-permute-done((f32[21,16,256]{2,1,0:T(8,128)S(1)}, f32[21,16,256]{2,1,0:T(8,128)S(1)}, u32[]{:S(2)}, u32[]{:S(2)}) %collective-permute-start.1) | collective-permute-done | bytes 344096 | tf_op jit(solution)/shard_map/ppermute | solution.py:681
  25.4 3.7 %collective-permute-start.8 = (f32[16,16,256]{2,1,0:T(8,128)S(1)}, f32[16,16,256]{2,1,0:T(8,128)S(1)}, u32[]{:S(2)}, u32[]{:S(2)}) collective-permute-start(f32[16,16,256]{2,1,0:T(8,128)S(1)} %pass_planes.5.after_ref), channel_id=1, source_target_pairs={{0,8},{8,16},{16,24},{12,4},{20,12},{28,20},{1,9},{9,17},{17,25},{... | collective-permute-start | bytes 786440 | tf_op jit(solution)/shard_map/ppermute | solution.py:686
  29.2 0.1 collective-permute-start.3
  29.2 1.4 %collective-permute-done.5.refs_2_ = f32[16,16,384]{2,1,0:T(8,128)S(1)} collective-permute-done((f32[16,16,384]{2,1,0:T(8,128)S(1)}, f32[16,16,384]{2,1,0:T(8,128)S(1)}, u32[]{:S(2)}, u32[]{:S(2)}) %collective-permute-start.5) | collective-permute-done | bytes 393248 | tf_op jit(solution)/shard_map/ppermute | solution.py:686
  30.6 2.7 %stream_faces.4.after_ref.refs_6_ = f32[5,4,16,384]{3,2,1,0:T(8,128)S(1)} custom-call(f32[5,4,32,512]{3,2,1,0:T(8,128)S(1)} %copy-done, f32[21,16,384]{2,1,0:T(8,128)S(1)} %collective-permute-done.2.pair_ref.refs_1_, f32[16,16,384]{2,1,0:T(8,128)S(1)} %collective-permute-done.5.refs_2_, s32[4,32,512]{2,1,0:T(8,128)S(1)} %copy-done.1, ...), custom_call_target="tpu_custom_call" | custom-call | flops 1800000000 | bytes 5399999 | tf_op jit(solution)/shard_map/stream_faces/pallas_call | solution.py:473
  33.3 0.0 collective-permute-done.4.pair_ref.refs_1_
  33.4 4.4 %collective-permute-start.9 = (f32[16,32,128]{2,1,0:T(8,128)S(1)}, f32[16,32,128]{2,1,0:T(8,128)S(1)}, u32[]{:S(2)}, u32[]{:S(2)}) collective-permute-start(f32[16,32,128]{2,1,0:T(8,128)S(1)} %pass_planes.6.after_ref), channel_id=1, source_target_pairs={{0,8},{8,16},{16,24},{12,4},{20,12},{28,20},{1,9},{9,17},{17,25},{... | collective-permute-start | bytes 786440 | tf_op jit(solution)/shard_map/ppermute | solution.py:686
  37.8 0.0 collective-permute-done.3.pair_ref.refs_1_
  37.9 3.5 %collective-permute-start.6 = (f32[16,16,128]{2,1,0:T(8,128)S(1)}, f32[16,16,128]{2,1,0:T(8,128)S(1)}, u32[]{:S(2)}, u32[]{:S(2)}) collective-permute-start(f32[16,16,128]{2,1,0:T(8,128)S(1)} %pass_planes.7.refs_5_), channel_id=1, source_target_pairs={{0,8},{8,16},{16,24},{12,4},{20,12},{28,20},{1,9},{9,17},{17,25},{... | collective-permute-start | bytes 393224 | tf_op jit(solution)/shard_map/ppermute | solution.py:686
  41.3 0.0 collective-permute-done.8.refs_2_
  41.3 1.8 %stream_faces.5.refs_5_.refs_7_ = f32[5,4,16,256]{3,2,1,0:T(8,128)S(1)} custom-call(f32[5,4,32,512]{3,2,1,0:T(8,128)S(1)} %copy-done, f32[21,16,256]{2,1,0:T(8,128)S(1)} %collective-permute-done.1.pair_ref.refs_1_, f32[16,16,256]{2,1,0:T(8,128)S(1)} %collective-permute-done.8.refs_2_, s32[4,32,512]{2,1,0:T(8,128)S(1)} %copy-done.1, ...), custom_call_target="tpu_custom_call" | custom-call | flops 1200000000 | bytes 3600000 | tf_op jit(solution)/shard_map/stream_faces/pallas_call | solution.py:473
  43.2 0.0 collective-permute-done.9.refs_2_
  43.2 1.8 %stream_faces.6.refs_8_ = f32[5,4,32,128]{3,2,1,0:T(8,128)S(1)} custom-call(f32[5,4,32,512]{3,2,1,0:T(8,128)S(1)} %copy-done, f32[21,32,128]{2,1,0:T(8,128)S(1)} %collective-permute-done.4.pair_ref.refs_1_, f32[16,32,128]{2,1,0:T(8,128)S(1)} %collective-permute-done.9.refs_2_, s32[4,32,512]{2,1,0:T(8,128)S(1)} %copy-done.1, ...), custom_call_target="tpu_custom_call" | custom-call | flops 1200000000 | bytes 3600000 | tf_op jit(solution)/shard_map/stream_faces/pallas_call | solution.py:473
  45.0 0.0 collective-permute-done.6.refs_2_
  45.0 0.0 collective-permute-done.7.refs_5_
  45.0 2.4 %stream_faces.7 = f32[5,4,32,512]{3,2,1,0:T(8,128)} custom-call(f32[5,4,32,512]{3,2,1,0:T(8,128)S(1)} %copy-done, f32[21,16,128]{2,1,0:T(8,128)S(1)} %collective-permute-done.3.pair_ref.refs_1_, f32[16,16,128]{2,1,0:T(8,128)S(1)} %collective-permute-done.6.refs_2_, s32[4,32,512]{2,1,0:T(8,128)S(1)} %copy-done.1, ...), custom_call_target="tpu_custom_call" | custom-call | flops 600000000 | bytes 1800000 | tf_op jit(solution)/shard_map/stream_faces/pallas_call | solution.py:473
  (7 shorter events, 0.2 us)
Async XLA Ops:
  0.0 5.0 %collective-permute-start = (f32[5,4,32,512]{3,2,1,0:T(8,128)}, f32[5,4,32,512]{3,2,1,0:T(8,128)S(1)}, u32[]{:S(2)}, u32[]{:S(2)}) collective-permute-start(f32[5,4,32,512]{3,2,1,0:T(8,128)} %refs_0_.7), channel_id=1, source_target_pairs={{0,1},{1,0},{2,3},{3,2},{4,5},{5,4},{6,7},{7,6},{8,9},{9,8},{10,11... | collective-permute-start | bytes 3932168 | tf_op jit(solution)/shard_map/ppermute | solution.py:651
  0.5 4.5 %copy-start.5 = (f32[1024]{0:T(1024)S(1)}, f32[1024]{0:T(1024)}, u32[]{:S(2)}) copy-start(f32[1024]{0:T(1024)} %param.9) | copy-start | bytes 12292
  0.5 4.6 %copy-start.3 = (f32[64,2048]{1,0:T(8,128)S(1)}, f32[64,2048]{1,0:T(8,128)}, u32[]{:S(2)}) copy-start(f32[64,2048]{1,0:T(8,128)} %constant.5.clone.outer_ref) | copy-start | bytes 1572868
  0.5 4.6 %copy-start.4 = (f32[64,128]{1,0:T(8,128)S(1)}, f32[64,128]{1,0:T(8,128)}, u32[]{:S(2)}) copy-start(f32[64,128]{1,0:T(8,128)} %constant.4.clone.inner_ref) | copy-start | bytes 98308
  2.4 15.6 %collective-permute-start.2 = (f32[21,16,384]{2,1,0:T(8,128)}, f32[21,16,384]{2,1,0:T(8,128)S(1)}, u32[]{:S(2)}, u32[]{:S(2)}) collective-permute-start(f32[21,16,384]{2,1,0:T(8,128)} %pack_bricks.1), channel_id=1, source_target_pairs={{0,4},{4,0},{8,12},{12,8},{16,20},{20,16},{24,28},{28,24},{1,5},{5... | collective-permute-start | bytes 1548296 | tf_op jit(solution)/shard_map/ppermute | solution.py:670
  5.0 1.3 %copy-start = (f32[5,4,32,512]{3,2,1,0:T(8,128)S(1)}, f32[5,4,32,512]{3,2,1,0:T(8,128)}, u32[]{:S(2)}) copy-start(f32[5,4,32,512]{3,2,1,0:T(8,128)} %refs_0_.7) | copy-start | bytes 3932164
  6.4 5.0 %copy-start.2 = (s32[4,32,512]{2,1,0:T(8,128)S(1)}, s32[4,32,512]{2,1,0:T(8,128)}, u32[]{:S(2)}) copy-start(s32[4,32,512]{2,1,0:T(8,128)} %mask_ref.8) | copy-start | bytes 786436
  9.8 35.2 %collective-permute-start.7 = (f32[5,4,32,512]{3,2,1,0:T(8,128)S(1)}, f32[5,4,32,512]{3,2,1,0:T(8,128)S(1)}, u32[]{:S(2)}, u32[]{:S(2)}) collective-permute-start(f32[5,4,32,512]{3,2,1,0:T(8,128)S(1)} %get-tuple-element.14), channel_id=1, source_target_pairs={{0,2},{1,3},{2,0},{3,1},{4,6},{5,7},{6,4},{7,5},{8,10},{9,11},{10,... | collective-permute-start | bytes 3932168 | tf_op jit(solution)/shard_map/ppermute | solution.py:651
  11.4 2.9 %copy-start.1 = (s32[4,32,512]{2,1,0:T(8,128)S(1)}, s32[4,32,512]{2,1,0:T(8,128)}, u32[]{:S(2)}) copy-start(s32[4,32,512]{2,1,0:T(8,128)} %refs_3_.7) | copy-start | bytes 786436
  14.3 11.1 %collective-permute-start.1 = (f32[21,16,256]{2,1,0:T(8,128)S(1)}, f32[21,16,256]{2,1,0:T(8,128)S(1)}, u32[]{:S(2)}, u32[]{:S(2)}) collective-permute-start(f32[21,16,256]{2,1,0:T(8,128)S(1)} %bring_planes.3.after_ref), channel_id=1, source_target_pairs={{0,4},{4,0},{8,12},{12,8},{16,20},{20,16},{24,28},{28,24},{1,5},{5... | collective-permute-start | bytes 1032200 | tf_op jit(solution)/shard_map/ppermute | solution.py:681
  18.0 12.6 %collective-permute-start.5 = (f32[16,16,384]{2,1,0:T(8,128)S(1)}, f32[16,16,384]{2,1,0:T(8,128)S(1)}, u32[]{:S(2)}, u32[]{:S(2)}) collective-permute-start(f32[16,16,384]{2,1,0:T(8,128)S(1)} %pass_planes.4.after_ref), channel_id=1, source_target_pairs={{0,8},{8,16},{16,24},{12,4},{20,12},{28,20},{1,9},{9,17},{17,25},{... | collective-permute-start | bytes 1179656 | tf_op jit(solution)/shard_map/ppermute | solution.py:686
  21.8 11.5 %collective-permute-start.4 = (f32[21,32,128]{2,1,0:T(8,128)S(1)}, f32[21,32,128]{2,1,0:T(8,128)S(1)}, u32[]{:S(2)}, u32[]{:S(2)}) collective-permute-start(f32[21,32,128]{2,1,0:T(8,128)S(1)} %bring_planes.4.after_ref), channel_id=1, source_target_pairs={{0,4},{4,0},{8,12},{12,8},{16,20},{20,16},{24,28},{28,24},{1,5},{5... | collective-permute-start | bytes 1032200 | tf_op jit(solution)/shard_map/ppermute | solution.py:681
  25.4 15.9 %collective-permute-start.8 = (f32[16,16,256]{2,1,0:T(8,128)S(1)}, f32[16,16,256]{2,1,0:T(8,128)S(1)}, u32[]{:S(2)}, u32[]{:S(2)}) collective-permute-start(f32[16,16,256]{2,1,0:T(8,128)S(1)} %pass_planes.5.after_ref), channel_id=1, source_target_pairs={{0,8},{8,16},{16,24},{12,4},{20,12},{28,20},{1,9},{9,17},{17,25},{... | collective-permute-start | bytes 786440 | tf_op jit(solution)/shard_map/ppermute | solution.py:686
  29.2 8.6 %collective-permute-start.3 = (f32[21,16,128]{2,1,0:T(8,128)S(1)}, f32[21,16,128]{2,1,0:T(8,128)S(1)}, u32[]{:S(2)}, u32[]{:S(2)}) collective-permute-start(f32[21,16,128]{2,1,0:T(8,128)S(1)} %bring_planes.5.refs_5_), channel_id=1, source_target_pairs={{0,4},{4,0},{8,12},{12,8},{16,20},{20,16},{24,28},{28,24},{1,5},{5... | collective-permute-start | bytes 516104 | tf_op jit(solution)/shard_map/ppermute | solution.py:681
  33.4 9.8 %collective-permute-start.9 = (f32[16,32,128]{2,1,0:T(8,128)S(1)}, f32[16,32,128]{2,1,0:T(8,128)S(1)}, u32[]{:S(2)}, u32[]{:S(2)}) collective-permute-start(f32[16,32,128]{2,1,0:T(8,128)S(1)} %pass_planes.6.after_ref), channel_id=1, source_target_pairs={{0,8},{8,16},{16,24},{12,4},{20,12},{28,20},{1,9},{9,17},{17,25},{... | collective-permute-start | bytes 786440 | tf_op jit(solution)/shard_map/ppermute | solution.py:686
  37.9 7.1 %collective-permute-start.6 = (f32[16,16,128]{2,1,0:T(8,128)S(1)}, f32[16,16,128]{2,1,0:T(8,128)S(1)}, u32[]{:S(2)}, u32[]{:S(2)}) collective-permute-start(f32[16,16,128]{2,1,0:T(8,128)S(1)} %pass_planes.7.refs_5_), channel_id=1, source_target_pairs={{0,8},{8,16},{16,24},{12,4},{20,12},{28,20},{1,9},{9,17},{17,25},{... | collective-permute-start | bytes 393224 | tf_op jit(solution)/shard_map/ppermute | solution.py:686

commit v7 on v6

--- a/solution.py
+++ b/solution.py
@@ -14,14 +14,13 @@
 ROWS = 8
 LANES = 128
 VMEM_BYTES = 24 * 1024 * 1024
-PACK_BYTES = 60 * 1024 * 1024
 FACE_SCALE = -TIME_STEP / 60.0
 PLACE = pl.BlockSpec(memory_space=pltpu.VMEM)
 ANYWHERE = pl.BlockSpec(memory_space=pl.ANY)
 HBM = pl.BlockSpec(memory_space=pltpu.HBM)
 
 
-def call(kernel, name, weight, ins, outs, out_shape, scratch=(), aliases=None, vmem=VMEM_BYTES):
+def call(kernel, name, weight, ins, outs, out_shape, scratch=(), aliases=None):
     return pl.pallas_call(
         kernel,
         out_shape=out_shape,
@@ -29,7 +28,7 @@
         out_specs=outs,
         scratch_shapes=list(scratch),
         input_output_aliases=aliases or {},
-        compiler_params=pltpu.CompilerParams(vmem_limit_bytes=vmem),
+        compiler_params=pltpu.CompilerParams(vmem_limit_bytes=VMEM_BYTES),
         cost_estimate=pl.CostEstimate(
             flops=int(weight * 1e9), bytes_accessed=int(weight * 3e6), transcendentals=0
         ),
@@ -198,47 +197,6 @@
     )(state, mask_y, after)
 
 
-def pack_kernel(parts, state_ref, mask_ref, *refs):
-    outs = refs[: len(parts)]
-    mask_s, sems = refs[len(parts) :]
-    planes = state_ref.shape[0]
-    mask_copy = pltpu.make_async_copy(mask_ref.at[0], mask_s, sems.at[len(parts)])
-    mask_copy.start()
-    copies = [
-        pltpu.make_async_copy(
-            state_ref.at[:, pl.ds(row, rows), pl.ds(lane, width)],
-            out.at[pl.ds(0, planes)],
-            sems.at[c],
-        )
-        for c, ((row, rows, lane, width), out) in enumerate(zip(parts, outs))
-    ]
-    for copy in copies:
-        copy.start()
-    mask_copy.wait()
-    for (row, rows, lane, width), out in zip(parts, outs):
-        out[planes] = mask_s[row : row + rows, lane : lane + width].astype(jnp.float32)
-    for copy in copies:
-        copy.wait()
-
-
-def pack_part(state, mask_x, parts):
-    fields, depth, rows_all, width = state.shape
-    planes = fields * depth
-    return call(
-        functools.partial(pack_kernel, parts),
-        "pack_bricks",
-        1.0,
-        [HBM, HBM],
-        [PLACE] * len(parts),
-        [shape_of(planes + 1, rows, lane_count) for _, rows, _, lane_count in parts],
-        [
-            pltpu.VMEM((rows_all, width), jnp.int32),
-            pltpu.SemaphoreType.DMA((len(parts) + 1,)),
-        ],
-        vmem=PACK_BYTES,
-    )(state.reshape(planes, rows_all, width), mask_x)
-
-
 def bring_kernel(part, state_ref, mask_ref, after_ref, out):
     row, rows, lane, width = part
     fields, depth, _, _ = state_ref.shape
@@ -666,7 +624,10 @@
         ]
     else:
         parts = [(row, rows_all // 4, 0, width) for row in range(0, rows_all, rows_all // 4)]
-    (brick,) = pack_part(state, mask_x, parts[:1])
+    row, rows, lane, count = parts[0]
+    cells = state[:, :, row : row + rows, lane : lane + count]
+    switches = mask_x[:1, row : row + rows, lane : lane + count]
+    brick = bring_part(cells, switches, (0, rows, 0, count), switches)
     pairs = [lax.ppermute(brick, "gx", swap)]
     band = circulant(span_filter, span, width, core)
 

time: 47.6 us -> 48.1 us (1.011)
  Pallas kernels: 23.1 us -> 21.2 us
  local copies, waits for them, and re-layouts: 0.59 us -> 2.4 us
  waiting for transfers between devices: 2.69 us -> 3.45 us
    pallas_call x1 -> x0, Pallas kernels: 1.93 us -> none  [pack_part(): call(functools.partial(pack_kernel, parts), 'pack_bricks', 1.0, [HBM, HBM...]
    slice x0 -> x2, local copies, waits for them, and re-layouts: none -> 1.81 us  [the longest x1 1.07 us: per_device(): cells = state[:, :, row:row + rows, lane:lane + count]]
    ppermute x4, waiting for transfers between devices: 1.4 us -> 1.96 us  [hand_on(): fars.append(lax.ppermute(planes, 'gx', carry))]
  transfers between devices with their start and end apart: 10 -> 10, of which waited for: 2 -> 2; matrix products, arithmetic and copies ran while one was open for 0% -> 4% of each run, Pallas kernels for 44% -> 39%
where the time goes in v7:
time: 48.1 us; the launch traced here: 47.8 us
  Pallas kernels  21.2 us (44%)
  starting transfers between devices  20.6 us (43%)
  waiting for transfers between devices  3.45 us (7%)
  local copies, waits for them, and re-layouts  2.4 us (5%)
    ppermute x4, starting transfers between devices, hand_on(): fars.append(lax.ppermute(planes, 'gx', carry))  14.9 us
    pallas_call x4, Pallas kernels, stream_part(): call(functools.partial(stream_kernel, part, places), 'stream_faces', 0.3...  8.71 us
    pallas_call x2, Pallas kernels, wall_part(): call(kernel, 'wall_faces', 5.0 * count / depth, [PLACE, PLACE, ANYWHERE],...  5.81 us
    pallas_call x1, Pallas kernels, away_part(): call(functools.partial(away_kernel, masks), 'span_away', 3.0, [PLACE] * 4...  3.41 us
    ppermute x1, starting transfers between devices, per_device(): pairs = [lax.ppermute(brick, 'gx', swap)]  2.63 us
    pallas_call x1, Pallas kernels, home_part(): call(home_kernel, 'span_home', 2.0, [PLACE] * 6 + [ANYWHERE], PLACE, shap...  2.2 us
    ppermute x2, starting transfers between devices, flip(): return lax.ppermute(array, 'gz', [(g, g ^ bit) for g in range(groups)])  2.11 us
    ppermute x4, waiting for transfers between devices, hand_on(): fars.append(lax.ppermute(planes, 'gx', carry))  1.96 us
  transfers between devices with their start and end apart: 10, of which 2 were waited for; matrix products, arithmetic and copies ran while one was open for 4% of the time, Pallas kernels for 39%

profile of v7, /device:TPU:0, one launch (start us, length us, event | category | flops | bytes accessed | tf_op | source)
XLA Modules:
  0.0 47.8 jit_solution(13031476670720783033)
XLA Ops:
  0.0 0.0 copy-start.3
  0.0 0.0 copy-start.4
  0.0 0.0 copy-start.5
  0.0 0.5 %collective-permute-start = (f32[5,4,32,512]{3,2,1,0:T(8,128)}, f32[5,4,32,512]{3,2,1,0:T(8,128)S(1)}, u32[]{:S(2)}, u32[]{:S(2)}) collective-permute-start(f32[5,4,32,512]{3,2,1,0:T(8,128)} %refs_0_.7), channel_id=1, source_target_pairs={{0,1},{1,0},{2,3},{3,2},{4,5},{5,4},{6,7},{7,6},{8,9},{9,8},{10,11... | collective-permute-start | bytes 3932168 | tf_op jit(solution)/shard_map/ppermute | solution.py:609
  0.5 1.1 %slice.6.state_ref = f32[5,4,16,384]{3,2,1,0:T(8,128)S(1)} slice(f32[5,4,32,512]{3,2,1,0:T(8,128)} %refs_0_.7), slice={[0:5], [0:4], [0:16], [0:384]} | slice | bytes 983040 | tf_op jit(solution)/shard_map/slice | solution.py:628
  1.6 0.7 %slice.7.mask_ref.after_ref = s32[1,16,384]{2,1,0:T(8,128)S(1)} slice(s32[4,32,512]{2,1,0:T(8,128)} %refs_3_.7), slice={[0:1], [0:16], [0:384]} | slice | bytes 49152 | tf_op jit(solution)/shard_map/slice | solution.py:629
  2.4 2.6 %collective-permute-start.2 = (f32[21,16,384]{2,1,0:T(8,128)S(1)}, f32[21,16,384]{2,1,0:T(8,128)S(1)}, u32[]{:S(2)}, u32[]{:S(2)}) collective-permute-start(f32[21,16,384]{2,1,0:T(8,128)S(1)} %bring_planes.5), channel_id=1, source_target_pairs={{0,4},{4,0},{8,12},{12,8},{16,20},{20,16},{24,28},{28,24},{1,5},{5... | collective-permute-start | bytes 1548296 | tf_op jit(solution)/shard_map/ppermute | solution.py:631
  5.0 0.0 copy-done.5
  5.0 0.1 reshape.3.filter_ref
  5.1 0.0 copy-start
  5.1 0.0 collective-permute-done.after_ref.core_ref
  5.1 0.0 copy-done.3
  5.1 0.0 copy-done.4
  5.1 0.8 %circulant_band.1 = (bf16[256,2560]{1,0:T(8,128)(2,1)S(1)}, bf16[256,2560]{1,0:T(8,128)(2,1)S(1)}) custom-call(f32[32,32]{1,0:T(8,128)S(1)} %reshape.3.filter_ref, f32[64,128]{1,0:T(8,128)S(1)} %copy-done.4, f32[64,2048]{1,0:T(8,128)S(1)} %copy-done.3, f32[5,4,32,512]{3,2,1,0:T(8,128)S(1)} %collective-permute-done.after_ref.core_ref), custom_call_target="tpu_custom_call" | custom-call | flops 1000000000 | bytes 3000000 | tf_op jit(solution)/shard_map/circulant_band/pallas_call | solution.py:508
  5.9 0.5 %copy-done = f32[5,4,32,512]{3,2,1,0:T(8,128)S(1)} copy-done((f32[5,4,32,512]{3,2,1,0:T(8,128)S(1)}, f32[5,4,32,512]{3,2,1,0:T(8,128)}, u32[]{:S(2)}) %copy-start) | copy-done | bytes 1310744
  6.4 0.0 copy-start.2
  6.4 3.4 %span_away.1 = (f32[5,4,32,512]{3,2,1,0:T(8,128)S(1)}, bf16[640,1024]{1,0:T(8,128)(2,1)S(1)}, bf16[640,1024]{1,0:T(8,128)(2,1)S(1)}) custom-call(bf16[256,2560]{1,0:T(8,128)(2,1)S(1)} %get-tuple-element.10.high_ref, bf16[256,2560]{1,0:T(8,128)(2,1)S(1)} %get-tuple-element.11.low_ref, f32[5,4,32,512]{3,2,1,0:T(8,128)S(1)} %copy-done, ...), custom_call_target="tpu_custom_call" | custom-call | flops 3000000000 | bytes 9000000 | tf_op jit(solution)/shard_map/span_away/pallas_call | solution.py:569
  9.8 1.6 %collective-permute-start.7 = (f32[5,4,32,512]{3,2,1,0:T(8,128)S(1)}, f32[5,4,32,512]{3,2,1,0:T(8,128)S(1)}, u32[]{:S(2)}, u32[]{:S(2)}) collective-permute-start(f32[5,4,32,512]{3,2,1,0:T(8,128)S(1)} %get-tuple-element.14), channel_id=1, source_target_pairs={{0,2},{1,3},{2,0},{3,1},{4,6},{5,7},{6,4},{7,5},{8,10},{9,11},{10,... | collective-permute-start | bytes 3932168 | tf_op jit(solution)/shard_map/ppermute | solution.py:609
  11.4 0.0 copy-done.2
  11.4 0.0 copy-start.1
  11.4 2.9 %wall_faces.2.after_ref.first_ref = f32[5,2,32,512]{3,2,1,0:T(8,128)S(1)} custom-call(f32[5,4,32,512]{3,2,1,0:T(8,128)S(1)} %copy-done, s32[4,32,512]{2,1,0:T(8,128)S(1)} %copy-done.2, bf16[640,1024]{1,0:T(8,128)(2,1)S(1)} %get-tuple-element.12.after_ref.xh), custom_call_target="tpu_custom_call" | custom-call | flops 2500000000 | bytes 7500000 | tf_op jit(solution)/shard_map/wall_faces/pallas_call | solution.py:189
  14.3 0.0 copy-done.1
  14.4 0.8 %collective-permute-start.1 = (f32[21,16,256]{2,1,0:T(8,128)S(1)}, f32[21,16,256]{2,1,0:T(8,128)S(1)}, u32[]{:S(2)}, u32[]{:S(2)}) collective-permute-start(f32[21,16,256]{2,1,0:T(8,128)S(1)} %bring_planes.4.after_ref), channel_id=1, source_target_pairs={{0,4},{4,0},{8,12},{12,8},{16,20},{20,16},{24,28},{28,24},{1,5},{5... | collective-permute-start | bytes 1032200 | tf_op jit(solution)/shard_map/ppermute | solution.py:642
  15.1 2.9 %wall_faces.3.after_ref.second_ref = f32[5,2,32,512]{3,2,1,0:T(8,128)S(1)} custom-call(f32[5,4,32,512]{3,2,1,0:T(8,128)S(1)} %copy-done, s32[4,32,512]{2,1,0:T(8,128)S(1)} %copy-done.2, f32[21,16,256]{2,1,0:T(8,128)S(1)} %bring_planes.4.after_ref), custom_call_target="tpu_custom_call" | custom-call | flops 2500000000 | bytes 7500000 | tf_op jit(solution)/shard_map/wall_faces/pallas_call | solution.py:189
  18.0 0.0 collective-permute-done.2.pair_ref.refs_1_
  18.1 3.5 %collective-permute-start.5 = (f32[16,16,384]{2,1,0:T(8,128)S(1)}, f32[16,16,384]{2,1,0:T(8,128)S(1)}, u32[]{:S(2)}, u32[]{:S(2)}) collective-permute-start(f32[16,16,384]{2,1,0:T(8,128)S(1)} %pass_planes.4.after_ref), channel_id=1, source_target_pairs={{0,8},{8,16},{16,24},{12,4},{20,12},{28,20},{1,9},{9,17},{17,25},{... | collective-permute-start | bytes 1179656 | tf_op jit(solution)/shard_map/ppermute | solution.py:647
  21.7 0.1 collective-permute-start.4
  21.8 2.2 %span_home.1.after_ref.refs_4_ = f32[5,4,32,512]{3,2,1,0:T(8,128)S(1)} custom-call(bf16[256,2560]{1,0:T(8,128)(2,1)S(1)} %get-tuple-element.10.high_ref, bf16[256,2560]{1,0:T(8,128)(2,1)S(1)} %get-tuple-element.11.low_ref, bf16[640,1024]{1,0:T(8,128)(2,1)S(1)} %get-tuple-element.12.after_ref.xh, bf16[640,1024]{1,0:T(8,128)(2,1)S(1)} %get-tuple-element.13.xl, ...), custom_call_target="tpu_custom_call" | custom-call | flops 2000000000 | bytes 6000000 | tf_op jit(solution)/shard_map/span_home/pallas_call | solution.py:591
  24.0 1.5 %collective-permute-done.1.pair_ref.refs_1_ = f32[21,16,256]{2,1,0:T(8,128)S(1)} collective-permute-done((f32[21,16,256]{2,1,0:T(8,128)S(1)}, f32[21,16,256]{2,1,0:T(8,128)S(1)}, u32[]{:S(2)}, u32[]{:S(2)}) %collective-permute-start.1) | collective-permute-done | bytes 344096 | tf_op jit(solution)/shard_map/ppermute | solution.py:642
  25.5 3.5 %collective-permute-start.8 = (f32[16,16,256]{2,1,0:T(8,128)S(1)}, f32[16,16,256]{2,1,0:T(8,128)S(1)}, u32[]{:S(2)}, u32[]{:S(2)}) collective-permute-start(f32[16,16,256]{2,1,0:T(8,128)S(1)} %pass_planes.5.after_ref), channel_id=1, source_target_pairs={{0,8},{8,16},{16,24},{12,4},{20,12},{28,20},{1,9},{9,17},{17,25},{... | collective-permute-start | bytes 786440 | tf_op jit(solution)/shard_map/ppermute | solution.py:647
  29.0 0.1 collective-permute-start.3
  29.1 2.0 %collective-permute-done.5.refs_2_ = f32[16,16,384]{2,1,0:T(8,128)S(1)} collective-permute-done((f32[16,16,384]{2,1,0:T(8,128)S(1)}, f32[16,16,384]{2,1,0:T(8,128)S(1)}, u32[]{:S(2)}, u32[]{:S(2)}) %collective-permute-start.5) | collective-permute-done | bytes 393248 | tf_op jit(solution)/shard_map/ppermute | solution.py:647
  31.1 2.7 %stream_faces.4.after_ref.refs_6_ = f32[5,4,16,384]{3,2,1,0:T(8,128)S(1)} custom-call(f32[5,4,32,512]{3,2,1,0:T(8,128)S(1)} %copy-done, f32[21,16,384]{2,1,0:T(8,128)S(1)} %collective-permute-done.2.pair_ref.refs_1_, f32[16,16,384]{2,1,0:T(8,128)S(1)} %collective-permute-done.5.refs_2_, s32[4,32,512]{2,1,0:T(8,128)S(1)} %copy-done.1, ...), custom_call_target="tpu_custom_call" | custom-call | flops 1800000000 | bytes 5399999 | tf_op jit(solution)/shard_map/stream_faces/pallas_call | solution.py:431
  33.8 0.0 collective-permute-done.4.pair_ref.refs_1_
  33.8 4.4 %collective-permute-start.9 = (f32[16,32,128]{2,1,0:T(8,128)S(1)}, f32[16,32,128]{2,1,0:T(8,128)S(1)}, u32[]{:S(2)}, u32[]{:S(2)}) collective-permute-start(f32[16,32,128]{2,1,0:T(8,128)S(1)} %pass_planes.6.after_ref), channel_id=1, source_target_pairs={{0,8},{8,16},{16,24},{12,4},{20,12},{28,20},{1,9},{9,17},{17,25},{... | collective-permute-start | bytes 786440 | tf_op jit(solution)/shard_map/ppermute | solution.py:647
  38.2 0.0 collective-permute-done.3.pair_ref.refs_1_
  38.3 3.5 %collective-permute-start.6 = (f32[16,16,128]{2,1,0:T(8,128)S(1)}, f32[16,16,128]{2,1,0:T(8,128)S(1)}, u32[]{:S(2)}, u32[]{:S(2)}) collective-permute-start(f32[16,16,128]{2,1,0:T(8,128)S(1)} %pass_planes.7.refs_5_), channel_id=1, source_target_pairs={{0,8},{8,16},{16,24},{12,4},{20,12},{28,20},{1,9},{9,17},{17,25},{... | collective-permute-start | bytes 393224 | tf_op jit(solution)/shard_map/ppermute | solution.py:647
  41.8 0.0 collective-permute-done.8.refs_2_
  41.8 1.8 %stream_faces.5.refs_5_.refs_7_ = f32[5,4,16,256]{3,2,1,0:T(8,128)S(1)} custom-call(f32[5,4,32,512]{3,2,1,0:T(8,128)S(1)} %copy-done, f32[21,16,256]{2,1,0:T(8,128)S(1)} %collective-permute-done.1.pair_ref.refs_1_, f32[16,16,256]{2,1,0:T(8,128)S(1)} %collective-permute-done.8.refs_2_, s32[4,32,512]{2,1,0:T(8,128)S(1)} %copy-done.1, ...), custom_call_target="tpu_custom_call" | custom-call | flops 1200000000 | bytes 3600000 | tf_op jit(solution)/shard_map/stream_faces/pallas_call | solution.py:431
  43.6 0.0 collective-permute-done.9.refs_2_
  43.6 1.8 %stream_faces.6.refs_8_ = f32[5,4,32,128]{3,2,1,0:T(8,128)S(1)} custom-call(f32[5,4,32,512]{3,2,1,0:T(8,128)S(1)} %copy-done, f32[21,32,128]{2,1,0:T(8,128)S(1)} %collective-permute-done.4.pair_ref.refs_1_, f32[16,32,128]{2,1,0:T(8,128)S(1)} %collective-permute-done.9.refs_2_, s32[4,32,512]{2,1,0:T(8,128)S(1)} %copy-done.1, ...), custom_call_target="tpu_custom_call" | custom-call | flops 1200000000 | bytes 3600000 | tf_op jit(solution)/shard_map/stream_faces/pallas_call | solution.py:431
  45.4 0.0 collective-permute-done.6.refs_2_
  45.4 0.0 collective-permute-done.7.refs_5_
  45.4 2.4 %stream_faces.7 = f32[5,4,32,512]{3,2,1,0:T(8,128)} custom-call(f32[5,4,32,512]{3,2,1,0:T(8,128)S(1)} %copy-done, f32[21,16,128]{2,1,0:T(8,128)S(1)} %collective-permute-done.3.pair_ref.refs_1_, f32[16,16,128]{2,1,0:T(8,128)S(1)} %collective-permute-done.6.refs_2_, s32[4,32,512]{2,1,0:T(8,128)S(1)} %copy-done.1, ...), custom_call_target="tpu_custom_call" | custom-call | flops 600000000 | bytes 1800000 | tf_op jit(solution)/shard_map/stream_faces/pallas_call | solution.py:431
  (8 shorter events, 0.3 us)
Async XLA Ops:
  0.0 5.1 %copy-start.3 = (f32[64,2048]{1,0:T(8,128)S(1)}, f32[64,2048]{1,0:T(8,128)}, u32[]{:S(2)}) copy-start(f32[64,2048]{1,0:T(8,128)} %constant.5.clone.outer_ref) | copy-start | bytes 1572868
  0.0 5.1 %copy-start.4 = (f32[64,128]{1,0:T(8,128)S(1)}, f32[64,128]{1,0:T(8,128)}, u32[]{:S(2)}) copy-start(f32[64,128]{1,0:T(8,128)} %constant.4.clone.inner_ref) | copy-start | bytes 98308
  0.0 5.0 %copy-start.5 = (f32[1024]{0:T(1024)S(1)}, f32[1024]{0:T(1024)}, u32[]{:S(2)}) copy-start(f32[1024]{0:T(1024)} %param.9) | copy-start | bytes 12292
  0.0 5.1 %collective-permute-start = (f32[5,4,32,512]{3,2,1,0:T(8,128)}, f32[5,4,32,512]{3,2,1,0:T(8,128)S(1)}, u32[]{:S(2)}, u32[]{:S(2)}) collective-permute-start(f32[5,4,32,512]{3,2,1,0:T(8,128)} %refs_0_.7), channel_id=1, source_target_pairs={{0,1},{1,0},{2,3},{3,2},{4,5},{5,4},{6,7},{7,6},{8,9},{9,8},{10,11... | collective-permute-start | bytes 3932168 | tf_op jit(solution)/shard_map/ppermute | solution.py:609
  2.4 15.7 %collective-permute-start.2 = (f32[21,16,384]{2,1,0:T(8,128)S(1)}, f32[21,16,384]{2,1,0:T(8,128)S(1)}, u32[]{:S(2)}, u32[]{:S(2)}) collective-permute-start(f32[21,16,384]{2,1,0:T(8,128)S(1)} %bring_planes.5), channel_id=1, source_target_pairs={{0,4},{4,0},{8,12},{12,8},{16,20},{20,16},{24,28},{28,24},{1,5},{5... | collective-permute-start | bytes 1548296 | tf_op jit(solution)/shard_map/ppermute | solution.py:631
  5.1 1.3 %copy-start = (f32[5,4,32,512]{3,2,1,0:T(8,128)S(1)}, f32[5,4,32,512]{3,2,1,0:T(8,128)}, u32[]{:S(2)}) copy-start(f32[5,4,32,512]{3,2,1,0:T(8,128)} %refs_0_.7) | copy-start | bytes 3932164
  6.4 5.0 %copy-start.2 = (s32[4,32,512]{2,1,0:T(8,128)S(1)}, s32[4,32,512]{2,1,0:T(8,128)}, u32[]{:S(2)}) copy-start(s32[4,32,512]{2,1,0:T(8,128)} %mask_ref.7) | copy-start | bytes 786436
  9.8 35.6 %collective-permute-start.7 = (f32[5,4,32,512]{3,2,1,0:T(8,128)S(1)}, f32[5,4,32,512]{3,2,1,0:T(8,128)S(1)}, u32[]{:S(2)}, u32[]{:S(2)}) collective-permute-start(f32[5,4,32,512]{3,2,1,0:T(8,128)S(1)} %get-tuple-element.14), channel_id=1, source_target_pairs={{0,2},{1,3},{2,0},{3,1},{4,6},{5,7},{6,4},{7,5},{8,10},{9,11},{10,... | collective-permute-start | bytes 3932168 | tf_op jit(solution)/shard_map/ppermute | solution.py:609
  11.4 2.9 %copy-start.1 = (s32[4,32,512]{2,1,0:T(8,128)S(1)}, s32[4,32,512]{2,1,0:T(8,128)}, u32[]{:S(2)}) copy-start(s32[4,32,512]{2,1,0:T(8,128)} %refs_3_.7) | copy-start | bytes 786436
  14.4 11.1 %collective-permute-start.1 = (f32[21,16,256]{2,1,0:T(8,128)S(1)}, f32[21,16,256]{2,1,0:T(8,128)S(1)}, u32[]{:S(2)}, u32[]{:S(2)}) collective-permute-start(f32[21,16,256]{2,1,0:T(8,128)S(1)} %bring_planes.4.after_ref), channel_id=1, source_target_pairs={{0,4},{4,0},{8,12},{12,8},{16,20},{20,16},{24,28},{28,24},{1,5},{5... | collective-permute-start | bytes 1032200 | tf_op jit(solution)/shard_map/ppermute | solution.py:642
  18.1 12.9 %collective-permute-start.5 = (f32[16,16,384]{2,1,0:T(8,128)S(1)}, f32[16,16,384]{2,1,0:T(8,128)S(1)}, u32[]{:S(2)}, u32[]{:S(2)}) collective-permute-start(f32[16,16,384]{2,1,0:T(8,128)S(1)} %pass_planes.4.after_ref), channel_id=1, source_target_pairs={{0,8},{8,16},{16,24},{12,4},{20,12},{28,20},{1,9},{9,17},{17,25},{... | collective-permute-start | bytes 1179656 | tf_op jit(solution)/shard_map/ppermute | solution.py:647
  21.7 12.1 %collective-permute-start.4 = (f32[21,32,128]{2,1,0:T(8,128)S(1)}, f32[21,32,128]{2,1,0:T(8,128)S(1)}, u32[]{:S(2)}, u32[]{:S(2)}) collective-permute-start(f32[21,32,128]{2,1,0:T(8,128)S(1)} %bring_planes.6.after_ref), channel_id=1, source_target_pairs={{0,4},{4,0},{8,12},{12,8},{16,20},{20,16},{24,28},{28,24},{1,5},{5... | collective-permute-start | bytes 1032200 | tf_op jit(solution)/shard_map/ppermute | solution.py:642
  25.5 16.3 %collective-permute-start.8 = (f32[16,16,256]{2,1,0:T(8,128)S(1)}, f32[16,16,256]{2,1,0:T(8,128)S(1)}, u32[]{:S(2)}, u32[]{:S(2)}) collective-permute-start(f32[16,16,256]{2,1,0:T(8,128)S(1)} %pass_planes.5.after_ref), channel_id=1, source_target_pairs={{0,8},{8,16},{16,24},{12,4},{20,12},{28,20},{1,9},{9,17},{17,25},{... | collective-permute-start | bytes 786440 | tf_op jit(solution)/shard_map/ppermute | solution.py:647
  29.0 9.2 %collective-permute-start.3 = (f32[21,16,128]{2,1,0:T(8,128)S(1)}, f32[21,16,128]{2,1,0:T(8,128)S(1)}, u32[]{:S(2)}, u32[]{:S(2)}) collective-permute-start(f32[21,16,128]{2,1,0:T(8,128)S(1)} %bring_planes.7.refs_5_), channel_id=1, source_target_pairs={{0,4},{4,0},{8,12},{12,8},{16,20},{20,16},{24,28},{28,24},{1,5},{5... | collective-permute-start | bytes 516104 | tf_op jit(solution)/shard_map/ppermute | solution.py:642
  33.8 9.8 %collective-permute-start.9 = (f32[16,32,128]{2,1,0:T(8,128)S(1)}, f32[16,32,128]{2,1,0:T(8,128)S(1)}, u32[]{:S(2)}, u32[]{:S(2)}) collective-permute-start(f32[16,32,128]{2,1,0:T(8,128)S(1)} %pass_planes.6.after_ref), channel_id=1, source_target_pairs={{0,8},{8,16},{16,24},{12,4},{20,12},{28,20},{1,9},{9,17},{17,25},{... | collective-permute-start | bytes 786440 | tf_op jit(solution)/shard_map/ppermute | solution.py:647
  38.3 7.1 %collective-permute-start.6 = (f32[16,16,128]{2,1,0:T(8,128)S(1)}, f32[16,16,128]{2,1,0:T(8,128)S(1)}, u32[]{:S(2)}, u32[]{:S(2)}) collective-permute-start(f32[16,16,128]{2,1,0:T(8,128)S(1)} %pass_planes.7.refs_5_), channel_id=1, source_target_pairs={{0,8},{8,16},{16,24},{12,4},{20,12},{28,20},{1,9},{9,17},{17,25},{... | collective-permute-start | bytes 393224 | tf_op jit(solution)/shard_map/ppermute | solution.py:647

commit v8 on v6

--- a/solution.py
+++ b/solution.py
@@ -290,8 +290,8 @@
         result = out_ref
     else:
         sum_ref, other_refs, refs = refs[0], refs[1 : 1 + len(others)], refs[1 + len(others) :]
-        out_ref, dq_s, df_s, both_s, alpha_s, result, sem, other_sem = refs[:8]
-        staged = refs[8:]
+        _, out_ref, dq_s, df_s, both_s, alpha_s, result, sem, other_sem = refs[:9]
+        staged = refs[9:]
     fields, depth, _, _ = state_ref.shape
     start, rows_y, start_lane, width = part
     stride = depth
@@ -436,7 +436,7 @@
         copy.wait()
 
 
-def stream_part(state, pair, far, mask_x, part, base, after=None, arrived=None, others=None):
+def stream_part(state, pair, far, mask_x, part, base, after, arrived=None, others=None, chained=False):
     fields, depth, _, _ = state.shape
     _, rows_y, _, width = part
     tiles = rows_y * width // (ROWS * LANES)
@@ -454,31 +454,28 @@
         vregs(tiles, depth + 1),
     ]
     inputs = [state, pair, far, mask_x, base]
-    places_in = [PLACE] * len(inputs)
     if others is None:
-        inputs.append(after)
-        places_in.append(ANYWHERE)
         places = None
         target, target_shape = PLACE, shape_of(*cells(part))
     else:
         places = [place for place, _ in others]
         inputs += [arrived] + [array for _, array in others]
-        places_in = [PLACE] * len(inputs)
         target, target_shape = HBM, shape_of(*state.shape)
         scratch += [
             pltpu.VMEM(cells(part), jnp.float32),
             pltpu.SemaphoreType.DMA((tiles,)),
-            pltpu.SemaphoreType.DMA((len(others),)),
+            pltpu.SemaphoreType.DMA((max(1, len(others)),)),
         ] + [pltpu.VMEM(cells(place), jnp.float32) for place in places]
     return call(
         functools.partial(stream_kernel, part, places),
         "stream_faces",
         0.3 * tiles,
-        places_in,
+        [PLACE] * len(inputs) + [HBM if chained else ANYWHERE],
         target,
         target_shape,
         scratch,
-    )(*inputs)
+        {len(inputs): 0} if chained else None,
+    )(*inputs, after)
 
 
 def circulant_tables(span):
@@ -674,7 +671,7 @@
     sums, lines = away_part(band, state, core, masks)
     arrived = sum(flip(part_sum, mask) for part_sum, mask in zip(sums, masks))
     half = depth // 2
-    fars, others = [], []
+    fars = []
 
     def exchange(c, after):
         brick = bring_part(state, mask_x, parts[c], after)
@@ -686,10 +683,8 @@
         fars.append(lax.ppermute(planes, "gx", carry))
         return planes
 
-    def stream(c, after):
-        done = stream_part(state, pairs[c], fars[c], mask_x, parts[c], base, after)
-        others.append((parts[c], done))
-        return done
+    def stream(c, after, *rest):
+        return stream_part(state, pairs[c], fars[c], mask_x, parts[c], base, after, *rest)
 
     acc_low = wall_part(state, mask_y, 0, half, lines[0])
     after = exchange(1, acc_low)
@@ -697,12 +692,11 @@
     after = exchange(2, hand_on(0, acc_high))
     base = home_part(band, lines, acc_low, acc_high, after)
     after = exchange(3, hand_on(1, base))
-    after = hand_on(2, stream(0, after))
-    after = hand_on(3, after)
-    stream(2, stream(1, after))
-    return stream_part(
-        state, pairs[3], fars[3], mask_x, parts[3], base, arrived=arrived, others=others
-    )
+    early = stream(0, after)
+    after = hand_on(3, hand_on(2, early))
+    out = stream(1, after, arrived, [])
+    out = stream(2, out, arrived, [], True)
+    return stream(3, out, arrived, [(parts[0], early)], True)
 
 
 def solution(mesh):

time: 47.6 us -> 48.5 us (1.019)
  Pallas kernels: 23.1 us -> 24 us
    pallas_call x4, Pallas kernels: 8.71 us -> 9.59 us  [stream_part(): call(functools.partial(stream_kernel, part, places), 'stream_faces', 0.3...]
  transfers between devices with their start and end apart: 10 -> 10, of which waited for: 2 -> 2; matrix products, arithmetic and copies ran while one was open for 0% -> 0% of each run, Pallas kernels for 44% -> 46%
where the time goes in v8:
time: 48.5 us; the launch traced here: 48.3 us
  Pallas kernels  24 us (49%)
  starting transfers between devices  20.8 us (43%)
  waiting for transfers between devices  2.69 us (6%)
  local copies, waits for them, and re-layouts  0.59 us (1%)
    ppermute x4, starting transfers between devices, hand_on(): fars.append(lax.ppermute(planes, 'gx', carry))  15.3 us
    pallas_call x4, Pallas kernels, stream_part(): call(functools.partial(stream_kernel, part, places), 'stream_faces', 0.3...  9.59 us
    pallas_call x2, Pallas kernels, wall_part(): call(kernel, 'wall_faces', 5.0 * count / depth, [PLACE, PLACE, ANYWHERE],...  5.81 us
    pallas_call x1, Pallas kernels, away_part(): call(functools.partial(away_kernel, masks), 'span_away', 3.0, [PLACE] * 4...  3.41 us
    ppermute x1, starting transfers between devices, per_device(): pairs = [lax.ppermute(brick, 'gx', swap)]  2.57 us
    pallas_call x1, Pallas kernels, home_part(): call(home_kernel, 'span_home', 2.0, [PLACE] * 6 + [ANYWHERE], PLACE, shap...  2.2 us
    ppermute x2, starting transfers between devices, flip(): return lax.ppermute(array, 'gz', [(g, g ^ bit) for g in range(groups)])  2.04 us
    pallas_call x1, Pallas kernels, pack_part(): call(functools.partial(pack_kernel, parts), 'pack_bricks', 1.0, [HBM, HBM...  1.93 us
  transfers between devices with their start and end apart: 10, of which 2 were waited for; matrix products, arithmetic and copies ran while one was open for 0% of the time, Pallas kernels for 46%

profile of v8, /device:TPU:0, one launch (start us, length us, event | category | flops | bytes accessed | tf_op | source)
XLA Modules:
  0.0 48.3 jit_solution(12788495461184818681)
XLA Ops:
  0.0 0.5 collective-permute-start
  0.5 0.0 copy-start.5
  0.5 0.0 copy-start.3
  0.5 0.0 copy-start.4
  0.5 1.9 %pack_bricks.1 = f32[21,16,384]{2,1,0:T(8,128)} custom-call(f32[20,32,512]{2,1,0:T(8,128)} %bitcast.1, s32[4,32,512]{2,1,0:T(8,128)} %refs_3_.7), custom_call_target="tpu_custom_call" | custom-call | flops 1000000000 | bytes 3000000 | tf_op jit(solution)/shard_map/pack_bricks/pallas_call | solution.py:227
  2.4 2.6 %collective-permute-start.2 = (f32[21,16,384]{2,1,0:T(8,128)}, f32[21,16,384]{2,1,0:T(8,128)S(1)}, u32[]{:S(2)}, u32[]{:S(2)}) collective-permute-start(f32[21,16,384]{2,1,0:T(8,128)} %pack_bricks.1), channel_id=1, source_target_pairs={{0,4},{4,0},{8,12},{12,8},{16,20},{20,16},{24,28},{28,24},{1,5},{5... | collective-permute-start | bytes 1548296 | tf_op jit(solution)/shard_map/ppermute | solution.py:667
  5.0 0.0 copy-done.5
  5.0 0.1 reshape.6.filter_ref
  5.0 0.0 copy-start
  5.0 0.0 collective-permute-done.after_ref.core_ref
  5.1 0.0 copy-done.3
  5.1 0.0 copy-done.4
  5.1 0.8 %circulant_band.1 = (bf16[256,2560]{1,0:T(8,128)(2,1)S(1)}, bf16[256,2560]{1,0:T(8,128)(2,1)S(1)}) custom-call(f32[32,32]{1,0:T(8,128)S(1)} %reshape.6.filter_ref, f32[64,128]{1,0:T(8,128)S(1)} %copy-done.4, f32[64,2048]{1,0:T(8,128)S(1)} %copy-done.3, f32[5,4,32,512]{3,2,1,0:T(8,128)S(1)} %collective-permute-done.after_ref.core_ref), custom_call_target="tpu_custom_call" | custom-call | flops 1000000000 | bytes 3000000 | tf_op jit(solution)/shard_map/circulant_band/pallas_call | solution.py:547
  5.9 0.5 %copy-done = f32[5,4,32,512]{3,2,1,0:T(8,128)S(1)} copy-done((f32[5,4,32,512]{3,2,1,0:T(8,128)S(1)}, f32[5,4,32,512]{3,2,1,0:T(8,128)}, u32[]{:S(2)}) %copy-start) | copy-done | bytes 1310744
  6.4 0.0 copy-start.2
  6.4 3.4 %span_away.1 = (f32[5,4,32,512]{3,2,1,0:T(8,128)S(1)}, bf16[640,1024]{1,0:T(8,128)(2,1)S(1)}, bf16[640,1024]{1,0:T(8,128)(2,1)S(1)}) custom-call(bf16[256,2560]{1,0:T(8,128)(2,1)S(1)} %get-tuple-element.10.high_ref, bf16[256,2560]{1,0:T(8,128)(2,1)S(1)} %get-tuple-element.11.low_ref, f32[5,4,32,512]{3,2,1,0:T(8,128)S(1)} %copy-done, ...), custom_call_target="tpu_custom_call" | custom-call | flops 3000000000 | bytes 9000000 | tf_op jit(solution)/shard_map/span_away/pallas_call | solution.py:608
  9.8 1.6 %collective-permute-start.7 = (f32[5,4,32,512]{3,2,1,0:T(8,128)S(1)}, f32[5,4,32,512]{3,2,1,0:T(8,128)S(1)}, u32[]{:S(2)}, u32[]{:S(2)}) collective-permute-start(f32[5,4,32,512]{3,2,1,0:T(8,128)S(1)} %get-tuple-element.14), channel_id=1, source_target_pairs={{0,2},{1,3},{2,0},{3,1},{4,6},{5,7},{6,4},{7,5},{8,10},{9,11},{10,... | collective-permute-start | bytes 3932168 | tf_op jit(solution)/shard_map/ppermute | solution.py:648
  11.4 0.0 copy-done.2
  11.4 0.0 copy-start.1
  11.4 2.9 %wall_faces.2.after_ref.first_ref = f32[5,2,32,512]{3,2,1,0:T(8,128)S(1)} custom-call(f32[5,4,32,512]{3,2,1,0:T(8,128)S(1)} %copy-done, s32[4,32,512]{2,1,0:T(8,128)S(1)} %copy-done.2, bf16[640,1024]{1,0:T(8,128)(2,1)S(1)} %get-tuple-element.12.after_ref.xh), custom_call_target="tpu_custom_call" | custom-call | flops 2500000000 | bytes 7500000 | tf_op jit(solution)/shard_map/wall_faces/pallas_call | solution.py:190
  14.3 0.0 copy-done.1
  14.3 0.7 %collective-permute-start.1 = (f32[21,16,256]{2,1,0:T(8,128)S(1)}, f32[21,16,256]{2,1,0:T(8,128)S(1)}, u32[]{:S(2)}, u32[]{:S(2)}) collective-permute-start(f32[21,16,256]{2,1,0:T(8,128)S(1)} %bring_planes.3.after_ref), channel_id=1, source_target_pairs={{0,4},{4,0},{8,12},{12,8},{16,20},{20,16},{24,28},{28,24},{1,5},{5... | collective-permute-start | bytes 1032200 | tf_op jit(solution)/shard_map/ppermute | solution.py:678
  15.1 2.9 %wall_faces.3.after_ref.second_ref = f32[5,2,32,512]{3,2,1,0:T(8,128)S(1)} custom-call(f32[5,4,32,512]{3,2,1,0:T(8,128)S(1)} %copy-done, s32[4,32,512]{2,1,0:T(8,128)S(1)} %copy-done.2, f32[21,16,256]{2,1,0:T(8,128)S(1)} %bring_planes.3.after_ref), custom_call_target="tpu_custom_call" | custom-call | flops 2500000000 | bytes 7500000 | tf_op jit(solution)/shard_map/wall_faces/pallas_call | solution.py:190
  18.0 0.0 collective-permute-done.2.pair_ref.refs_1_
  18.0 3.7 %collective-permute-start.5 = (f32[16,16,384]{2,1,0:T(8,128)S(1)}, f32[16,16,384]{2,1,0:T(8,128)S(1)}, u32[]{:S(2)}, u32[]{:S(2)}) collective-permute-start(f32[16,16,384]{2,1,0:T(8,128)S(1)} %pass_planes.4.after_ref), channel_id=1, source_target_pairs={{0,8},{8,16},{16,24},{12,4},{20,12},{28,20},{1,9},{9,17},{17,25},{... | collective-permute-start | bytes 1179656 | tf_op jit(solution)/shard_map/ppermute | solution.py:683
  21.8 0.1 collective-permute-start.4
  21.9 2.2 %span_home.1.after_ref.refs_4_ = f32[5,4,32,512]{3,2,1,0:T(8,128)S(1)} custom-call(bf16[256,2560]{1,0:T(8,128)(2,1)S(1)} %get-tuple-element.10.high_ref, bf16[256,2560]{1,0:T(8,128)(2,1)S(1)} %get-tuple-element.11.low_ref, bf16[640,1024]{1,0:T(8,128)(2,1)S(1)} %get-tuple-element.12.after_ref.xh, bf16[640,1024]{1,0:T(8,128)(2,1)S(1)} %get-tuple-element.13.xl, ...), custom_call_target="tpu_custom_call" | custom-call | flops 2000000000 | bytes 6000000 | tf_op jit(solution)/shard_map/span_home/pallas_call | solution.py:630
  24.1 1.3 %collective-permute-done.1.pair_ref.refs_1_ = f32[21,16,256]{2,1,0:T(8,128)S(1)} collective-permute-done((f32[21,16,256]{2,1,0:T(8,128)S(1)}, f32[21,16,256]{2,1,0:T(8,128)S(1)}, u32[]{:S(2)}, u32[]{:S(2)}) %collective-permute-start.1) | collective-permute-done | bytes 344096 | tf_op jit(solution)/shard_map/ppermute | solution.py:678
  25.4 3.7 %collective-permute-start.9 = (f32[16,16,256]{2,1,0:T(8,128)S(1)}, f32[16,16,256]{2,1,0:T(8,128)S(1)}, u32[]{:S(2)}, u32[]{:S(2)}) collective-permute-start(f32[16,16,256]{2,1,0:T(8,128)S(1)} %pass_planes.5.after_ref), channel_id=1, source_target_pairs={{0,8},{8,16},{16,24},{12,4},{20,12},{28,20},{1,9},{9,17},{17,25},{... | collective-permute-start | bytes 786440 | tf_op jit(solution)/shard_map/ppermute | solution.py:683
  29.2 0.1 collective-permute-start.3
  29.2 1.4 %collective-permute-done.5.refs_2_ = f32[16,16,384]{2,1,0:T(8,128)S(1)} collective-permute-done((f32[16,16,384]{2,1,0:T(8,128)S(1)}, f32[16,16,384]{2,1,0:T(8,128)S(1)}, u32[]{:S(2)}, u32[]{:S(2)}) %collective-permute-start.5) | collective-permute-done | bytes 393248 | tf_op jit(solution)/shard_map/ppermute | solution.py:683
  30.6 2.7 %stream_faces.4.after_ref.refs_6_ = f32[5,4,16,384]{3,2,1,0:T(8,128)S(1)} custom-call(f32[5,4,32,512]{3,2,1,0:T(8,128)S(1)} %copy-done, f32[21,16,384]{2,1,0:T(8,128)S(1)} %collective-permute-done.2.pair_ref.refs_1_, f32[16,16,384]{2,1,0:T(8,128)S(1)} %collective-permute-done.5.refs_2_, s32[4,32,512]{2,1,0:T(8,128)S(1)} %copy-done.1, ...), custom_call_target="tpu_custom_call" | custom-call | flops 1800000000 | bytes 5399999 | tf_op jit(solution)/shard_map/stream_faces/pallas_call | solution.py:469
  33.4 0.0 collective-permute-done.4.pair_ref.refs_1_
  33.4 4.4 %collective-permute-start.8 = (f32[16,32,128]{2,1,0:T(8,128)S(1)}, f32[16,32,128]{2,1,0:T(8,128)S(1)}, u32[]{:S(2)}, u32[]{:S(2)}) collective-permute-start(f32[16,32,128]{2,1,0:T(8,128)S(1)} %pass_planes.6.after_ref), channel_id=1, source_target_pairs={{0,8},{8,16},{16,24},{12,4},{20,12},{28,20},{1,9},{9,17},{17,25},{... | collective-permute-start | bytes 786440 | tf_op jit(solution)/shard_map/ppermute | solution.py:683
  37.8 0.0 collective-permute-done.3.pair_ref.refs_1_
  37.9 3.5 %collective-permute-start.6 = (f32[16,16,128]{2,1,0:T(8,128)S(1)}, f32[16,16,128]{2,1,0:T(8,128)S(1)}, u32[]{:S(2)}, u32[]{:S(2)}) collective-permute-start(f32[16,16,128]{2,1,0:T(8,128)S(1)} %pass_planes.7.refs_6_), channel_id=1, source_target_pairs={{0,8},{8,16},{16,24},{12,4},{20,12},{28,20},{1,9},{9,17},{17,25},{... | collective-permute-start | bytes 393224 | tf_op jit(solution)/shard_map/ppermute | solution.py:683
  41.3 0.0 collective-permute-done.9.refs_2_
  41.4 0.0 collective-permute-done.7.refs_5_
  41.4 2.5 %stream_faces.5.refs_6_ = f32[5,4,32,512]{3,2,1,0:T(8,128)} custom-call(f32[5,4,32,512]{3,2,1,0:T(8,128)S(1)} %copy-done, f32[21,16,256]{2,1,0:T(8,128)S(1)} %collective-permute-done.1.pair_ref.refs_1_, f32[16,16,256]{2,1,0:T(8,128)S(1)} %collective-permute-done.9.refs_2_, s32[4,32,512]{2,1,0:T(8,128)S(1)} %copy-done.1, ...), custom_call_target="tpu_custom_call" | custom-call | flops 1200000000 | bytes 3600000 | tf_op jit(solution)/shard_map/stream_faces/pallas_call | solution.py:469
  43.9 0.0 collective-permute-done.8.refs_2_
  43.9 2.5 %stream_faces.6.refs_7_ = f32[5,4,32,512]{3,2,1,0:T(8,128)} custom-call(f32[5,4,32,512]{3,2,1,0:T(8,128)S(1)} %copy-done, f32[21,32,128]{2,1,0:T(8,128)S(1)} %collective-permute-done.4.pair_ref.refs_1_, f32[16,32,128]{2,1,0:T(8,128)S(1)} %collective-permute-done.8.refs_2_, s32[4,32,512]{2,1,0:T(8,128)S(1)} %copy-done.1, ...), custom_call_target="tpu_custom_call", output_to_operand_aliasing={{}: (6, {})} | custom-call | flops 1200000000 | bytes 3600000 | tf_op jit(solution)/shard_map/stream_faces/pallas_call | solution.py:469
  46.4 0.0 collective-permute-done.6.refs_2_
  46.4 1.8 %stream_faces.7 = f32[5,4,32,512]{3,2,1,0:T(8,128)} custom-call(f32[5,4,32,512]{3,2,1,0:T(8,128)S(1)} %copy-done, f32[21,16,128]{2,1,0:T(8,128)S(1)} %collective-permute-done.3.pair_ref.refs_1_, f32[16,16,128]{2,1,0:T(8,128)S(1)} %collective-permute-done.6.refs_2_, s32[4,32,512]{2,1,0:T(8,128)S(1)} %copy-done.1, ...), custom_call_target="tpu_custom_call", output_to_operand_aliasing={{}: (7, {})} | custom-call | flops 600000000 | bytes 1800000 | tf_op jit(solution)/shard_map/stream_faces/pallas_call | solution.py:469
  (7 shorter events, 0.2 us)
Async XLA Ops:
  0.0 5.0 %collective-permute-start = (f32[5,4,32,512]{3,2,1,0:T(8,128)}, f32[5,4,32,512]{3,2,1,0:T(8,128)S(1)}, u32[]{:S(2)}, u32[]{:S(2)}) collective-permute-start(f32[5,4,32,512]{3,2,1,0:T(8,128)} %refs_0_.7), channel_id=1, source_target_pairs={{0,1},{1,0},{2,3},{3,2},{4,5},{5,4},{6,7},{7,6},{8,9},{9,8},{10,11... | collective-permute-start | bytes 3932168 | tf_op jit(solution)/shard_map/ppermute | solution.py:648
  0.5 4.5 %copy-start.5 = (f32[1024]{0:T(1024)S(1)}, f32[1024]{0:T(1024)}, u32[]{:S(2)}) copy-start(f32[1024]{0:T(1024)} %param.9) | copy-start | bytes 12292
  0.5 4.6 %copy-start.3 = (f32[64,2048]{1,0:T(8,128)S(1)}, f32[64,2048]{1,0:T(8,128)}, u32[]{:S(2)}) copy-start(f32[64,2048]{1,0:T(8,128)} %constant.5.clone.outer_ref) | copy-start | bytes 1572868
  0.5 4.6 %copy-start.4 = (f32[64,128]{1,0:T(8,128)S(1)}, f32[64,128]{1,0:T(8,128)}, u32[]{:S(2)}) copy-start(f32[64,128]{1,0:T(8,128)} %constant.4.clone.inner_ref) | copy-start | bytes 98308
  2.4 15.6 %collective-permute-start.2 = (f32[21,16,384]{2,1,0:T(8,128)}, f32[21,16,384]{2,1,0:T(8,128)S(1)}, u32[]{:S(2)}, u32[]{:S(2)}) collective-permute-start(f32[21,16,384]{2,1,0:T(8,128)} %pack_bricks.1), channel_id=1, source_target_pairs={{0,4},{4,0},{8,12},{12,8},{16,20},{20,16},{24,28},{28,24},{1,5},{5... | collective-permute-start | bytes 1548296 | tf_op jit(solution)/shard_map/ppermute | solution.py:667
  5.0 1.3 %copy-start = (f32[5,4,32,512]{3,2,1,0:T(8,128)S(1)}, f32[5,4,32,512]{3,2,1,0:T(8,128)}, u32[]{:S(2)}) copy-start(f32[5,4,32,512]{3,2,1,0:T(8,128)} %refs_0_.7) | copy-start | bytes 3932164
  6.4 5.0 %copy-start.2 = (s32[4,32,512]{2,1,0:T(8,128)S(1)}, s32[4,32,512]{2,1,0:T(8,128)}, u32[]{:S(2)}) copy-start(s32[4,32,512]{2,1,0:T(8,128)} %mask_ref.8) | copy-start | bytes 786436
  9.8 31.6 %collective-permute-start.7 = (f32[5,4,32,512]{3,2,1,0:T(8,128)S(1)}, f32[5,4,32,512]{3,2,1,0:T(8,128)S(1)}, u32[]{:S(2)}, u32[]{:S(2)}) collective-permute-start(f32[5,4,32,512]{3,2,1,0:T(8,128)S(1)} %get-tuple-element.14), channel_id=1, source_target_pairs={{0,2},{1,3},{2,0},{3,1},{4,6},{5,7},{6,4},{7,5},{8,10},{9,11},{10,... | collective-permute-start | bytes 3932168 | tf_op jit(solution)/shard_map/ppermute | solution.py:648
  11.4 2.9 %copy-start.1 = (s32[4,32,512]{2,1,0:T(8,128)S(1)}, s32[4,32,512]{2,1,0:T(8,128)}, u32[]{:S(2)}) copy-start(s32[4,32,512]{2,1,0:T(8,128)} %refs_3_.7) | copy-start | bytes 786436
  14.3 11.1 %collective-permute-start.1 = (f32[21,16,256]{2,1,0:T(8,128)S(1)}, f32[21,16,256]{2,1,0:T(8,128)S(1)}, u32[]{:S(2)}, u32[]{:S(2)}) collective-permute-start(f32[21,16,256]{2,1,0:T(8,128)S(1)} %bring_planes.3.after_ref), channel_id=1, source_target_pairs={{0,4},{4,0},{8,12},{12,8},{16,20},{20,16},{24,28},{28,24},{1,5},{5... | collective-permute-start | bytes 1032200 | tf_op jit(solution)/shard_map/ppermute | solution.py:678
  18.0 12.6 %collective-permute-start.5 = (f32[16,16,384]{2,1,0:T(8,128)S(1)}, f32[16,16,384]{2,1,0:T(8,128)S(1)}, u32[]{:S(2)}, u32[]{:S(2)}) collective-permute-start(f32[16,16,384]{2,1,0:T(8,128)S(1)} %pass_planes.4.after_ref), channel_id=1, source_target_pairs={{0,8},{8,16},{16,24},{12,4},{20,12},{28,20},{1,9},{9,17},{17,25},{... | collective-permute-start | bytes 1179656 | tf_op jit(solution)/shard_map/ppermute | solution.py:683
  21.8 11.5 %collective-permute-start.4 = (f32[21,32,128]{2,1,0:T(8,128)S(1)}, f32[21,32,128]{2,1,0:T(8,128)S(1)}, u32[]{:S(2)}, u32[]{:S(2)}) collective-permute-start(f32[21,32,128]{2,1,0:T(8,128)S(1)} %bring_planes.4.after_ref), channel_id=1, source_target_pairs={{0,4},{4,0},{8,12},{12,8},{16,20},{20,16},{24,28},{28,24},{1,5},{5... | collective-permute-start | bytes 1032200 | tf_op jit(solution)/shard_map/ppermute | solution.py:678
  25.4 15.9 %collective-permute-start.9 = (f32[16,16,256]{2,1,0:T(8,128)S(1)}, f32[16,16,256]{2,1,0:T(8,128)S(1)}, u32[]{:S(2)}, u32[]{:S(2)}) collective-permute-start(f32[16,16,256]{2,1,0:T(8,128)S(1)} %pass_planes.5.after_ref), channel_id=1, source_target_pairs={{0,8},{8,16},{16,24},{12,4},{20,12},{28,20},{1,9},{9,17},{17,25},{... | collective-permute-start | bytes 786440 | tf_op jit(solution)/shard_map/ppermute | solution.py:683
  29.2 8.7 %collective-permute-start.3 = (f32[21,16,128]{2,1,0:T(8,128)S(1)}, f32[21,16,128]{2,1,0:T(8,128)S(1)}, u32[]{:S(2)}, u32[]{:S(2)}) collective-permute-start(f32[21,16,128]{2,1,0:T(8,128)S(1)} %bring_planes.5.refs_5_), channel_id=1, source_target_pairs={{0,4},{4,0},{8,12},{12,8},{16,20},{20,16},{24,28},{28,24},{1,5},{5... | collective-permute-start | bytes 516104 | tf_op jit(solution)/shard_map/ppermute | solution.py:678
  33.4 10.5 %collective-permute-start.8 = (f32[16,32,128]{2,1,0:T(8,128)S(1)}, f32[16,32,128]{2,1,0:T(8,128)S(1)}, u32[]{:S(2)}, u32[]{:S(2)}) collective-permute-start(f32[16,32,128]{2,1,0:T(8,128)S(1)} %pass_planes.6.after_ref), channel_id=1, source_target_pairs={{0,8},{8,16},{16,24},{12,4},{20,12},{28,20},{1,9},{9,17},{17,25},{... | collective-permute-start | bytes 786440 | tf_op jit(solution)/shard_map/ppermute | solution.py:683
  37.9 8.6 %collective-permute-start.6 = (f32[16,16,128]{2,1,0:T(8,128)S(1)}, f32[16,16,128]{2,1,0:T(8,128)S(1)}, u32[]{:S(2)}, u32[]{:S(2)}) collective-permute-start(f32[16,16,128]{2,1,0:T(8,128)S(1)} %pass_planes.7.refs_6_), channel_id=1, source_target_pairs={{0,8},{8,16},{16,24},{12,4},{20,12},{28,20},{1,9},{9,17},{17,25},{... | collective-permute-start | bytes 393224 | tf_op jit(solution)/shard_map/ppermute | solution.py:683

commit v9 on v6

--- a/solution.py
+++ b/solution.py
@@ -659,9 +659,9 @@
     if width % (4 * LANES) == 0:
         lane = width // 4
         parts = [
+            (0, rows_all, 3 * lane, lane),
             (0, low, 0, 3 * lane),
             (low, low, 0, 2 * lane),
-            (0, rows_all, 3 * lane, lane),
             (low, low, 2 * lane, lane),
         ]
     else:

time: 47.6 us -> 50.6 us (1.063)
  waiting for transfers between devices: 2.69 us -> 6.99 us
  starting transfers between devices: 20.8 us -> 19.6 us
    ppermute x3, waiting for transfers between devices: 1.28 us -> 6.97 us  [exchange(): pairs.append(lax.ppermute(brick, 'gx', swap))]
    ppermute x4, waiting for transfers between devices: 1.4 us -> 0.01 us  [hand_on(): fars.append(lax.ppermute(planes, 'gx', carry))]
    ppermute x4, starting transfers between devices: 15.3 us -> 14 us  [hand_on(): fars.append(lax.ppermute(planes, 'gx', carry))]
  transfers between devices with their start and end apart: 10 -> 10, of which waited for: 2 -> 2; matrix products, arithmetic and copies ran while one was open for 0% -> 0% of each run, Pallas kernels for 44% -> 41%
where the time goes in v9:
time: 50.6 us; the launch traced here: 50.3 us
  Pallas kernels  23 us (45%)
  starting transfers between devices  19.6 us (39%)
  waiting for transfers between devices  6.99 us (14%)
  local copies, waits for them, and re-layouts  0.59 us (1%)
    ppermute x4, starting transfers between devices, hand_on(): fars.append(lax.ppermute(planes, 'gx', carry))  14 us
    pallas_call x4, Pallas kernels, stream_part(): call(functools.partial(stream_kernel, part, places), 'stream_faces', 0.3...  8.74 us
    ppermute x3, waiting for transfers between devices, exchange(): pairs.append(lax.ppermute(brick, 'gx', swap))  6.97 us
    pallas_call x2, Pallas kernels, wall_part(): call(kernel, 'wall_faces', 5.0 * count / depth, [PLACE, PLACE, ANYWHERE],...  5.81 us
    pallas_call x1, Pallas kernels, away_part(): call(functools.partial(away_kernel, masks), 'span_away', 3.0, [PLACE] * 4...  3.41 us
    ppermute x1, starting transfers between devices, per_device(): pairs = [lax.ppermute(brick, 'gx', swap)]  2.57 us
    pallas_call x1, Pallas kernels, home_part(): call(home_kernel, 'span_home', 2.0, [PLACE] * 6 + [ANYWHERE], PLACE, shap...  2.2 us
    ppermute x2, starting transfers between devices, flip(): return lax.ppermute(array, 'gz', [(g, g ^ bit) for g in range(groups)])  2.04 us
  transfers between devices with their start and end apart: 10, of which 2 were waited for; matrix products, arithmetic and copies ran while one was open for 0% of the time, Pallas kernels for 41%

profile of v9, /device:TPU:0, one launch (start us, length us, event | category | flops | bytes accessed | tf_op | source)
XLA Modules:
  0.0 50.3 jit_solution(587307094678048856)
XLA Ops:
  0.0 0.5 collective-permute-start
  0.5 0.0 copy-start.5
  0.5 0.0 copy-start.3
  0.5 0.0 copy-start.4
  0.5 1.8 %pack_bricks.1 = f32[21,32,128]{2,1,0:T(8,128)} custom-call(f32[20,32,512]{2,1,0:T(8,128)} %bitcast.1, s32[4,32,512]{2,1,0:T(8,128)} %refs_3_.7), custom_call_target="tpu_custom_call" | custom-call | flops 1000000000 | bytes 3000000 | tf_op jit(solution)/shard_map/pack_bricks/pallas_call | solution.py:227
  2.3 2.6 %collective-permute-start.2 = (f32[21,32,128]{2,1,0:T(8,128)}, f32[21,32,128]{2,1,0:T(8,128)S(1)}, u32[]{:S(2)}, u32[]{:S(2)}) collective-permute-start(f32[21,32,128]{2,1,0:T(8,128)} %pack_bricks.1), channel_id=1, source_target_pairs={{0,4},{4,0},{8,12},{12,8},{16,20},{20,16},{24,28},{28,24},{1,5},{5... | collective-permute-start | bytes 1032200 | tf_op jit(solution)/shard_map/ppermute | solution.py:670
  4.8 0.0 copy-done.5
  4.9 0.1 reshape.6.filter_ref
  4.9 0.0 copy-start
  4.9 0.0 collective-permute-done.after_ref.core_ref
  4.9 0.0 copy-done.3
  4.9 0.0 copy-done.4
  4.9 0.8 %circulant_band.1 = (bf16[256,2560]{1,0:T(8,128)(2,1)S(1)}, bf16[256,2560]{1,0:T(8,128)(2,1)S(1)}) custom-call(f32[32,32]{1,0:T(8,128)S(1)} %reshape.6.filter_ref, f32[64,128]{1,0:T(8,128)S(1)} %copy-done.4, f32[64,2048]{1,0:T(8,128)S(1)} %copy-done.3, f32[5,4,32,512]{3,2,1,0:T(8,128)S(1)} %collective-permute-done.after_ref.core_ref), custom_call_target="tpu_custom_call" | custom-call | flops 1000000000 | bytes 3000000 | tf_op jit(solution)/shard_map/circulant_band/pallas_call | solution.py:550
  5.7 0.5 copy-done
  6.2 0.0 copy-start.2
  6.2 3.4 %span_away.1 = (f32[5,4,32,512]{3,2,1,0:T(8,128)S(1)}, bf16[640,1024]{1,0:T(8,128)(2,1)S(1)}, bf16[640,1024]{1,0:T(8,128)(2,1)S(1)}) custom-call(bf16[256,2560]{1,0:T(8,128)(2,1)S(1)} %get-tuple-element.10.high_ref, bf16[256,2560]{1,0:T(8,128)(2,1)S(1)} %get-tuple-element.11.low_ref, f32[5,4,32,512]{3,2,1,0:T(8,128)S(1)} %copy-done, ...), custom_call_target="tpu_custom_call" | custom-call | flops 3000000000 | bytes 9000000 | tf_op jit(solution)/shard_map/span_away/pallas_call | solution.py:611
  9.7 1.6 %collective-permute-start.7 = (f32[5,4,32,512]{3,2,1,0:T(8,128)S(1)}, f32[5,4,32,512]{3,2,1,0:T(8,128)S(1)}, u32[]{:S(2)}, u32[]{:S(2)}) collective-permute-start(f32[5,4,32,512]{3,2,1,0:T(8,128)S(1)} %get-tuple-element.14), channel_id=1, source_target_pairs={{0,2},{1,3},{2,0},{3,1},{4,6},{5,7},{6,4},{7,5},{8,10},{9,11},{10,... | collective-permute-start | bytes 3932168 | tf_op jit(solution)/shard_map/ppermute | solution.py:651
  11.2 0.0 copy-done.2
  11.2 0.0 copy-start.1
  11.3 2.9 %wall_faces.2.after_ref.first_ref = f32[5,2,32,512]{3,2,1,0:T(8,128)S(1)} custom-call(f32[5,4,32,512]{3,2,1,0:T(8,128)S(1)} %copy-done, s32[4,32,512]{2,1,0:T(8,128)S(1)} %copy-done.2, bf16[640,1024]{1,0:T(8,128)(2,1)S(1)} %get-tuple-element.12.after_ref.xh), custom_call_target="tpu_custom_call" | custom-call | flops 2500000000 | bytes 7500000 | tf_op jit(solution)/shard_map/wall_faces/pallas_call | solution.py:190
  14.2 0.0 copy-done.1
  14.2 0.9 %collective-permute-start.1 = (f32[21,16,384]{2,1,0:T(8,128)S(1)}, f32[21,16,384]{2,1,0:T(8,128)S(1)}, u32[]{:S(2)}, u32[]{:S(2)}) collective-permute-start(f32[21,16,384]{2,1,0:T(8,128)S(1)} %bring_planes.3.after_ref), channel_id=1, source_target_pairs={{0,4},{4,0},{8,12},{12,8},{16,20},{20,16},{24,28},{28,24},{1,5},{5... | collective-permute-start | bytes 1548296 | tf_op jit(solution)/shard_map/ppermute | solution.py:681
  15.1 2.9 %wall_faces.3.after_ref.second_ref = f32[5,2,32,512]{3,2,1,0:T(8,128)S(1)} custom-call(f32[5,4,32,512]{3,2,1,0:T(8,128)S(1)} %copy-done, s32[4,32,512]{2,1,0:T(8,128)S(1)} %copy-done.2, f32[21,16,384]{2,1,0:T(8,128)S(1)} %bring_planes.3.after_ref), custom_call_target="tpu_custom_call" | custom-call | flops 2500000000 | bytes 7500000 | tf_op jit(solution)/shard_map/wall_faces/pallas_call | solution.py:190
  18.0 0.0 collective-permute-done.2.pair_ref.refs_1_
  18.0 3.5 %collective-permute-start.5 = (f32[16,32,128]{2,1,0:T(8,128)S(1)}, f32[16,32,128]{2,1,0:T(8,128)S(1)}, u32[]{:S(2)}, u32[]{:S(2)}) collective-permute-start(f32[16,32,128]{2,1,0:T(8,128)S(1)} %pass_planes.4.after_ref), channel_id=1, source_target_pairs={{0,8},{8,16},{16,24},{12,4},{20,12},{28,20},{1,9},{9,17},{17,25},{... | collective-permute-start | bytes 786440 | tf_op jit(solution)/shard_map/ppermute | solution.py:686
  21.6 0.1 collective-permute-start.4
  21.6 2.2 %span_home.1.after_ref.refs_4_ = f32[5,4,32,512]{3,2,1,0:T(8,128)S(1)} custom-call(bf16[256,2560]{1,0:T(8,128)(2,1)S(1)} %get-tuple-element.10.high_ref, bf16[256,2560]{1,0:T(8,128)(2,1)S(1)} %get-tuple-element.11.low_ref, bf16[640,1024]{1,0:T(8,128)(2,1)S(1)} %get-tuple-element.12.after_ref.xh, bf16[640,1024]{1,0:T(8,128)(2,1)S(1)} %get-tuple-element.13.xl, ...), custom_call_target="tpu_custom_call" | custom-call | flops 2000000000 | bytes 6000000 | tf_op jit(solution)/shard_map/span_home/pallas_call | solution.py:633
  23.9 5.1 %collective-permute-done.1.pair_ref.refs_1_ = f32[21,16,384]{2,1,0:T(8,128)S(1)} collective-permute-done((f32[21,16,384]{2,1,0:T(8,128)S(1)}, f32[21,16,384]{2,1,0:T(8,128)S(1)}, u32[]{:S(2)}, u32[]{:S(2)}) %collective-permute-start.1) | collective-permute-done | bytes 516128 | tf_op jit(solution)/shard_map/ppermute | solution.py:681
  28.9 3.5 %collective-permute-start.8 = (f32[16,16,384]{2,1,0:T(8,128)S(1)}, f32[16,16,384]{2,1,0:T(8,128)S(1)}, u32[]{:S(2)}, u32[]{:S(2)}) collective-permute-start(f32[16,16,384]{2,1,0:T(8,128)S(1)} %pass_planes.5.after_ref), channel_id=1, source_target_pairs={{0,8},{8,16},{16,24},{12,4},{20,12},{28,20},{1,9},{9,17},{17,25},{... | collective-permute-start | bytes 1179656 | tf_op jit(solution)/shard_map/ppermute | solution.py:686
  32.5 0.1 collective-permute-start.3
  32.6 0.0 collective-permute-done.5.refs_2_
  32.6 1.8 %stream_faces.4.after_ref.refs_6_ = f32[5,4,32,128]{3,2,1,0:T(8,128)S(1)} custom-call(f32[5,4,32,512]{3,2,1,0:T(8,128)S(1)} %copy-done, f32[21,32,128]{2,1,0:T(8,128)S(1)} %collective-permute-done.2.pair_ref.refs_1_, f32[16,32,128]{2,1,0:T(8,128)S(1)} %collective-permute-done.5.refs_2_, s32[4,32,512]{2,1,0:T(8,128)S(1)} %copy-done.1, ...), custom_call_target="tpu_custom_call" | custom-call | flops 1200000000 | bytes 3600000 | tf_op jit(solution)/shard_map/stream_faces/pallas_call | solution.py:473
  34.4 1.9 %collective-permute-done.4.pair_ref.refs_1_ = f32[21,16,256]{2,1,0:T(8,128)S(1)} collective-permute-done((f32[21,16,256]{2,1,0:T(8,128)S(1)}, f32[21,16,256]{2,1,0:T(8,128)S(1)}, u32[]{:S(2)}, u32[]{:S(2)}) %collective-permute-start.4) | collective-permute-done | bytes 344096 | tf_op jit(solution)/shard_map/ppermute | solution.py:681
  36.3 3.5 %collective-permute-start.9 = (f32[16,16,256]{2,1,0:T(8,128)S(1)}, f32[16,16,256]{2,1,0:T(8,128)S(1)}, u32[]{:S(2)}, u32[]{:S(2)}) collective-permute-start(f32[16,16,256]{2,1,0:T(8,128)S(1)} %pass_planes.6.after_ref), channel_id=1, source_target_pairs={{0,8},{8,16},{16,24},{12,4},{20,12},{28,20},{1,9},{9,17},{17,25},{... | collective-permute-start | bytes 786440 | tf_op jit(solution)/shard_map/ppermute | solution.py:686
  39.8 0.0 collective-permute-done.3.pair_ref.refs_1_
  39.9 3.5 %collective-permute-start.6 = (f32[16,16,128]{2,1,0:T(8,128)S(1)}, f32[16,16,128]{2,1,0:T(8,128)S(1)}, u32[]{:S(2)}, u32[]{:S(2)}) collective-permute-start(f32[16,16,128]{2,1,0:T(8,128)S(1)} %pass_planes.7.refs_5_), channel_id=1, source_target_pairs={{0,8},{8,16},{16,24},{12,4},{20,12},{28,20},{1,9},{9,17},{17,25},{... | collective-permute-start | bytes 393224 | tf_op jit(solution)/shard_map/ppermute | solution.py:686
  43.3 0.0 collective-permute-done.8.refs_2_
  43.4 2.7 %stream_faces.5.refs_5_.refs_7_ = f32[5,4,16,384]{3,2,1,0:T(8,128)S(1)} custom-call(f32[5,4,32,512]{3,2,1,0:T(8,128)S(1)} %copy-done, f32[21,16,384]{2,1,0:T(8,128)S(1)} %collective-permute-done.1.pair_ref.refs_1_, f32[16,16,384]{2,1,0:T(8,128)S(1)} %collective-permute-done.8.refs_2_, s32[4,32,512]{2,1,0:T(8,128)S(1)} %copy-done.1, ...), custom_call_target="tpu_custom_call" | custom-call | flops 1800000000 | bytes 5399999 | tf_op jit(solution)/shard_map/stream_faces/pallas_call | solution.py:473
  46.1 0.0 collective-permute-done.9.refs_2_
  46.1 1.8 %stream_faces.6.refs_8_ = f32[5,4,16,256]{3,2,1,0:T(8,128)S(1)} custom-call(f32[5,4,32,512]{3,2,1,0:T(8,128)S(1)} %copy-done, f32[21,16,256]{2,1,0:T(8,128)S(1)} %collective-permute-done.4.pair_ref.refs_1_, f32[16,16,256]{2,1,0:T(8,128)S(1)} %collective-permute-done.9.refs_2_, s32[4,32,512]{2,1,0:T(8,128)S(1)} %copy-done.1, ...), custom_call_target="tpu_custom_call" | custom-call | flops 1200000000 | bytes 3600000 | tf_op jit(solution)/shard_map/stream_faces/pallas_call | solution.py:473
  47.9 0.0 collective-permute-done.6.refs_2_
  47.9 0.0 collective-permute-done.7.refs_5_
  48.0 2.4 %stream_faces.7 = f32[5,4,32,512]{3,2,1,0:T(8,128)} custom-call(f32[5,4,32,512]{3,2,1,0:T(8,128)S(1)} %copy-done, f32[21,16,128]{2,1,0:T(8,128)S(1)} %collective-permute-done.3.pair_ref.refs_1_, f32[16,16,128]{2,1,0:T(8,128)S(1)} %collective-permute-done.6.refs_2_, s32[4,32,512]{2,1,0:T(8,128)S(1)} %copy-done.1, ...), custom_call_target="tpu_custom_call" | custom-call | flops 600000000 | bytes 1800000 | tf_op jit(solution)/shard_map/stream_faces/pallas_call | solution.py:473
  (7 shorter events, 0.2 us)
Async XLA Ops:
  0.0 4.9 %collective-permute-start = (f32[5,4,32,512]{3,2,1,0:T(8,128)}, f32[5,4,32,512]{3,2,1,0:T(8,128)S(1)}, u32[]{:S(2)}, u32[]{:S(2)}) collective-permute-start(f32[5,4,32,512]{3,2,1,0:T(8,128)} %refs_0_.7), channel_id=1, source_target_pairs={{0,1},{1,0},{2,3},{3,2},{4,5},{5,4},{6,7},{7,6},{8,9},{9,8},{10,11... | collective-permute-start | bytes 3932168 | tf_op jit(solution)/shard_map/ppermute | solution.py:651
  0.5 4.4 %copy-start.5 = (f32[1024]{0:T(1024)S(1)}, f32[1024]{0:T(1024)}, u32[]{:S(2)}) copy-start(f32[1024]{0:T(1024)} %param.9) | copy-start | bytes 12292
  0.5 4.5 %copy-start.3 = (f32[64,2048]{1,0:T(8,128)S(1)}, f32[64,2048]{1,0:T(8,128)}, u32[]{:S(2)}) copy-start(f32[64,2048]{1,0:T(8,128)} %constant.5.clone.outer_ref) | copy-start | bytes 1572868
  0.5 4.5 %copy-start.4 = (f32[64,128]{1,0:T(8,128)S(1)}, f32[64,128]{1,0:T(8,128)}, u32[]{:S(2)}) copy-start(f32[64,128]{1,0:T(8,128)} %constant.4.clone.inner_ref) | copy-start | bytes 98308
  2.3 15.7 %collective-permute-start.2 = (f32[21,32,128]{2,1,0:T(8,128)}, f32[21,32,128]{2,1,0:T(8,128)S(1)}, u32[]{:S(2)}, u32[]{:S(2)}) collective-permute-start(f32[21,32,128]{2,1,0:T(8,128)} %pack_bricks.1), channel_id=1, source_target_pairs={{0,4},{4,0},{8,12},{12,8},{16,20},{20,16},{24,28},{28,24},{1,5},{5... | collective-permute-start | bytes 1032200 | tf_op jit(solution)/shard_map/ppermute | solution.py:670
  4.9 1.3 %copy-start = (f32[5,4,32,512]{3,2,1,0:T(8,128)S(1)}, f32[5,4,32,512]{3,2,1,0:T(8,128)}, u32[]{:S(2)}) copy-start(f32[5,4,32,512]{3,2,1,0:T(8,128)} %refs_0_.7) | copy-start | bytes 3932164
  6.2 5.0 %copy-start.2 = (s32[4,32,512]{2,1,0:T(8,128)S(1)}, s32[4,32,512]{2,1,0:T(8,128)}, u32[]{:S(2)}) copy-start(s32[4,32,512]{2,1,0:T(8,128)} %mask_ref.8) | copy-start | bytes 786436
  9.7 38.3 %collective-permute-start.7 = (f32[5,4,32,512]{3,2,1,0:T(8,128)S(1)}, f32[5,4,32,512]{3,2,1,0:T(8,128)S(1)}, u32[]{:S(2)}, u32[]{:S(2)}) collective-permute-start(f32[5,4,32,512]{3,2,1,0:T(8,128)S(1)} %get-tuple-element.14), channel_id=1, source_target_pairs={{0,2},{1,3},{2,0},{3,1},{4,6},{5,7},{6,4},{7,5},{8,10},{9,11},{10,... | collective-permute-start | bytes 3932168 | tf_op jit(solution)/shard_map/ppermute | solution.py:651
  11.2 2.9 %copy-start.1 = (s32[4,32,512]{2,1,0:T(8,128)S(1)}, s32[4,32,512]{2,1,0:T(8,128)}, u32[]{:S(2)}) copy-start(s32[4,32,512]{2,1,0:T(8,128)} %refs_3_.7) | copy-start | bytes 786436
  14.2 14.7 %collective-permute-start.1 = (f32[21,16,384]{2,1,0:T(8,128)S(1)}, f32[21,16,384]{2,1,0:T(8,128)S(1)}, u32[]{:S(2)}, u32[]{:S(2)}) collective-permute-start(f32[21,16,384]{2,1,0:T(8,128)S(1)} %bring_planes.3.after_ref), channel_id=1, source_target_pairs={{0,4},{4,0},{8,12},{12,8},{16,20},{20,16},{24,28},{28,24},{1,5},{5... | collective-permute-start | bytes 1548296 | tf_op jit(solution)/shard_map/ppermute | solution.py:681
  18.0 14.5 %collective-permute-start.5 = (f32[16,32,128]{2,1,0:T(8,128)S(1)}, f32[16,32,128]{2,1,0:T(8,128)S(1)}, u32[]{:S(2)}, u32[]{:S(2)}) collective-permute-start(f32[16,32,128]{2,1,0:T(8,128)S(1)} %pass_planes.4.after_ref), channel_id=1, source_target_pairs={{0,8},{8,16},{16,24},{12,4},{20,12},{28,20},{1,9},{9,17},{17,25},{... | collective-permute-start | bytes 786440 | tf_op jit(solution)/shard_map/ppermute | solution.py:686
  21.6 14.7 %collective-permute-start.4 = (f32[21,16,256]{2,1,0:T(8,128)S(1)}, f32[21,16,256]{2,1,0:T(8,128)S(1)}, u32[]{:S(2)}, u32[]{:S(2)}) collective-permute-start(f32[21,16,256]{2,1,0:T(8,128)S(1)} %bring_planes.4.after_ref), channel_id=1, source_target_pairs={{0,4},{4,0},{8,12},{12,8},{16,20},{20,16},{24,28},{28,24},{1,5},{5... | collective-permute-start | bytes 1032200 | tf_op jit(solution)/shard_map/ppermute | solution.py:681
  28.9 14.4 %collective-permute-start.8 = (f32[16,16,384]{2,1,0:T(8,128)S(1)}, f32[16,16,384]{2,1,0:T(8,128)S(1)}, u32[]{:S(2)}, u32[]{:S(2)}) collective-permute-start(f32[16,16,384]{2,1,0:T(8,128)S(1)} %pass_planes.5.after_ref), channel_id=1, source_target_pairs={{0,8},{8,16},{16,24},{12,4},{20,12},{28,20},{1,9},{9,17},{17,25},{... | collective-permute-start | bytes 1179656 | tf_op jit(solution)/shard_map/ppermute | solution.py:686
  32.5 7.3 %collective-permute-start.3 = (f32[21,16,128]{2,1,0:T(8,128)S(1)}, f32[21,16,128]{2,1,0:T(8,128)S(1)}, u32[]{:S(2)}, u32[]{:S(2)}) collective-permute-start(f32[21,16,128]{2,1,0:T(8,128)S(1)} %bring_planes.5.refs_5_), channel_id=1, source_target_pairs={{0,4},{4,0},{8,12},{12,8},{16,20},{20,16},{24,28},{28,24},{1,5},{5... | collective-permute-start | bytes 516104 | tf_op jit(solution)/shard_map/ppermute | solution.py:681
  36.3 9.8 %collective-permute-start.9 = (f32[16,16,256]{2,1,0:T(8,128)S(1)}, f32[16,16,256]{2,1,0:T(8,128)S(1)}, u32[]{:S(2)}, u32[]{:S(2)}) collective-permute-start(f32[16,16,256]{2,1,0:T(8,128)S(1)} %pass_planes.6.after_ref), channel_id=1, source_target_pairs={{0,8},{8,16},{16,24},{12,4},{20,12},{28,20},{1,9},{9,17},{17,25},{... | collective-permute-start | bytes 786440 | tf_op jit(solution)/shard_map/ppermute | solution.py:686
  39.9 8.1 %collective-permute-start.6 = (f32[16,16,128]{2,1,0:T(8,128)S(1)}, f32[16,16,128]{2,1,0:T(8,128)S(1)}, u32[]{:S(2)}, u32[]{:S(2)}) collective-permute-start(f32[16,16,128]{2,1,0:T(8,128)S(1)} %pass_planes.7.refs_5_), channel_id=1, source_target_pairs={{0,8},{8,16},{16,24},{12,4},{20,12},{28,20},{1,9},{9,17},{17,25},{... | collective-permute-start | bytes 393224 | tf_op jit(solution)/shard_map/ppermute | solution.py:686
